TPU v7x, 32 devices: a whole 2x2x4 slice. The times are simulated.
32 devices in a mesh: members: 2 (over x), gy: 8 (over z, y), gx: 2 (over core).
Axes of the slice: x: 2, y: 2, z: 4, core: 2. Of those that a mesh axis runs over, the one named last changes fastest.
Arguments:
- right_side: float32 [2048, 2048], P(('members', 'gy'), 'gx'), parts along dimension 0, may hold values from -60 to 60
- faces: float32 [2, 1024, 2048], P(None, 'gy', 'gx'), may hold values from 0.3 to 3
- ratio: float32 [1024, 2048], P('gy', 'gx'), may hold values from 0.05 to 0.5
- centre: float32 [1024, 2048], P('gy', 'gx'), may hold values from 0.5 to 1
- offdiag: float32 [8, 1024, 2048], P(None, 'gy', 'gx'), may hold values from 0.005 to 0.05
- mask: int32 [1024, 2048], P('gy', 'gx'), may hold values 0 or 1
Outputs:
- solution: float32 [2048, 2048], P(('members', 'gy'), 'gx'), parts along dimension 0
- residual: float32 [2048, 2048], P(('members', 'gy'), 'gx'), parts along dimension 0
There are 2 independent parts, one for each index of `members`. A program takes and returns all parts, laid end to end along the dimension named above; an argument that names none is the same for every part. Nothing has to cross between parts.
All inputs are finite; a program needn't handle non-finite values. No bound on the sum of `mask` on one device may be relied on, other than what follows from the above.
Results may differ from a plain program's by a relative error of at most 0.00012.
Values sent between devices are 32-bit elements; how exact they have to be, the bound alone decides.
No kernel may reach another device: no remote copies, remote signals or barrier semaphores. Data moves between devices by JAX's collectives and lax.ppermute only.
A program may use at most 64 MiB of HBM per device.

v0:
```python
import jax
import jax.numpy as jnp
from jax import lax
from jax.sharding import PartitionSpec as P

ITERS = 3


neighbour_steps = [(-1, -1), (-1, 0), (-1, 1), (0, -1), (0, 1), (1, -1), (1, 0), (1, 1)]


def padded_2(block, sides, width):
    for axis, dim in sides:
        count = lax.axis_size(axis)
        forward = [(i, i + 1) for i in range(count - 1)]
        backward = [(target, source) for source, target in forward]
        low = lax.ppermute(
            lax.slice_in_dim(block, block.shape[dim] - width, None, axis=dim), axis, forward
        )
        high = lax.ppermute(lax.slice_in_dim(block, 0, width, axis=dim), axis, backward)
        block = jnp.concatenate([low, block, high], axis=dim)
    return block


def window(padded, margin, extend, down, across, height, breadth):
    first_row = margin - extend + down
    first_column = margin - extend + across
    return padded[
        ...,
        first_row : first_row + height + 2 * extend,
        first_column : first_column + breadth + 2 * extend,
    ]


def body(right_side, faces, ratio, centre, offdiag, mask):
    height, breadth = right_side.shape
    wet_cells = mask.astype(jnp.float32)
    margin = 1
    stacked = jnp.concatenate([faces, offdiag], axis=0)
    coefficients = padded_2(stacked, (("gy", 1), ("gx", 2)), margin)
    west_face = faces[0]
    south_face = faces[1]
    east_face = window(coefficients[0], margin, 0, 0, 1, height, breadth)
    north_face = window(coefficients[1], margin, 0, 1, 0, height, breadth)
    diagonal = west_face + east_face + south_face + north_face + ratio
    weights_pad = coefficients[2:10]
    residual = wet_cells * right_side
    solution = jnp.zeros_like(residual)
    direction = jnp.zeros_like(residual)
    image = jnp.zeros_like(residual)
    rz_before = jnp.float32(1.0)
    for iteration in range(ITERS):
        residual_pad = padded_2(residual, (("gy", 0), ("gx", 1)), 1)
        total = centre * window(residual_pad, margin, 0, 0, 0, height, breadth)
        for offset_index, (down, across) in enumerate(neighbour_steps):
            product = weights_pad[offset_index] * residual_pad
            total = total + window(product, margin, 0, -down, -across, height, breadth)
        smoothed = wet_cells * total
        smoothed_pad = padded_2(smoothed, (("gy", 0), ("gx", 1)), 1)
        operate_total = diagonal * window(smoothed_pad, 1, 0, 0, 0, height, breadth)
        operate_total = operate_total - west_face * window(
            smoothed_pad, 1, 0, 0, -1, height, breadth
        )
        operate_total = operate_total - east_face * window(
            smoothed_pad, 1, 0, 0, 1, height, breadth
        )
        operate_total = operate_total - south_face * window(
            smoothed_pad, 1, 0, -1, 0, height, breadth
        )
        operate_total = operate_total - north_face * window(
            smoothed_pad, 1, 0, 1, 0, height, breadth
        )
        applied = wet_cells * operate_total
        rz_now = lax.psum(jnp.sum(residual * smoothed), ("gy", "gx"))
        if iteration == 0:
            direction = smoothed
            image = applied
        else:
            ratio_now = rz_now / rz_before
            direction = smoothed + ratio_now * direction
            image = applied + ratio_now * image
        curvature = lax.psum(jnp.sum(direction * image), ("gy", "gx"))
        step_size = rz_now / curvature
        solution = solution + step_size * direction
        residual = residual - step_size * image
        rz_before = rz_now
    return (solution, residual)


def solution(mesh):
    return jax.shard_map(
        body,
        mesh=mesh,
        in_specs=(
            P(("members", "gy"), "gx"),
            P(None, "gy", "gx"),
            P("gy", "gx"),
            P("gy", "gx"),
            P(None, "gy", "gx"),
            P("gy", "gx"),
        ),
        out_specs=(P(("members", "gy"), "gx"), P(("members", "gy"), "gx")),
        check_vma=False,
    )
```

profile of v0, /device:TPU:0, one launch (start us, length us, event | category | flops | bytes accessed | tf_op | source)
XLA Modules:
  0.0 295.2 jit_solution(18364622553167783723)
XLA Ops:
  1.9 4.9 %collective-permute-start.4 = (f32[1,1024]{1,0:T(1,128)S(1)}, f32[1,1024]{1,0:T(1,128)S(1)}, u32[]{:S(2)}, u32[]{:S(2)}) collective-permute-start(f32[1,1024]{1,0:T(1,128)S(1)} %get-tuple-element.53), channel_id=1, source_target_pairs={{0,2},{2,4},{4,6},{6,8},{8,10},{10,12},{12,14},{1,3},{3,5},{5,7},{... | collective-permute-start | bytes 12296 | tf_op jit(solution)/shard_map/ppermute | solution.py:17
  9.4 2.5 constant_dynamic-update-slice_fusion
  12.0 4.5 %collective-permute-start = (f32[10,1,1024]{2,1,0:T(1,128)S(1)}, f32[10,1,1024]{2,1,0:T(1,128)S(1)}, u32[]{:S(2)}, u32[]{:S(2)}) collective-permute-start(f32[10,1,1024]{2,1,0:T(1,128)S(1)} %get-tuple-element.29), channel_id=1, source_target_pairs={{0,2},{2,4},{4,6},{6,8},{8,10},{10,12},{12,14},{1,3},{3,5},{5,7},{... | collective-permute-start | bytes 122888 | tf_op jit(solution)/shard_map/ppermute | solution.py:17
  18.2 4.7 %collective-permute-done.1 = f32[10,1,1024]{2,1,0:T(1,128)S(1)} collective-permute-done((f32[10,1,1024]{2,1,0:T(1,128)S(1)}, f32[10,1,1024]{2,1,0:T(1,128)S(1)}, u32[]{:S(2)}, u32[]{:S(2)}) %collective-permute-start.1) | collective-permute-done | bytes 40992 | tf_op jit(solution)/shard_map/ppermute | solution.py:20
  24.2 2.4 copy-done
  31.6 3.0 %collective-permute-start.6 = (f32[130,1]{1,0:T(8,128)S(1)}, f32[130,1]{1,0:T(8,128)S(1)}, u32[]{:S(2)}, u32[]{:S(2)}) collective-permute-start(f32[130,1]{1,0:T(8,128)S(1)} %get-tuple-element.36), channel_id=1, source_target_pairs={{0,1},{2,3},{4,5},{6,7},{8,9},{10,11},{12,13},{14,15},{16,17},{18,... | collective-permute-start | bytes 1568 | tf_op jit(solution)/shard_map/ppermute | solution.py:17
  36.5 8.4 %concatenate.77 = f32[10,130,1026]{2,1,0:T(8,128)} concatenate(f32[10,130,1]{2,1,0:T(8,128)S(1)} %copy.22, f32[10,130,1024]{2,1,0:T(8,128)} %copy-done, f32[10,130,1]{2,1,0:T(8,128)S(1)} %copy.23), dimensions={2} | concatenate | bytes 10670400 | tf_op jit(solution)/shard_map/concatenate | solution.py:21
  44.9 3.3 %slice_bitcast_fusion.1 = (f32[130,1026]{1,0:T(8,128)S(1)}, f32[130,1026]{1,0:T(8,128)S(1)}, f32[130,1026]{1,0:T(8,128)S(1)}, f32[130,1026]{1,0:T(8,128)S(1)}, f...) fusion(f32[10,130,1026]{2,1,0:T(8,128)} %concatenate.77), kind=kLoop, calls=%fused_computation.2 | loop fusion | bytes 10670400 | tf_op jit(solution)/shard_map/squeeze | solution.py:43
  48.3 1.6 fusion.48
  50.5 4.8 %collective-permute-start.8 = (f32[1,1024]{1,0:T(1,128)S(1)}, f32[1,1024]{1,0:T(1,128)S(1)}, u32[]{:S(2)}, u32[]{:S(2)}) collective-permute-start(f32[1,1024]{1,0:T(1,128)S(1)} %get-tuple-element.51), channel_id=1, source_target_pairs={{0,2},{2,4},{4,6},{6,8},{8,10},{10,12},{12,14},{1,3},{3,5},{5,7},{... | collective-permute-start | bytes 12296 | tf_op jit(solution)/shard_map/ppermute | solution.py:17
  56.6 4.2 %collective-permute-done.9 = f32[1,1024]{1,0:T(1,128)S(1)} collective-permute-done((f32[1,1024]{1,0:T(1,128)S(1)}, f32[1,1024]{1,0:T(1,128)S(1)}, u32[]{:S(2)}, u32[]{:S(2)}) %collective-permute-start.9) | collective-permute-done | bytes 4128 | tf_op jit(solution)/shard_map/ppermute | solution.py:20
  63.5 1.8 collective-permute-done.11
  65.4 1.4 multiply_reduce_fusion.4
  66.8 30.3 %all-reduce = (f32[]{:T(128)}, f32[]{:T(128)}) all-reduce(f32[]{:T(128)} %get-tuple-element.5, f32[]{:T(128)} %get-tuple-element.4), channel_id=1, replica_groups=mesh['members'=2,'gy'=8,'gx'=2] {'gy','gx'}, use_global_device_ids=true, to_apply=%region_1.0 | all-reduce | flops 2 | bytes 16 | tf_op jit(solution)/shard_map/psum | solution.py:74
  101.1 4.2 %collective-permute-done.13 = f32[1,1024]{1,0:T(1,128)S(1)} collective-permute-done((f32[1,1024]{1,0:T(1,128)S(1)}, f32[1,1024]{1,0:T(1,128)S(1)}, u32[]{:S(2)}, u32[]{:S(2)}) %collective-permute-start.13) | collective-permute-done | bytes 4128 | tf_op jit(solution)/shard_map/ppermute | solution.py:20
  106.7 3.0 %collective-permute-start.14 = (f32[130,1]{1,0:T(8,128)S(1)}, f32[130,1]{1,0:T(8,128)S(1)}, u32[]{:S(2)}, u32[]{:S(2)}) collective-permute-start(f32[130,1]{1,0:T(8,128)S(1)} %get-tuple-element.34), channel_id=1, source_target_pairs={{0,1},{2,3},{4,5},{6,7},{8,9},{10,11},{12,13},{14,15},{16,17},{18,... | collective-permute-start | bytes 1568 | tf_op jit(solution)/shard_map/ppermute | solution.py:17
  112.1 4.7 %multiply_reduce_fusion.3 = (f32[]{:T(128)}, f32[128,1024]{1,0:T(8,128)S(1)}) fusion(f32[128,1024]{1,0:T(8,128)} %copy-done.6, f32[130,1026]{1,0:T(8,128)S(1)} %concatenate.86, f32[130,1026]{1,0:T(8,128)} %copy-done.10, f32[130,1026]{1,0:T(8,128)} %copy-done.11, f32[130,1026]{1,0:T(8,128)} %copy-done.12, f32[130,1026]{1,0:T(8,128)} %copy-done.13, ...), kind=kLoop, calls=%fused_computation.130 | loop fusion | flops 2752511 | bytes 10485764 | tf_op jit(solution)/shard_map/reduce_sum | solution.py:74
  116.8 1.8 collective-permute-start.16
  119.9 4.2 %collective-permute-done.17 = f32[1,1024]{1,0:T(1,128)S(1)} collective-permute-done((f32[1,1024]{1,0:T(1,128)S(1)}, f32[1,1024]{1,0:T(1,128)S(1)}, u32[]{:S(2)}, u32[]{:S(2)}) %collective-permute-start.17) | collective-permute-done | bytes 4128 | tf_op jit(solution)/shard_map/ppermute | solution.py:20
  126.8 31.2 %psum.44 = f32[]{:T(128)} all-reduce(f32[]{:T(128)} %get-tuple-element.14), channel_id=1, replica_groups=mesh['members'=2,'gy'=8,'gx'=2] {'gy','gx'}, use_global_device_ids=true, to_apply=%region_5.0 | all-reduce | flops 1 | bytes 8 | tf_op jit(solution)/shard_map/psum | solution.py:74
  159.3 3.9 %multiply_reduce_fusion.2 = (f32[]{:T(128)}, f32[128,1024]{1,0:T(8,128)}) fusion(f32[128,1024]{1,0:T(8,128)S(1)} %get-tuple-element.15, f32[128,1024]{1,0:T(8,128)S(1)} %fusion.48, f32[]{:T(128)S(6)} %div.16, f32[128,1024]{1,0:T(8,128)} %copy-done.19, f32[1,1024]{1,0:T(1,128)S(1)} %collective-permute-done.17, f32[1,1024]{1,0:T(1,128)S(1)} %collective-permute-done.16, ...), kind=kLoop, calls=%fused_computation.128 | loop fusion | flops 3801087 | bytes 5252120 | tf_op jit(solution)/shard_map/reduce_sum | solution.py:82
  163.2 30.1 %psum.45 = f32[]{:T(128)} all-reduce(f32[]{:T(128)} %get-tuple-element.12), channel_id=1, replica_groups=mesh['members'=2,'gy'=8,'gx'=2] {'gy','gx'}, use_global_device_ids=true, to_apply=%region_7.0 | all-reduce | flops 1 | bytes 8 | tf_op jit(solution)/shard_map/psum | solution.py:82
  198.4 4.2 %collective-permute-done.21 = f32[1,1024]{1,0:T(1,128)S(1)} collective-permute-done((f32[1,1024]{1,0:T(1,128)S(1)}, f32[1,1024]{1,0:T(1,128)S(1)}, u32[]{:S(2)}, u32[]{:S(2)}) %collective-permute-start.21) | collective-permute-done | bytes 4128 | tf_op jit(solution)/shard_map/ppermute | solution.py:20
  204.0 3.2 %collective-permute-start.22 = (f32[130,1]{1,0:T(8,128)S(1)}, f32[130,1]{1,0:T(8,128)S(1)}, u32[]{:S(2)}, u32[]{:S(2)}) collective-permute-start(f32[130,1]{1,0:T(8,128)S(1)} %get-tuple-element.32), channel_id=1, source_target_pairs={{0,1},{2,3},{4,5},{6,7},{8,9},{10,11},{12,13},{14,15},{16,17},{18,... | collective-permute-start | bytes 1568 | tf_op jit(solution)/shard_map/ppermute | solution.py:17
  209.4 4.7 %multiply_reduce_fusion.1 = (f32[]{:T(128)}, f32[128,1024]{1,0:T(8,128)S(1)}) fusion(f32[128,1024]{1,0:T(8,128)} %copy-done.5, f32[130,1026]{1,0:T(8,128)S(1)} %concatenate.93, f32[130,1026]{1,0:T(8,128)} %copy-done.10, f32[130,1026]{1,0:T(8,128)} %copy-done.11, f32[130,1026]{1,0:T(8,128)} %copy-done.12, f32[130,1026]{1,0:T(8,128)} %copy-done.13, ...), kind=kLoop, calls=%fused_computation.126 | loop fusion | flops 2752511 | bytes 10485764 | tf_op jit(solution)/shard_map/reduce_sum | solution.py:74
  214.1 1.7 collective-permute-start.24
  217.1 4.2 %collective-permute-done.25 = f32[1,1024]{1,0:T(1,128)S(1)} collective-permute-done((f32[1,1024]{1,0:T(1,128)S(1)}, f32[1,1024]{1,0:T(1,128)S(1)}, u32[]{:S(2)}, u32[]{:S(2)}) %collective-permute-start.25) | collective-permute-done | bytes 4128 | tf_op jit(solution)/shard_map/ppermute | solution.py:20
  221.4 1.4 collective-permute-start.26
  224.1 31.1 %psum.46 = f32[]{:T(128)} all-reduce(f32[]{:T(128)} %get-tuple-element.10), channel_id=1, replica_groups=mesh['members'=2,'gy'=8,'gx'=2] {'gy','gx'}, use_global_device_ids=true, to_apply=%region_9.0 | all-reduce | flops 1 | bytes 8 | tf_op jit(solution)/shard_map/psum | solution.py:74
  256.6 4.7 %multiply_reduce_fusion = (f32[]{:T(128)}, f32[128,1024]{1,0:T(8,128)}) fusion(f32[128,1024]{1,0:T(8,128)} %copy-done.3, f32[]{:T(128)S(6)} %div.18, f32[128,1024]{1,0:T(8,128)S(1)} %get-tuple-element.15, f32[128,1024]{1,0:T(8,128)S(1)} %fusion.48, f32[]{:T(128)S(6)} %div.16, f32[128,1024]{1,0:T(8,128)} %get-tuple-element.13, ...), kind=kLoop, calls=%fused_computation.124 | loop fusion | flops 4063231 | bytes 5776412 | tf_op jit(solution)/shard_map/reduce_sum | solution.py:82
  261.3 30.2 %psum.47 = f32[]{:T(128)} all-reduce(f32[]{:T(128)} %get-tuple-element.8), channel_id=1, replica_groups=mesh['members'=2,'gy'=8,'gx'=2] {'gy','gx'}, use_global_device_ids=true, to_apply=%region_11.0 | all-reduce | flops 1 | bytes 8 | tf_op jit(solution)/shard_map/psum | solution.py:82
  292.8 2.4 multiply_subtract_fusion
  (114 shorter events, 38.5 us)
Async XLA Ops:
  1.9 15.9 %collective-permute-start.4 = (f32[1,1024]{1,0:T(1,128)S(1)}, f32[1,1024]{1,0:T(1,128)S(1)}, u32[]{:S(2)}, u32[]{:S(2)}) collective-permute-start(f32[1,1024]{1,0:T(1,128)S(1)} %get-tuple-element.53), channel_id=1, source_target_pairs={{0,2},{2,4},{4,6},{6,8},{8,10},{10,12},{12,14},{1,3},{3,5},{5,7},{... | collective-permute-start | bytes 12296 | tf_op jit(solution)/shard_map/ppermute | solution.py:17
  6.8 11.0 %collective-permute-start.5 = (f32[1,1024]{1,0:T(1,128)S(1)}, f32[1,1024]{1,0:T(1,128)S(1)}, u32[]{:S(2)}, u32[]{:S(2)}) collective-permute-start(f32[1,1024]{1,0:T(1,128)S(1)} %get-tuple-element.54), channel_id=1, source_target_pairs={{2,0},{4,2},{6,4},{8,6},{10,8},{12,10},{14,12},{3,1},{5,3},{7,5},{... | collective-permute-start | bytes 12296 | tf_op jit(solution)/shard_map/ppermute | solution.py:20
  12.0 6.2 %collective-permute-start = (f32[10,1,1024]{2,1,0:T(1,128)S(1)}, f32[10,1,1024]{2,1,0:T(1,128)S(1)}, u32[]{:S(2)}, u32[]{:S(2)}) collective-permute-start(f32[10,1,1024]{2,1,0:T(1,128)S(1)} %get-tuple-element.29), channel_id=1, source_target_pairs={{0,2},{2,4},{4,6},{6,8},{8,10},{10,12},{12,14},{1,3},{3,5},{5,7},{... | collective-permute-start | bytes 122888 | tf_op jit(solution)/shard_map/ppermute | solution.py:17
  16.5 6.3 %collective-permute-start.1 = (f32[10,1,1024]{2,1,0:T(1,128)S(1)}, f32[10,1,1024]{2,1,0:T(1,128)S(1)}, u32[]{:S(2)}, u32[]{:S(2)}) collective-permute-start(f32[10,1,1024]{2,1,0:T(1,128)S(1)} %get-tuple-element.30), channel_id=1, source_target_pairs={{2,0},{4,2},{6,4},{8,6},{10,8},{12,10},{14,12},{3,1},{5,3},{7,5},{... | collective-permute-start | bytes 122888 | tf_op jit(solution)/shard_map/ppermute | solution.py:20
  27.6 8.6 %collective-permute-start.2 = (f32[10,130,1]{1,2,0:T(1,128)S(1)}, f32[10,130,1]{1,2,0:T(1,128)S(1)}, u32[]{:S(2)}, u32[]{:S(2)}) collective-permute-start(f32[10,130,1]{1,2,0:T(1,128)S(1)} %copy.20), channel_id=1, source_target_pairs={{0,1},{2,3},{4,5},{6,7},{8,9},{10,11},{12,13},{14,15},{16,17},{18,... | collective-permute-start | bytes 15608 | tf_op jit(solution)/shard_map/ppermute | solution.py:17
  28.9 7.0 %collective-permute-start.3 = (f32[10,130,1]{1,2,0:T(1,128)S(1)}, f32[10,130,1]{1,2,0:T(1,128)S(1)}, u32[]{:S(2)}, u32[]{:S(2)}) collective-permute-start(f32[10,130,1]{1,2,0:T(1,128)S(1)} %copy.21), channel_id=1, source_target_pairs={{1,0},{3,2},{5,4},{7,6},{9,8},{11,10},{13,12},{15,14},{17,16},{19,... | collective-permute-start | bytes 15608 | tf_op jit(solution)/shard_map/ppermute | solution.py:20
  30.3 4.3 %collective-permute-start.7 = (f32[130,1]{1,0:T(8,128)S(1)}, f32[130,1]{1,0:T(8,128)S(1)}, u32[]{:S(2)}, u32[]{:S(2)}) collective-permute-start(f32[130,1]{1,0:T(8,128)S(1)} %get-tuple-element.35), channel_id=1, source_target_pairs={{1,0},{3,2},{5,4},{7,6},{9,8},{11,10},{13,12},{15,14},{17,16},{19,... | collective-permute-start | bytes 1568 | tf_op jit(solution)/shard_map/ppermute | solution.py:20
  31.6 3.9 %collective-permute-start.6 = (f32[130,1]{1,0:T(8,128)S(1)}, f32[130,1]{1,0:T(8,128)S(1)}, u32[]{:S(2)}, u32[]{:S(2)}) collective-permute-start(f32[130,1]{1,0:T(8,128)S(1)} %get-tuple-element.36), channel_id=1, source_target_pairs={{0,1},{2,3},{4,5},{6,7},{8,9},{10,11},{12,13},{14,15},{16,17},{18,... | collective-permute-start | bytes 1568 | tf_op jit(solution)/shard_map/ppermute | solution.py:17
  48.2 17.1 %copy-start.8 = (f32[130,1026]{1,0:T(8,128)}, f32[130,1026]{1,0:T(8,128)S(1)}, u32[]{:S(2)}) copy-start(f32[130,1026]{1,0:T(8,128)S(1)} %get-tuple-element.17) | copy-start | bytes 1600564
  50.5 6.1 %collective-permute-start.8 = (f32[1,1024]{1,0:T(1,128)S(1)}, f32[1,1024]{1,0:T(1,128)S(1)}, u32[]{:S(2)}, u32[]{:S(2)}) collective-permute-start(f32[1,1024]{1,0:T(1,128)S(1)} %get-tuple-element.51), channel_id=1, source_target_pairs={{0,2},{2,4},{4,6},{6,8},{8,10},{10,12},{12,14},{1,3},{3,5},{5,7},{... | collective-permute-start | bytes 12296 | tf_op jit(solution)/shard_map/ppermute | solution.py:17
  55.3 5.5 %collective-permute-start.9 = (f32[1,1024]{1,0:T(1,128)S(1)}, f32[1,1024]{1,0:T(1,128)S(1)}, u32[]{:S(2)}, u32[]{:S(2)}) collective-permute-start(f32[1,1024]{1,0:T(1,128)S(1)} %get-tuple-element.52), channel_id=1, source_target_pairs={{2,0},{4,2},{6,4},{8,6},{10,8},{12,10},{14,12},{3,1},{5,3},{7,5},{... | collective-permute-start | bytes 12296 | tf_op jit(solution)/shard_map/ppermute | solution.py:20
  60.9 2.6 collective-permute-start.10
  62.2 3.2 %collective-permute-start.11 = (f32[130,1]{1,0:T(8,128)S(1)}, f32[130,1]{1,0:T(8,128)S(1)}, u32[]{:S(2)}, u32[]{:S(2)}) collective-permute-start(f32[130,1]{1,0:T(8,128)S(1)} %get-tuple-element.42), channel_id=1, source_target_pairs={{1,0},{3,2},{5,4},{7,6},{9,8},{11,10},{13,12},{15,14},{17,16},{19,... | collective-permute-start | bytes 1568 | tf_op jit(solution)/shard_map/ppermute | solution.py:20
  66.8 43.0 %copy-start.19 = (f32[128,1024]{1,0:T(8,128)}, f32[128,1024]{1,0:T(8,128)S(1)}, u32[]{:S(2)}) copy-start(f32[128,1024]{1,0:T(8,128)S(1)} %get-tuple-element.16) | copy-start | bytes 1572868
  98.5 2.6 collective-permute-start.12
  99.8 5.5 %collective-permute-start.13 = (f32[1,1024]{1,0:T(1,128)S(1)}, f32[1,1024]{1,0:T(1,128)S(1)}, u32[]{:S(2)}, u32[]{:S(2)}) collective-permute-start(f32[1,1024]{1,0:T(1,128)S(1)} %get-tuple-element.50), channel_id=1, source_target_pairs={{2,0},{4,2},{6,4},{8,6},{10,8},{12,10},{14,12},{3,1},{5,3},{7,5},{... | collective-permute-start | bytes 12296 | tf_op jit(solution)/shard_map/ppermute | solution.py:20
  105.4 4.3 %collective-permute-start.15 = (f32[130,1]{1,0:T(8,128)S(1)}, f32[130,1]{1,0:T(8,128)S(1)}, u32[]{:S(2)}, u32[]{:S(2)}) collective-permute-start(f32[130,1]{1,0:T(8,128)S(1)} %get-tuple-element.33), channel_id=1, source_target_pairs={{1,0},{3,2},{5,4},{7,6},{9,8},{11,10},{13,12},{15,14},{17,16},{19,... | collective-permute-start | bytes 1568 | tf_op jit(solution)/shard_map/ppermute | solution.py:20
  106.7 3.9 %collective-permute-start.14 = (f32[130,1]{1,0:T(8,128)S(1)}, f32[130,1]{1,0:T(8,128)S(1)}, u32[]{:S(2)}, u32[]{:S(2)}) collective-permute-start(f32[130,1]{1,0:T(8,128)S(1)} %get-tuple-element.34), channel_id=1, source_target_pairs={{0,1},{2,3},{4,5},{6,7},{8,9},{10,11},{12,13},{14,15},{16,17},{18,... | collective-permute-start | bytes 1568 | tf_op jit(solution)/shard_map/ppermute | solution.py:17
  116.8 77.8 %copy-start.7 = (f32[128,1024]{1,0:T(8,128)S(1)}, f32[128,1024]{1,0:T(8,128)}, u32[]{:S(2)}) copy-start(f32[128,1024]{1,0:T(8,128)} %copy-done.6) | copy-start | bytes 1572868
  116.8 3.1 %collective-permute-start.16 = (f32[1,1024]{1,0:T(1,128)S(1)}, f32[1,1024]{1,0:T(1,128)S(1)}, u32[]{:S(2)}, u32[]{:S(2)}) collective-permute-start(f32[1,1024]{1,0:T(1,128)S(1)} %get-tuple-element.47), channel_id=1, source_target_pairs={{0,2},{2,4},{4,6},{6,8},{8,10},{10,12},{12,14},{1,3},{3,5},{5,7},{... | collective-permute-start | bytes 12296 | tf_op jit(solution)/shard_map/ppermute | solution.py:17
  118.6 5.5 %collective-permute-start.17 = (f32[1,1024]{1,0:T(1,128)S(1)}, f32[1,1024]{1,0:T(1,128)S(1)}, u32[]{:S(2)}, u32[]{:S(2)}) collective-permute-start(f32[1,1024]{1,0:T(1,128)S(1)} %get-tuple-element.48), channel_id=1, source_target_pairs={{2,0},{4,2},{6,4},{8,6},{10,8},{12,10},{14,12},{3,1},{5,3},{7,5},{... | collective-permute-start | bytes 12296 | tf_op jit(solution)/shard_map/ppermute | solution.py:20
  124.2 35.1 %collective-permute-start.18 = (f32[130,1]{1,0:T(8,128)S(1)}, f32[130,1]{1,0:T(8,128)S(1)}, u32[]{:S(2)}, u32[]{:S(2)}) collective-permute-start(f32[130,1]{1,0:T(8,128)S(1)} %get-tuple-element.39), channel_id=1, source_target_pairs={{0,1},{2,3},{4,5},{6,7},{8,9},{10,11},{12,13},{14,15},{16,17},{18,... | collective-permute-start | bytes 1568 | tf_op jit(solution)/shard_map/ppermute | solution.py:17
  125.5 33.8 %collective-permute-start.19 = (f32[130,1]{1,0:T(8,128)S(1)}, f32[130,1]{1,0:T(8,128)S(1)}, u32[]{:S(2)}, u32[]{:S(2)}) collective-permute-start(f32[130,1]{1,0:T(8,128)S(1)} %get-tuple-element.40), channel_id=1, source_target_pairs={{1,0},{3,2},{5,4},{7,6},{9,8},{11,10},{13,12},{15,14},{17,16},{19,... | collective-permute-start | bytes 1568 | tf_op jit(solution)/shard_map/ppermute | solution.py:20
  195.8 2.6 collective-permute-start.20
  197.1 5.5 %collective-permute-start.21 = (f32[1,1024]{1,0:T(1,128)S(1)}, f32[1,1024]{1,0:T(1,128)S(1)}, u32[]{:S(2)}, u32[]{:S(2)}) collective-permute-start(f32[1,1024]{1,0:T(1,128)S(1)} %get-tuple-element.46), channel_id=1, source_target_pairs={{2,0},{4,2},{6,4},{8,6},{10,8},{12,10},{14,12},{3,1},{5,3},{7,5},{... | collective-permute-start | bytes 12296 | tf_op jit(solution)/shard_map/ppermute | solution.py:20
  202.8 4.5 %collective-permute-start.23 = (f32[130,1]{1,0:T(8,128)S(1)}, f32[130,1]{1,0:T(8,128)S(1)}, u32[]{:S(2)}, u32[]{:S(2)}) collective-permute-start(f32[130,1]{1,0:T(8,128)S(1)} %get-tuple-element.31), channel_id=1, source_target_pairs={{1,0},{3,2},{5,4},{7,6},{9,8},{11,10},{13,12},{15,14},{17,16},{19,... | collective-permute-start | bytes 1568 | tf_op jit(solution)/shard_map/ppermute | solution.py:20
  204.0 3.9 %collective-permute-start.22 = (f32[130,1]{1,0:T(8,128)S(1)}, f32[130,1]{1,0:T(8,128)S(1)}, u32[]{:S(2)}, u32[]{:S(2)}) collective-permute-start(f32[130,1]{1,0:T(8,128)S(1)} %get-tuple-element.32), channel_id=1, source_target_pairs={{0,1},{2,3},{4,5},{6,7},{8,9},{10,11},{12,13},{14,15},{16,17},{18,... | collective-permute-start | bytes 1568 | tf_op jit(solution)/shard_map/ppermute | solution.py:17
  214.1 3.0 %collective-permute-start.24 = (f32[1,1024]{1,0:T(1,128)S(1)}, f32[1,1024]{1,0:T(1,128)S(1)}, u32[]{:S(2)}, u32[]{:S(2)}) collective-permute-start(f32[1,1024]{1,0:T(1,128)S(1)} %get-tuple-element.43), channel_id=1, source_target_pairs={{0,2},{2,4},{4,6},{6,8},{8,10},{10,12},{12,14},{1,3},{3,5},{5,7},{... | collective-permute-start | bytes 12296 | tf_op jit(solution)/shard_map/ppermute | solution.py:17
  215.8 5.5 %collective-permute-start.25 = (f32[1,1024]{1,0:T(1,128)S(1)}, f32[1,1024]{1,0:T(1,128)S(1)}, u32[]{:S(2)}, u32[]{:S(2)}) collective-permute-start(f32[1,1024]{1,0:T(1,128)S(1)} %get-tuple-element.44), channel_id=1, source_target_pairs={{2,0},{4,2},{6,4},{8,6},{10,8},{12,10},{14,12},{3,1},{5,3},{7,5},{... | collective-permute-start | bytes 12296 | tf_op jit(solution)/shard_map/ppermute | solution.py:20
  221.4 71.4 %copy-start.4 = (f32[128,1024]{1,0:T(8,128)S(1)}, f32[128,1024]{1,0:T(8,128)}, u32[]{:S(2)}) copy-start(f32[128,1024]{1,0:T(8,128)} %copy-done.3) | copy-start | bytes 1572868
  221.4 35.2 %collective-permute-start.26 = (f32[130,1]{1,0:T(8,128)S(1)}, f32[130,1]{1,0:T(8,128)S(1)}, u32[]{:S(2)}, u32[]{:S(2)}) collective-permute-start(f32[130,1]{1,0:T(8,128)S(1)} %get-tuple-element.37), channel_id=1, source_target_pairs={{0,1},{2,3},{4,5},{6,7},{8,9},{10,11},{12,13},{14,15},{16,17},{18,... | collective-permute-start | bytes 1568 | tf_op jit(solution)/shard_map/ppermute | solution.py:17
  222.8 33.8 %collective-permute-start.27 = (f32[130,1]{1,0:T(8,128)S(1)}, f32[130,1]{1,0:T(8,128)S(1)}, u32[]{:S(2)}, u32[]{:S(2)}) collective-permute-start(f32[130,1]{1,0:T(8,128)S(1)} %get-tuple-element.38), channel_id=1, source_target_pairs={{1,0},{3,2},{5,4},{7,6},{9,8},{11,10},{13,12},{15,14},{17,16},{19,... | collective-permute-start | bytes 1568 | tf_op jit(solution)/shard_map/ppermute | solution.py:20
  (19 other events, 114.5 us)
where the time goes:
time: 297 us; the launch traced here: 295 us
  blocking collectives  153 us (52%)
  starting transfers between devices  52.9 us (18%)
  waiting for transfers between devices  30.2 us (10%)
  other arithmetic  27.8 us (9%)
  local copies, waits for them, and re-layouts  23.6 us (8%)
  between operations  7.9 us (3%)
    psum x3, blocking collectives, body(): rz_now = lax.psum(jnp.sum(residual * smoothed), ('gy', 'gx'))  92.6 us
    psum x2, blocking collectives, body(): curvature = lax.psum(jnp.sum(direction * image), ('gy', 'gx'))  60.3 us
    ppermute x14, starting transfers between devices, padded_2(): lax.ppermute(lax.slice_in_dim(block, block.shape[dim] - width, None, axis...  34.8 us
    ppermute x14, waiting for transfers between devices, padded_2(): lax.ppermute(lax.slice_in_dim(block, 0, width, axis=dim), axis, backward)  27.5 us
    ppermute x14, starting transfers between devices, padded_2(): lax.ppermute(lax.slice_in_dim(block, 0, width, axis=dim), axis, backward)  18.1 us
    concatenate x4, local copies, waits for them, and re-layouts, padded_2(): block = jnp.concatenate([low, block, high], axis=dim)  11.5 us
    reduce_sum x3, other arithmetic, body(): curvature = lax.psum(jnp.sum(direction * image), ('gy', 'gx'))  10.1 us
    reduce_sum x2, other arithmetic, body(): rz_now = lax.psum(jnp.sum(residual * smoothed), ('gy', 'gx'))  9.47 us
  transfers between devices with their start and end apart: 28, of which 11 were waited for; matrix products, arithmetic and copies ran while one was open for 2% of the time, Pallas kernels for 0%

commit v1 on v0

v1 whole, which is shorter than its diff:
```python
import functools

import jax
import jax.numpy as jnp
from jax import lax
from jax.experimental import pallas as pl
from jax.experimental.pallas import tpu as pltpu
from jax.sharding import PartitionSpec as P

ITERS = 3
SHIFT = 1.0
SCALE = 4.0
LANES = 128
STRIP = 8
EDGE = 2 * STRIP

neighbour_steps = [(-1, -1), (-1, 0), (-1, 1), (0, -1), (0, 1), (1, -1), (1, 0), (1, 1)]

FIELDS = 6 + len(neighbour_steps)
REACH = 2 * ITERS
LOW_ROWS = [REACH, REACH - 1, REACH - 1, REACH - 2, REACH - 2, REACH - 2] + [
    REACH - 1 + down for down, _ in neighbour_steps
]
HIGH_ROWS = [REACH, REACH - 1, REACH - 1, REACH - 2, REACH - 2, REACH - 1] + [
    REACH - 1 - down for down, _ in neighbour_steps
]
PACKED = -(-max(sum(LOW_ROWS), sum(HIGH_ROWS)) // STRIP) * STRIP
PRODUCTS = (ITERS + 1) * ITERS
KEPT = 2 * ITERS + 1
VMEM_BYTES = 48 * 1024 * 1024


def field(refs, which, rows):
    right_side, mask, centre, ratio, faces, offdiag = refs
    if which == 0:
        return mask[rows, :].astype(jnp.float32) * right_side[rows, :]
    if which == 1:
        return mask[rows, :].astype(jnp.float32)
    if which == 2:
        return centre[rows, :]
    if which == 3:
        return ratio[rows, :]
    if which < 6:
        return faces[which - 4, rows, :]
    return offdiag[which - 6, rows, :]


def pack_rows_kernel(*refs):
    first, last = refs[0:6], refs[6:12]
    up, down = refs[12:14]
    place = 0
    for which, count in enumerate(LOW_ROWS):
        up[place : place + count, :] = field(last, which, slice(STRIP - count, STRIP))
        place += count
    if place < PACKED:
        up[place:PACKED, :] = jnp.zeros((PACKED - place, up.shape[1]), jnp.float32)
    place = 0
    for which, count in enumerate(HIGH_ROWS):
        down[place : place + count, :] = field(first, which, slice(0, count))
        place += count
    if place < PACKED:
        down[place:PACKED, :] = jnp.zeros((PACKED - place, down.shape[1]), jnp.float32)


def facing(west, east, side):
    lane = lax.broadcasted_iota(jnp.int32, west.shape, west.ndim - 1)
    return jnp.where(
        side == 0,
        jnp.where(lane >= LANES // 2, east, 0.0),
        jnp.where(lane < LANES // 2, west, 0.0),
    )


def pack_columns_kernel(*refs):
    west, east, out = refs[0:6], refs[6:12], refs[12]
    side = lax.axis_index("gx")
    everything = slice(None)
    for which in range(FIELDS):
        out[which] = facing(
            field(west, which, everything), field(east, which, everything), side
        )


def row_above(block, before):
    row = lax.broadcasted_iota(jnp.int32, block.shape, 0)
    return jnp.where(row == 0, pltpu.roll(before, 1, 0), pltpu.roll(block, 1, 0))


def row_below(block, after):
    row = lax.broadcasted_iota(jnp.int32, block.shape, 0)
    last = STRIP - 1
    return jnp.where(row == last, pltpu.roll(after, last, 0), pltpu.roll(block, last, 0))


def strip_rows(strip):
    return pl.ds(pl.multiple_of(strip * STRIP, STRIP), STRIP)


def krylov(load, strips, counted, sums, coef, kept):
    width = kept.shape[2]
    breadth = width - LANES
    zero = jnp.zeros((STRIP, width), jnp.float32)

    def west_of(block):
        return pltpu.roll(block, 1, 1)

    def east_of(block):
        return pltpu.roll(block, width - 1, 1)

    def prepare(step, south_after):
        strip = strips - 1 - step
        rows = strip_rows(strip)
        kept[0, rows, :] = load(0, strip)
        wet = load(1, strip)
        coef[4, rows, :] = load(2, strip)
        for index, (down, across) in enumerate(neighbour_steps):
            weight = load(6 + index, strip)
            if across == 1:
                weight = west_of(weight)
            elif across == -1:
                weight = east_of(weight)
            coef[(down + 1) * 3 + across + 1, rows, :] = weight
        west = load(4, strip)
        south = load(5, strip)
        east = east_of(west)
        north = row_below(south, south_after)
        scaled = wet * (1.0 / SCALE)
        coef[9, rows, :] = wet
        coef[10, rows, :] = scaled * (west + east + south + north + load(3, strip))
        coef[11, rows, :] = scaled * west
        coef[12, rows, :] = scaled * east
        coef[13, rows, :] = scaled * south
        coef[14, rows, :] = scaled * north
        return south

    lax.fori_loop(0, strips, prepare, zero)

    for order in range(ITERS):
        smoothed = ITERS + 1 + order

        def smooth(strip, carried):
            above, partial = carried
            rows = strip_rows(strip)
            block = kept[order, rows, :]
            shifted = {-1: east_of(block), 0: block, 1: west_of(block)}
            totals = []
            for down in range(3):
                totals.append(
                    coef[down * 3, rows, :] * shifted[-1]
                    + coef[down * 3 + 1, rows, :] * shifted[0]
                    + coef[down * 3 + 2, rows, :] * shifted[1]
                )
            row = lax.broadcasted_iota(jnp.int32, block.shape, 0)
            rising = pltpu.roll(totals[0], STRIP - 1, 0)
            falling = pltpu.roll(totals[2], 1, 0)
            done = strip_rows(jnp.maximum(strip - 1, 0))
            kept[smoothed, done, :] = coef[9, done, :] * (
                partial + jnp.where(row == STRIP - 1, rising, 0.0)
            )
            partial = (
                totals[1]
                + jnp.where(row == 0, above, falling)
                + jnp.where(row == STRIP - 1, 0.0, rising)
            )
            return falling, partial

        _, partial = lax.fori_loop(0, strips, smooth, (zero, zero))
        done = slice((strips - 1) * STRIP, strips * STRIP)
        kept[smoothed, done, :] = coef[9, done, :] * partial

        def operate(strip, carried):
            rows = strip_rows(strip)
            block = kept[smoothed, rows, :]
            before = kept[smoothed, strip_rows(jnp.maximum(strip - 1, 0)), :]
            after = kept[smoothed, strip_rows(jnp.minimum(strip + 1, strips - 1)), :]
            kept[order + 1, rows, :] = (
                coef[10, rows, :] * block
                - coef[11, rows, :] * west_of(block)
                - coef[12, rows, :] * east_of(block)
                - coef[13, rows, :] * row_above(block, before)
                - coef[14, rows, :] * row_below(block, after)
                - (SHIFT / SCALE) * kept[order, rows, :]
            )
            return carried

        lax.fori_loop(0, strips, operate, 0)

    def gather(step, totals):
        strip = counted(step)
        rows = strip_rows(strip)
        result = list(totals)
        for start in range(0, breadth, LANES):
            lanes = slice(start, start + LANES)
            bases = [kept[i, rows, lanes] for i in range(KEPT)]
            for i in range(ITERS + 1):
                for j in range(ITERS):
                    result[i * ITERS + j] += bases[i] * bases[ITERS + 1 + j]
        return tuple(result)

    return gather


def tile_kernel(*refs):
    own, columns, kept, sums, coef = refs[0:6], refs[6], refs[7], refs[8], refs[9]
    strips = kept.shape[1] // STRIP

    def load(which, strip):
        rows = strip_rows(strip)
        return jnp.concatenate(
            [field(own, which, rows), columns[which, rows, :]], axis=1
        )

    gather = krylov(load, strips, lambda step: step + 1, None, coef, kept)
    zero = jnp.zeros((STRIP, LANES), jnp.float32)
    totals = lax.fori_loop(0, strips - 2, gather, (zero,) * PRODUCTS)
    for index in range(PRODUCTS):
        sums[index] = totals[index]


def edge_kernel(*refs):
    first, last = refs[0:6], refs[6:12]
    columns_first, columns_last, low, high, corners, sums = refs[12:18]
    kept, gram = refs[18:20]
    joined, coef = refs[20:22]
    breadth = low.shape[1]
    width = breadth + LANES
    rows = kept.shape[1]
    everything = slice(0, EDGE)
    place_low, place_high = 0, PACKED
    for which in range(FIELDS):
        joined[which, 0:STRIP, :] = jnp.zeros((STRIP, width), jnp.float32)
        count = LOW_ROWS[which]
        target = slice(STRIP - count, STRIP)
        joined[which, target, 0:breadth] = low[place_low : place_low + count, :]
        joined[which, target, breadth:width] = corners[place_low : place_low + count, :]
        place_low += count
        target = slice(STRIP, STRIP + EDGE)
        joined[which, target, 0:breadth] = field(first, which, everything)
        joined[which, target, breadth:width] = columns_first[which]
        target = slice(STRIP + EDGE, STRIP + 2 * EDGE)
        joined[which, target, 0:breadth] = field(last, which, everything)
        joined[which, target, breadth:width] = columns_last[which]
        joined[which, rows - STRIP : rows, :] = jnp.zeros((STRIP, width), jnp.float32)
        count = HIGH_ROWS[which]
        target = slice(rows - STRIP, rows - STRIP + count)
        joined[which, target, 0:breadth] = high[
            place_high - PACKED : place_high - PACKED + count, :
        ]
        joined[which, target, breadth:width] = corners[place_high : place_high + count, :]
        place_high += count

    def load(which, strip):
        return joined[which, strip_rows(strip), :]

    gather = krylov(load, rows // STRIP, lambda step: 1 + 3 * step, None, coef, kept)
    totals = lax.fori_loop(0, 2, gather, tuple(sums[i] for i in range(PRODUCTS)))
    gram[...] = jnp.zeros(gram.shape, jnp.float32)
    for index in range(PRODUCTS):
        total = jnp.sum(jnp.sum(totals[index], axis=0, keepdims=True), axis=1, keepdims=True)
        gram[index : index + 1, :] = jnp.broadcast_to(total, (1, LANES))


def recurrences(gram):
    shift, scale = SHIFT, SCALE
    residual = [1.0]
    direction = []
    steps = [0.0] * ITERS
    rz_before = None
    for order in range(ITERS):
        rz = None
        for i in range(order + 1):
            inner = None
            for j in range(order + 1):
                term = residual[j] * gram[i][j]
                inner = term if inner is None else inner + term
            inner = residual[i] * inner
            rz = inner if rz is None else rz + inner
        if order == 0:
            direction = [1.0]
        else:
            ratio = rz / rz_before
            direction = [
                residual[i] + ratio * direction[i] if i < order else residual[i]
                for i in range(order + 1)
            ]
        image = [0.0] * (order + 2)
        for i in range(order + 1):
            image[i] = image[i] + shift * direction[i]
            image[i + 1] = image[i + 1] + scale * direction[i]
        curvature = None
        for i in range(order + 2):
            inner = None
            for j in range(order + 1):
                term = direction[j] * gram[i][j]
                inner = term if inner is None else inner + term
            inner = image[i] * inner
            curvature = inner if curvature is None else curvature + inner
        step = rz / curvature
        for i in range(order + 1):
            steps[i] = steps[i] + step * direction[i]
        residual = [
            (residual[i] if i < order + 1 else 0.0) - step * image[i]
            for i in range(order + 2)
        ]
        rz_before = rz
    return steps, residual


def combine_kernel(gram_ref, kept, edges, solution_ref, residual_ref):
    height, breadth = solution_ref.shape
    gram = [
        [gram_ref[i * ITERS + j : i * ITERS + j + 1, :] for j in range(ITERS)]
        for i in range(ITERS + 1)
    ]
    steps, residual = recurrences(gram)

    def wide(value):
        value = jnp.broadcast_to(value, (STRIP, LANES))
        return jnp.concatenate([value] * (breadth // LANES), axis=1)

    def put(source, rows_from, rows_to):
        total = None
        for j in range(ITERS):
            term = wide(steps[j]) * source[ITERS + 1 + j, rows_from, 0:breadth]
            total = term if total is None else total + term
        solution_ref[rows_to, :] = total
        total = None
        for i in range(ITERS + 1):
            term = wide(residual[i]) * source[i, rows_from, 0:breadth]
            total = term if total is None else total + term
        residual_ref[rows_to, :] = total

    put(edges, slice(STRIP, 2 * STRIP), slice(0, STRIP))
    put(edges, slice(4 * STRIP, 5 * STRIP), slice(height - STRIP, height))

    def middle(strip, carried):
        rows = strip_rows(strip)
        put(kept, rows, rows)
        return carried

    lax.fori_loop(1, height // STRIP - 1, middle, 0)


def params():
    return pltpu.CompilerParams(vmem_limit_bytes=VMEM_BYTES)


def cost(flops, moved):
    return pl.CostEstimate(flops=flops, bytes_accessed=moved, transcendentals=0)


def blocks(shapes, rows, columns, at):
    specs = []
    for shape in shapes:
        lead = tuple(shape[:-2])
        block = lead + (rows, columns)
        index = (0,) * len(lead) + at
        specs.append(pl.BlockSpec(block, lambda step, index=index: index))
    return specs


def whole(*shapes):
    return [pl.BlockSpec(shape, lambda step, n=len(shape): (0,) * n) for shape in shapes]


def body(right_side, faces, ratio, centre, offdiag, mask):
    height, breadth = right_side.shape
    width = breadth + LANES
    args = (right_side, mask, centre, ratio, faces, offdiag)
    shapes = [a.shape for a in args]
    f32 = jnp.float32
    side = lax.axis_index("gx")
    gy = lax.axis_size("gy")
    forward = [(i, i + 1) for i in range(gy - 1)]
    backward = [(b, a) for a, b in forward]
    swap = [(0, 1), (1, 0)]

    packed = jax.ShapeDtypeStruct((PACKED, breadth), f32)
    up, down = pl.pallas_call(
        pack_rows_kernel,
        grid=(1,),
        in_specs=blocks(shapes, STRIP, breadth, (0, 0))
        + blocks(shapes, STRIP, breadth, (height // STRIP - 1, 0)),
        out_specs=whole(packed.shape, packed.shape),
        out_shape=(packed, packed),
        compiler_params=params(),
        cost_estimate=cost(0, 2 * 4 * PACKED * breadth * 2),
        name="pack_rows",
    )(*args, *args)
    low = lax.ppermute(up, "gy", forward)
    high = lax.ppermute(down, "gy", backward)

    columns = jax.ShapeDtypeStruct((FIELDS, height, LANES), f32)
    columns = pl.pallas_call(
        pack_columns_kernel,
        grid=(1,),
        in_specs=blocks(shapes, height, LANES, (0, 0))
        + blocks(shapes, height, LANES, (0, breadth // LANES - 1)),
        out_specs=whole(columns.shape)[0],
        out_shape=columns,
        compiler_params=params(),
        cost_estimate=cost(0, 3 * 4 * FIELDS * height * LANES),
        name="pack_columns",
    )(*args, *args)
    columns = lax.ppermute(columns, "gx", swap)

    cells = height * width
    kept, sums = pl.pallas_call(
        tile_kernel,
        grid=(1,),
        in_specs=whole(*shapes, columns.shape),
        out_specs=whole((KEPT, height, width), (PRODUCTS, STRIP, LANES)),
        out_shape=(
            jax.ShapeDtypeStruct((KEPT, height, width), f32),
            jax.ShapeDtypeStruct((PRODUCTS, STRIP, LANES), f32),
        ),
        scratch_shapes=[pltpu.VMEM((15, height, width), f32)],
        compiler_params=params(),
        cost_estimate=cost(100 * cells, 4 * cells * (FIELDS + KEPT)),
        name="tile",
    )(*args, columns)

    received = jnp.concatenate([low, high], axis=0)
    corners = lax.ppermute(
        facing(received[:, :LANES], received[:, breadth - LANES :], side), "gx", swap
    )

    rows = 2 * (STRIP + EDGE)
    edges, gram = pl.pallas_call(
        edge_kernel,
        grid=(1,),
        in_specs=blocks(shapes, EDGE, breadth, (0, 0))
        + blocks(shapes, EDGE, breadth, (height // EDGE - 1, 0))
        + blocks([columns.shape], EDGE, LANES, (0, 0))
        + blocks([columns.shape], EDGE, LANES, (height // EDGE - 1, 0))
        + whole(low.shape, high.shape, corners.shape, sums.shape),
        out_specs=whole((KEPT, rows, width), (2 * STRIP, LANES)),
        out_shape=(
            jax.ShapeDtypeStruct((KEPT, rows, width), f32),
            jax.ShapeDtypeStruct((2 * STRIP, LANES), f32),
        ),
        scratch_shapes=[
            pltpu.VMEM((FIELDS, rows, width), f32),
            pltpu.VMEM((15, rows, width), f32),
        ],
        compiler_params=params(),
        cost_estimate=cost(100 * rows * width, 4 * rows * width * (FIELDS + KEPT)),
        name="edge",
    )(*args, *args, columns, columns, low, high, corners, sums)

    gram = gram + lax.ppermute(gram, "gx", swap)
    reach = 1
    while reach < gy:
        gram = gram + lax.ppermute(gram, "gy", [(i, i ^ reach) for i in range(gy)])
        reach *= 2

    tile = jax.ShapeDtypeStruct((height, breadth), f32)
    return pl.pallas_call(
        combine_kernel,
        grid=(1,),
        in_specs=whole(gram.shape, kept.shape, edges.shape),
        out_specs=whole(tile.shape, tile.shape),
        out_shape=(tile, tile),
        compiler_params=params(),
        cost_estimate=cost(14 * height * breadth, 4 * height * breadth * (KEPT + 2)),
        name="combine",
    )(gram, kept, edges)


def solution(mesh):
    return jax.shard_map(
        body,
        mesh=mesh,
        in_specs=(
            P(("members", "gy"), "gx"),
            P(None, "gy", "gx"),
            P("gy", "gx"),
            P("gy", "gx"),
            P(None, "gy", "gx"),
            P("gy", "gx"),
        ),
        out_specs=(P(("members", "gy"), "gx"), P(("members", "gy"), "gx")),
        check_vma=False,
    )
```

time: 297 us -> 72.2 us (0.24)
  blocking collectives: 153 us -> 0 us
  starting transfers between devices: 52.9 us -> 15.1 us
  Pallas kernels: 0 us -> 30 us
  other arithmetic: 27.8 us -> 0.03 us
  local copies, waits for them, and re-layouts: 23.6 us -> 7.81 us
  waiting for transfers between devices: 30.2 us -> 17.9 us
  between operations: 7.9 us -> 0.78 us
    psum x5 -> x0, blocking collectives: 153 us -> none  [the longest x3 92.6 us: body(): rz_now = lax.psum(jnp.sum(residual * smoothed), ('gy', 'gx'))]
    ppermute x28 -> x8, starting transfers between devices: 52.9 us -> 15.1 us  [the longest x3 8.46 us: body(): gram = gram + lax.ppermute(gram, 'gy', [(i, i ^ reach) for i in range(gy)])]
    pallas_call x0 -> x5, Pallas kernels: none -> 30 us  [the longest x1 16.7 us: body(): pl.pallas_call(tile_kernel, grid=(1,), in_specs=whole(*shapes, columns.sh...]
    reduce_sum x5 -> x0, other arithmetic: 19.5 us -> none  [the longest x3 10.1 us: body(): curvature = lax.psum(jnp.sum(direction * image), ('gy', 'gx'))]
    concatenate x5 -> x1, local copies, waits for them, and re-layouts: 14 us -> 0.98 us  [body(): received = jnp.concatenate([low, high], axis=0)]
    ppermute x28 -> x8, waiting for transfers between devices: 30.2 us -> 17.9 us  [the longest x1 12.2 us: body(): low = lax.ppermute(up, 'gy', forward)]
    sub x3 -> x0, other arithmetic: 3.62 us -> none  [body(): residual = residual - step_size * image]
    squeeze x1 -> x0, local copies, waits for them, and re-layouts: 3.26 us -> none  [body(): east_face = window(coefficients[0], margin, 0, 0, 1, height, breadth)]
  transfers between devices with their start and end apart: 28 -> 8, of which waited for: 11 -> 5; matrix products, arithmetic and copies ran while one was open for 2% -> 1% of each run, Pallas kernels for 0% -> 26%
where the time goes in v1:
time: 72.2 us; the launch traced here: 71.7 us
  Pallas kernels  30 us (42%)
  waiting for transfers between devices  17.9 us (25%)
  starting transfers between devices  15.1 us (21%)
  local copies, waits for them, and re-layouts  7.81 us (11%)
  between operations  0.78 us (1%)
    pallas_call x1, Pallas kernels, body(): pl.pallas_call(tile_kernel, grid=(1,), in_specs=whole(*shapes, columns.sh...  16.7 us
    ppermute x1, waiting for transfers between devices, body(): low = lax.ppermute(up, 'gy', forward)  12.2 us
    ppermute x3, starting transfers between devices, body(): gram = gram + lax.ppermute(gram, 'gy', [(i, i ^ reach) for i in range(gy)])  8.46 us
    pallas_call x1, Pallas kernels, body(): pl.pallas_call(edge_kernel, grid=(1,), in_specs=blocks(shapes, EDGE, brea...  7.45 us
    unnamed x25, local copies, waits for them, and re-layouts  6.83 us
    ppermute x3, waiting for transfers between devices, body(): gram = gram + lax.ppermute(gram, 'gy', [(i, i ^ reach) for i in range(gy)])  4.88 us
    ppermute x1, starting transfers between devices, body(): low = lax.ppermute(up, 'gy', forward)  4.33 us
    pallas_call x1, Pallas kernels, body(): pl.pallas_call(pack_columns_kernel, grid=(1,), in_specs=blocks(shapes, he...  2.29 us
  transfers between devices with their start and end apart: 8, of which 5 were waited for; matrix products, arithmetic and copies ran while one was open for 1% of the time, Pallas kernels for 26%

profile of v1, /device:TPU:0, one launch (start us, length us, event | category | flops | bytes accessed | tf_op | source)
XLA Modules:
  0.0 71.7 jit_solution(916401689225669955)
XLA Ops:
  0.6 0.0 copy-start
  0.6 1.2 %copy-done = f32[2,128,1024]{2,1,0:T(8,128)S(1)} copy-done((f32[2,128,1024]{2,1,0:T(8,128)S(1)}, f32[2,128,1024]{2,1,0:T(8,128)}, u32[]{:S(2)}) %copy-start) | copy-done | bytes 1048600
  1.9 1.0 %copy-done.2 = f32[128,1024]{1,0:T(8,128)S(1)} copy-done((f32[128,1024]{1,0:T(8,128)S(1)}, f32[128,1024]{1,0:T(8,128)}, u32[]{:S(2)}) %copy-start.2) | copy-done | bytes 524312
  2.9 1.0 %copy-done.4 = s32[128,1024]{1,0:T(8,128)S(1)} copy-done((s32[128,1024]{1,0:T(8,128)S(1)}, s32[128,1024]{1,0:T(8,128)}, u32[]{:S(2)}) %copy-start.4) | copy-done | bytes 524312
  3.9 1.0 %copy-done.6 = f32[128,1024]{1,0:T(8,128)S(1)} copy-done((f32[128,1024]{1,0:T(8,128)S(1)}, f32[128,1024]{1,0:T(8,128)}, u32[]{:S(2)}) %copy-start.6) | copy-done | bytes 524312
  5.0 1.0 %copy-done.8 = f32[128,1024]{1,0:T(8,128)S(1)} copy-done((f32[128,1024]{1,0:T(8,128)S(1)}, f32[128,1024]{1,0:T(8,128)}, u32[]{:S(2)}) %copy-start.8) | copy-done | bytes 524312
  6.0 2.3 %pack_columns.1 = f32[14,128,128]{2,1,0:T(8,128)} custom-call(f32[128,1024]{1,0:T(8,128)S(1)} %copy-done.2, s32[128,1024]{1,0:T(8,128)S(1)} %copy-done.4, f32[128,1024]{1,0:T(8,128)S(1)} %copy-done.6, f32[128,1024]{1,0:T(8,128)S(1)} %copy-done.8, f32[2,128,1024]{2,1,0:T(8,128)S(1)} %copy-done, f32[8,128,1024]{2,1,0:T(8,128)} %refs_11_.5, ...), custom_call_target="tpu_custom_call" | custom-call | bytes 2752512 | tf_op jit(solution)/shard_map/pack_columns/pallas_call | solution.py:394
  8.3 0.0 copy-start.9
  8.3 0.5 collective-permute-start
  8.9 2.2 %pack_rows.1 = (f32[72,1024]{1,0:T(8,128)}, f32[72,1024]{1,0:T(8,128)}) custom-call(f32[128,1024]{1,0:T(8,128)S(1)} %copy-done.2, s32[128,1024]{1,0:T(8,128)S(1)} %copy-done.4, f32[128,1024]{1,0:T(8,128)S(1)} %copy-done.6, f32[128,1024]{1,0:T(8,128)S(1)} %copy-done.8, f32[2,128,1024]{2,1,0:T(8,128)S(1)} %copy-done, f32[8,128,1024]{2,1,0:T(8,128)} %refs_11_.5, ...), custom_call_target="tpu_custom_call" | custom-call | bytes 1179648 | tf_op jit(solution)/shard_map/pack_rows/pallas_call | solution.py:379
  11.1 4.3 %collective-permute-start.1 = (f32[72,1024]{1,0:T(8,128)}, f32[72,1024]{1,0:T(8,128)S(1)}, u32[]{:S(2)}, u32[]{:S(2)}) collective-permute-start(f32[72,1024]{1,0:T(8,128)} %get-tuple-element.8), channel_id=1, source_target_pairs={{0,2},{2,4},{4,6},{6,8},{8,10},{10,12},{12,14},{1,3},{3,5},{5,7},{... | collective-permute-start | bytes 884744 | tf_op jit(solution)/shard_map/ppermute | solution.py:390
  15.4 1.3 %collective-permute-start.2 = (f32[72,1024]{1,0:T(8,128)}, f32[72,1024]{1,0:T(8,128)}, u32[]{:S(2)}, u32[]{:S(2)}) collective-permute-start(f32[72,1024]{1,0:T(8,128)} %get-tuple-element.9), channel_id=1, source_target_pairs={{2,0},{4,2},{6,4},{8,6},{10,8},{12,10},{14,12},{3,1},{5,3},{7,5},{... | collective-permute-start | bytes 884744 | tf_op jit(solution)/shard_map/ppermute | solution.py:391
  16.7 12.2 %collective-permute-done.1.refs_14_ = f32[72,1024]{1,0:T(8,128)S(1)} collective-permute-done((f32[72,1024]{1,0:T(8,128)}, f32[72,1024]{1,0:T(8,128)S(1)}, u32[]{:S(2)}, u32[]{:S(2)}) %collective-permute-start.1) | collective-permute-done | bytes 294944 | tf_op jit(solution)/shard_map/ppermute | solution.py:390
  29.0 0.0 collective-permute-done.2.refs_15_
  29.0 1.0 %constant_dynamic-update-slice_fusion = f32[144,1024]{1,0:T(8,128)S(1)} fusion(f32[144,1024]{1,0:T(8,128)S(1)} %constant_dynamic-update-slice_fusion.1, f32[72,1024]{1,0:T(8,128)} %collective-permute-done.2.refs_15_), kind=kLoop, calls=%fused_computation.3 | loop fusion | bytes 589824 | tf_op jit(solution)/shard_map/concatenate | solution.py:423
  30.0 0.1 collective-permute-start.3
  30.1 0.0 collective-permute-done.refs_6_.refs_12_.refs_13_
  30.1 0.0 copy-done.1
  30.1 0.0 copy-done.3
  30.1 16.7 %tile.1 = (f32[7,128,1152]{2,1,0:T(8,128)}, f32[12,8,128]{2,1,0:T(8,128)S(1)}) custom-call(f32[128,1024]{1,0:T(8,128)S(1)} %copy-done.3, s32[128,1024]{1,0:T(8,128)S(1)} %copy-done.5, f32[128,1024]{1,0:T(8,128)S(1)} %copy-done.7, f32[128,1024]{1,0:T(8,128)S(1)} %copy-done.9, f32[2,128,1024]{2,1,0:T(8,128)S(1)} %copy-done.1, f32[8,128,1024]{2,1,0:T(8,128)} %refs_11_.5, ...), custom_call_target="tpu_custom_call" | custom-call | flops 14745600 | bytes 12386304 | tf_op jit(solution)/shard_map/tile/pallas_call | solution.py:408
  46.8 0.0 collective-permute-done.3.refs_16_
  46.8 7.5 %edge.1 = (f32[7,48,1152]{2,1,0:T(8,128)}, f32[16,128]{1,0:T(8,128)S(1)}) custom-call(f32[128,1024]{1,0:T(8,128)S(1)} %copy-done.3, s32[128,1024]{1,0:T(8,128)S(1)} %copy-done.5, f32[128,1024]{1,0:T(8,128)S(1)} %copy-done.7, f32[128,1024]{1,0:T(8,128)S(1)} %copy-done.9, f32[2,128,1024]{2,1,0:T(8,128)S(1)} %copy-done.1, f32[8,128,1024]{2,1,0:T(8,128)} %refs_11_.5, ...), custom_call_target="tpu_custom_call" | custom-call | flops 5529600 | bytes 4644864 | tf_op jit(solution)/shard_map/edge/pallas_call | solution.py:429
  54.3 0.5 collective-permute-start.4
  54.8 0.8 %collective-permute-done.4 = f32[16,128]{1,0:T(8,128)S(1)} collective-permute-done((f32[16,128]{1,0:T(8,128)S(1)}, f32[16,128]{1,0:T(8,128)S(1)}, u32[]{:S(2)}, u32[]{:S(2)}) %collective-permute-start.4) | collective-permute-done | bytes 8224 | tf_op jit(solution)/shard_map/ppermute | solution.py:451
  55.6 2.4 %collective-permute-start.5 = (f32[16,128]{1,0:T(8,128)S(1)}, f32[16,128]{1,0:T(8,128)S(1)}, u32[]{:S(2)}, u32[]{:S(2)}) collective-permute-start(f32[16,128]{1,0:T(8,128)S(1)} %add.12), channel_id=1, source_target_pairs={{0,2},{2,0},{4,6},{6,4},{8,10},{10,8},{12,14},{14,12},{1,3},{3,1},... | collective-permute-start | bytes 24584 | tf_op jit(solution)/shard_map/ppermute | solution.py:454
  58.0 1.6 %collective-permute-done.5 = f32[16,128]{1,0:T(8,128)S(1)} collective-permute-done((f32[16,128]{1,0:T(8,128)S(1)}, f32[16,128]{1,0:T(8,128)S(1)}, u32[]{:S(2)}, u32[]{:S(2)}) %collective-permute-start.5) | collective-permute-done | bytes 8224 | tf_op jit(solution)/shard_map/ppermute | solution.py:454
  59.6 3.0 %collective-permute-start.6 = (f32[16,128]{1,0:T(8,128)S(1)}, f32[16,128]{1,0:T(8,128)S(1)}, u32[]{:S(2)}, u32[]{:S(2)}) collective-permute-start(f32[16,128]{1,0:T(8,128)S(1)} %add.13), channel_id=1, source_target_pairs={{0,4},{2,6},{4,0},{6,2},{8,12},{10,14},{12,8},{14,10},{1,5},{3,7},... | collective-permute-start | bytes 24584 | tf_op jit(solution)/shard_map/ppermute | solution.py:454
  62.7 1.6 %collective-permute-done.6 = f32[16,128]{1,0:T(8,128)S(1)} collective-permute-done((f32[16,128]{1,0:T(8,128)S(1)}, f32[16,128]{1,0:T(8,128)S(1)}, u32[]{:S(2)}, u32[]{:S(2)}) %collective-permute-start.6) | collective-permute-done | bytes 8224 | tf_op jit(solution)/shard_map/ppermute | solution.py:454
  64.3 3.0 %collective-permute-start.7 = (f32[16,128]{1,0:T(8,128)S(1)}, f32[16,128]{1,0:T(8,128)S(1)}, u32[]{:S(2)}, u32[]{:S(2)}) collective-permute-start(f32[16,128]{1,0:T(8,128)S(1)} %add.14), channel_id=1, source_target_pairs={{0,8},{2,10},{4,12},{6,14},{8,0},{10,2},{12,4},{14,6},{1,9},{3,11}... | collective-permute-start | bytes 24584 | tf_op jit(solution)/shard_map/ppermute | solution.py:454
  67.3 1.6 %collective-permute-done.7 = f32[16,128]{1,0:T(8,128)S(1)} collective-permute-done((f32[16,128]{1,0:T(8,128)S(1)}, f32[16,128]{1,0:T(8,128)S(1)}, u32[]{:S(2)}, u32[]{:S(2)}) %collective-permute-start.7) | collective-permute-done | bytes 8224 | tf_op jit(solution)/shard_map/ppermute | solution.py:454
  69.0 1.4 %copy-done.11 = f32[7,48,1152]{2,1,0:T(8,128)S(1)} copy-done((f32[7,48,1152]{2,1,0:T(8,128)S(1)}, f32[7,48,1152]{2,1,0:T(8,128)}, u32[]{:S(2)}) %copy-start.11) | copy-done | bytes 1548312
  70.4 1.3 %combine.1 = (f32[128,1024]{1,0:T(8,128)}, f32[128,1024]{1,0:T(8,128)}) custom-call(f32[16,128]{1,0:T(8,128)S(1)} %add.15.gram_ref, f32[7,128,1152]{2,1,0:T(8,128)S(1)} %copy-done.10, f32[7,48,1152]{2,1,0:T(8,128)S(1)} %copy-done.11), custom_call_target="tpu_custom_call" | custom-call | flops 1835008 | bytes 4718592 | tf_op jit(solution)/shard_map/combine/pallas_call | solution.py:458
  (21 shorter events, 0.1 us)
Async XLA Ops:
  0.6 1.2 %copy-start = (f32[2,128,1024]{2,1,0:T(8,128)S(1)}, f32[2,128,1024]{2,1,0:T(8,128)}, u32[]{:S(2)}) copy-start(f32[2,128,1024]{2,1,0:T(8,128)} %refs_10_.5) | copy-start | bytes 3145732
  1.9 1.0 %copy-start.2 = (f32[128,1024]{1,0:T(8,128)S(1)}, f32[128,1024]{1,0:T(8,128)}, u32[]{:S(2)}) copy-start(f32[128,1024]{1,0:T(8,128)} %refs_6_.5) | copy-start | bytes 1572868
  2.9 1.0 %copy-start.4 = (s32[128,1024]{1,0:T(8,128)S(1)}, s32[128,1024]{1,0:T(8,128)}, u32[]{:S(2)}) copy-start(s32[128,1024]{1,0:T(8,128)} %refs_7_.5) | copy-start | bytes 1572868
  3.9 1.0 %copy-start.6 = (f32[128,1024]{1,0:T(8,128)S(1)}, f32[128,1024]{1,0:T(8,128)}, u32[]{:S(2)}) copy-start(f32[128,1024]{1,0:T(8,128)} %refs_8_.5) | copy-start | bytes 1572868
  5.0 1.0 %copy-start.8 = (f32[128,1024]{1,0:T(8,128)S(1)}, f32[128,1024]{1,0:T(8,128)}, u32[]{:S(2)}) copy-start(f32[128,1024]{1,0:T(8,128)} %refs_9_.5) | copy-start | bytes 1572868
  8.3 21.8 %copy-start.1 = (f32[2,128,1024]{2,1,0:T(8,128)S(1)}, f32[2,128,1024]{2,1,0:T(8,128)}, u32[]{:S(2)}) copy-start(f32[2,128,1024]{2,1,0:T(8,128)} %refs_10_.5) | copy-start | bytes 3145732
  8.3 21.8 %copy-start.3 = (f32[128,1024]{1,0:T(8,128)S(1)}, f32[128,1024]{1,0:T(8,128)}, u32[]{:S(2)}) copy-start(f32[128,1024]{1,0:T(8,128)} %refs_6_.5) | copy-start | bytes 1572868
  8.3 21.8 %copy-start.5 = (s32[128,1024]{1,0:T(8,128)S(1)}, s32[128,1024]{1,0:T(8,128)}, u32[]{:S(2)}) copy-start(s32[128,1024]{1,0:T(8,128)} %refs_7_.5) | copy-start | bytes 1572868
  8.3 21.8 %copy-start.7 = (f32[128,1024]{1,0:T(8,128)S(1)}, f32[128,1024]{1,0:T(8,128)}, u32[]{:S(2)}) copy-start(f32[128,1024]{1,0:T(8,128)} %refs_8_.5) | copy-start | bytes 1572868
  8.3 21.8 %copy-start.9 = (f32[128,1024]{1,0:T(8,128)S(1)}, f32[128,1024]{1,0:T(8,128)}, u32[]{:S(2)}) copy-start(f32[128,1024]{1,0:T(8,128)} %refs_9_.5) | copy-start | bytes 1572868
  8.3 21.7 %collective-permute-start = (f32[14,128,128]{2,1,0:T(8,128)}, f32[14,128,128]{2,1,0:T(8,128)}, u32[]{:S(2)}, u32[]{:S(2)}) collective-permute-start(f32[14,128,128]{2,1,0:T(8,128)} %pack_columns.1), channel_id=1, source_target_pairs={{0,1},{1,0},{2,3},{3,2},{4,5},{5,4},{6,7},{7,6},{8,9},{9,8},{10,11... | collective-permute-start | bytes 2752520 | tf_op jit(solution)/shard_map/ppermute | solution.py:405
  11.1 17.9 %collective-permute-start.1 = (f32[72,1024]{1,0:T(8,128)}, f32[72,1024]{1,0:T(8,128)S(1)}, u32[]{:S(2)}, u32[]{:S(2)}) collective-permute-start(f32[72,1024]{1,0:T(8,128)} %get-tuple-element.8), channel_id=1, source_target_pairs={{0,2},{2,4},{4,6},{6,8},{8,10},{10,12},{12,14},{1,3},{3,5},{5,7},{... | collective-permute-start | bytes 884744 | tf_op jit(solution)/shard_map/ppermute | solution.py:390
  15.4 13.6 %collective-permute-start.2 = (f32[72,1024]{1,0:T(8,128)}, f32[72,1024]{1,0:T(8,128)}, u32[]{:S(2)}, u32[]{:S(2)}) collective-permute-start(f32[72,1024]{1,0:T(8,128)} %get-tuple-element.9), channel_id=1, source_target_pairs={{2,0},{4,2},{6,4},{8,6},{10,8},{12,10},{14,12},{3,1},{5,3},{7,5},{... | collective-permute-start | bytes 884744 | tf_op jit(solution)/shard_map/ppermute | solution.py:391
  30.0 16.8 %collective-permute-start.3 = (f32[144,128]{1,0:T(8,128)S(1)}, f32[144,128]{1,0:T(8,128)S(1)}, u32[]{:S(2)}, u32[]{:S(2)}) collective-permute-start(f32[144,128]{1,0:T(8,128)S(1)} %fusion), channel_id=1, source_target_pairs={{0,1},{1,0},{2,3},{3,2},{4,5},{5,4},{6,7},{7,6},{8,9},{9,8},{10,11... | collective-permute-start | bytes 221192 | tf_op jit(solution)/shard_map/ppermute | solution.py:424
  46.8 22.1 %copy-start.10 = (f32[7,128,1152]{2,1,0:T(8,128)S(1)}, f32[7,128,1152]{2,1,0:T(8,128)}, u32[]{:S(2)}) copy-start(f32[7,128,1152]{2,1,0:T(8,128)} %get-tuple-element.12.kept) | copy-start | bytes 12386308
  54.3 1.3 %collective-permute-start.4 = (f32[16,128]{1,0:T(8,128)S(1)}, f32[16,128]{1,0:T(8,128)S(1)}, u32[]{:S(2)}, u32[]{:S(2)}) collective-permute-start(f32[16,128]{1,0:T(8,128)S(1)} %get-tuple-element.11), channel_id=1, source_target_pairs={{0,1},{1,0},{2,3},{3,2},{4,5},{5,4},{6,7},{7,6},{8,9},{9,8},{10,11... | collective-permute-start | bytes 24584 | tf_op jit(solution)/shard_map/ppermute | solution.py:451
  55.6 4.0 %collective-permute-start.5 = (f32[16,128]{1,0:T(8,128)S(1)}, f32[16,128]{1,0:T(8,128)S(1)}, u32[]{:S(2)}, u32[]{:S(2)}) collective-permute-start(f32[16,128]{1,0:T(8,128)S(1)} %add.12), channel_id=1, source_target_pairs={{0,2},{2,0},{4,6},{6,4},{8,10},{10,8},{12,14},{14,12},{1,3},{3,1},... | collective-permute-start | bytes 24584 | tf_op jit(solution)/shard_map/ppermute | solution.py:454
  59.6 4.7 %collective-permute-start.6 = (f32[16,128]{1,0:T(8,128)S(1)}, f32[16,128]{1,0:T(8,128)S(1)}, u32[]{:S(2)}, u32[]{:S(2)}) collective-permute-start(f32[16,128]{1,0:T(8,128)S(1)} %add.13), channel_id=1, source_target_pairs={{0,4},{2,6},{4,0},{6,2},{8,12},{10,14},{12,8},{14,10},{1,5},{3,7},... | collective-permute-start | bytes 24584 | tf_op jit(solution)/shard_map/ppermute | solution.py:454
  64.3 4.7 %collective-permute-start.7 = (f32[16,128]{1,0:T(8,128)S(1)}, f32[16,128]{1,0:T(8,128)S(1)}, u32[]{:S(2)}, u32[]{:S(2)}) collective-permute-start(f32[16,128]{1,0:T(8,128)S(1)} %add.14), channel_id=1, source_target_pairs={{0,8},{2,10},{4,12},{6,14},{8,0},{10,2},{12,4},{14,6},{1,9},{3,11}... | collective-permute-start | bytes 24584 | tf_op jit(solution)/shard_map/ppermute | solution.py:454
  69.0 1.4 %copy-start.11 = (f32[7,48,1152]{2,1,0:T(8,128)S(1)}, f32[7,48,1152]{2,1,0:T(8,128)}, u32[]{:S(2)}) copy-start(f32[7,48,1152]{2,1,0:T(8,128)} %get-tuple-element.13.edges) | copy-start | bytes 4644868

commit v2 on v1

--- a/solution.py
+++ b/solution.py
@@ -27,7 +27,8 @@
 PACKED = -(-max(sum(LOW_ROWS), sum(HIGH_ROWS)) // STRIP) * STRIP
 PRODUCTS = (ITERS + 1) * ITERS
 KEPT = 2 * ITERS + 1
-VMEM_BYTES = 48 * 1024 * 1024
+VMEM_BYTES = 32 * 1024 * 1024
+PACK_VMEM_BYTES = 62 * 1024 * 1024
 
 
 def field(refs, which, rows):
@@ -72,7 +73,7 @@
 
 
 def pack_columns_kernel(*refs):
-    west, east, out = refs[0:6], refs[6:12], refs[12]
+    west, east, out = refs[0:6], refs[6:12], refs[13]
     side = lax.axis_index("gx")
     everything = slice(None)
     for which in range(FIELDS):
@@ -96,7 +97,7 @@
     return pl.ds(pl.multiple_of(strip * STRIP, STRIP), STRIP)
 
 
-def krylov(load, strips, counted, sums, coef, kept):
+def krylov(load, strips, counted, unroll, coef, kept):
     width = kept.shape[2]
     breadth = width - LANES
     zero = jnp.zeros((STRIP, width), jnp.float32)
@@ -133,7 +134,7 @@
         coef[14, rows, :] = scaled * north
         return south
 
-    lax.fori_loop(0, strips, prepare, zero)
+    lax.fori_loop(0, strips, prepare, zero, unroll=unroll)
 
     for order in range(ITERS):
         smoothed = ITERS + 1 + order
@@ -164,7 +165,7 @@
             )
             return falling, partial
 
-        _, partial = lax.fori_loop(0, strips, smooth, (zero, zero))
+        _, partial = lax.fori_loop(0, strips, smooth, (zero, zero), unroll=unroll)
         done = slice((strips - 1) * STRIP, strips * STRIP)
         kept[smoothed, done, :] = coef[9, done, :] * partial
 
@@ -183,7 +184,7 @@
             )
             return carried
 
-        lax.fori_loop(0, strips, operate, 0)
+        lax.fori_loop(0, strips, operate, 0, unroll=unroll)
 
     def gather(step, totals):
         strip = counted(step)
@@ -210,9 +211,9 @@
             [field(own, which, rows), columns[which, rows, :]], axis=1
         )
 
-    gather = krylov(load, strips, lambda step: step + 1, None, coef, kept)
+    gather = krylov(load, strips, lambda step: step + 1, 16, coef, kept)
     zero = jnp.zeros((STRIP, LANES), jnp.float32)
-    totals = lax.fori_loop(0, strips - 2, gather, (zero,) * PRODUCTS)
+    totals = lax.fori_loop(0, strips - 2, gather, (zero,) * PRODUCTS, unroll=2)
     for index in range(PRODUCTS):
         sums[index] = totals[index]
 
@@ -252,8 +253,8 @@
     def load(which, strip):
         return joined[which, strip_rows(strip), :]
 
-    gather = krylov(load, rows // STRIP, lambda step: 1 + 3 * step, None, coef, kept)
-    totals = lax.fori_loop(0, 2, gather, tuple(sums[i] for i in range(PRODUCTS)))
+    gather = krylov(load, rows // STRIP, lambda step: 1 + 3 * step, 6, coef, kept)
+    totals = lax.fori_loop(0, 2, gather, tuple(sums[i] for i in range(PRODUCTS)), unroll=2)
     gram[...] = jnp.zeros(gram.shape, jnp.float32)
     for index in range(PRODUCTS):
         total = jnp.sum(jnp.sum(totals[index], axis=0, keepdims=True), axis=1, keepdims=True)
@@ -341,8 +342,8 @@
     lax.fori_loop(1, height // STRIP - 1, middle, 0)
 
 
-def params():
-    return pltpu.CompilerParams(vmem_limit_bytes=VMEM_BYTES)
+def params(limit=VMEM_BYTES):
+    return pltpu.CompilerParams(vmem_limit_bytes=limit)
 
 
 def cost(flops, moved):
@@ -383,7 +384,7 @@
         + blocks(shapes, STRIP, breadth, (height // STRIP - 1, 0)),
         out_specs=whole(packed.shape, packed.shape),
         out_shape=(packed, packed),
-        compiler_params=params(),
+        compiler_params=params(PACK_VMEM_BYTES),
         cost_estimate=cost(0, 2 * 4 * PACKED * breadth * 2),
         name="pack_rows",
     )(*args, *args)
@@ -395,13 +396,14 @@
         pack_columns_kernel,
         grid=(1,),
         in_specs=blocks(shapes, height, LANES, (0, 0))
-        + blocks(shapes, height, LANES, (0, breadth // LANES - 1)),
+        + blocks(shapes, height, LANES, (0, breadth // LANES - 1))
+        + [pl.BlockSpec(memory_space=pl.ANY)],
         out_specs=whole(columns.shape)[0],
         out_shape=columns,
-        compiler_params=params(),
+        compiler_params=params(PACK_VMEM_BYTES),
         cost_estimate=cost(0, 3 * 4 * FIELDS * height * LANES),
         name="pack_columns",
-    )(*args, *args)
+    )(*args, *args, up)
     columns = lax.ppermute(columns, "gx", swap)
 
     cells = height * width
@@ -416,14 +418,15 @@
         ),
         scratch_shapes=[pltpu.VMEM((15, height, width), f32)],
         compiler_params=params(),
-        cost_estimate=cost(100 * cells, 4 * cells * (FIELDS + KEPT)),
+        cost_estimate=cost(100000 * cells, 4 * cells * (FIELDS + KEPT)),
         name="tile",
     )(*args, columns)
 
-    received = jnp.concatenate([low, high], axis=0)
-    corners = lax.ppermute(
-        facing(received[:, :LANES], received[:, breadth - LANES :], side), "gx", swap
+    sums, low, high = lax.optimization_barrier((sums, low, high))
+    corners = jnp.concatenate(
+        [facing(r[:, :LANES], r[:, breadth - LANES :], side) for r in (low, high)], axis=0
     )
+    corners = lax.ppermute(corners, "gx", swap)
 
     rows = 2 * (STRIP + EDGE)
     edges, gram = pl.pallas_call(

time: 72.2 us -> 43.1 us (0.60)
  Pallas kernels: 30 us -> 13.1 us
  waiting for transfers between devices: 17.9 us -> 8.61 us
  local copies, waits for them, and re-layouts: 7.81 us -> 5.32 us
    pallas_call x1, Pallas kernels: 16.7 us -> 5.08 us  [body(): pl.pallas_call(tile_kernel, grid=(1,), in_specs=whole(*shapes, columns.sh...]
    ppermute x1, waiting for transfers between devices: 12.2 us -> 1.45 us  [body(): low = lax.ppermute(up, 'gy', forward)]
    pallas_call x1, Pallas kernels: 7.45 us -> 1.89 us  [body(): pl.pallas_call(edge_kernel, grid=(1,), in_specs=blocks(shapes, EDGE, brea...]
    unnamed x25 -> x14, local copies, waits for them, and re-layouts: 6.83 us -> 5.32 us
    ppermute x1, waiting for transfers between devices: 0.01 us -> 1.25 us  [body(): corners = lax.ppermute(corners, 'gx', swap)]
    concatenate x1 -> x0, local copies, waits for them, and re-layouts: 0.98 us -> none  [body(): received = jnp.concatenate([low, high], axis=0)]
  transfers between devices with their start and end apart: 8 -> 8, of which waited for: 5 -> 6; matrix products, arithmetic and copies ran while one was open for 1% -> 0% of each run, Pallas kernels for 26% -> 12%
where the time goes in v2:
time: 43.1 us; the launch traced here: 42.8 us
  starting transfers between devices  14.9 us (35%)
  Pallas kernels  13.1 us (30%)
  waiting for transfers between devices  8.61 us (20%)
  local copies, waits for them, and re-layouts  5.32 us (12%)
  between operations  0.75 us (2%)
    ppermute x3, starting transfers between devices, body(): gram = gram + lax.ppermute(gram, 'gy', [(i, i ^ reach) for i in range(gy)])  8.5 us
    unnamed x14, local copies, waits for them, and re-layouts  5.32 us
    pallas_call x1, Pallas kernels, body(): pl.pallas_call(tile_kernel, grid=(1,), in_specs=whole(*shapes, columns.sh...  5.08 us
    ppermute x3, waiting for transfers between devices, body(): gram = gram + lax.ppermute(gram, 'gy', [(i, i ^ reach) for i in range(gy)])  4.88 us
    ppermute x1, starting transfers between devices, body(): low = lax.ppermute(up, 'gy', forward)  4.44 us
    pallas_call x1, Pallas kernels, body(): pl.pallas_call(pack_columns_kernel, grid=(1,), in_specs=blocks(shapes, he...  2.66 us
    pallas_call x1, Pallas kernels, body(): pl.pallas_call(pack_rows_kernel, grid=(1,), in_specs=blocks(shapes, STRIP...  2.15 us
    pallas_call x1, Pallas kernels, body(): pl.pallas_call(edge_kernel, grid=(1,), in_specs=blocks(shapes, EDGE, brea...  1.89 us
  transfers between devices with their start and end apart: 8, of which 6 were waited for; matrix products, arithmetic and copies ran while one was open for 0% of the time, Pallas kernels for 12%

profile of v2, /device:TPU:0, one launch (start us, length us, event | category | flops | bytes accessed | tf_op | source)
XLA Modules:
  0.0 42.8 jit_solution(1676025516125123296)
XLA Ops:
  0.6 2.2 %pack_rows.1 = (f32[72,1024]{1,0:T(8,128)}, f32[72,1024]{1,0:T(8,128)}) custom-call(f32[128,1024]{1,0:T(8,128)} %refs_6_.5, s32[128,1024]{1,0:T(8,128)} %refs_7_.5, f32[128,1024]{1,0:T(8,128)} %refs_8_.5, f32[128,1024]{1,0:T(8,128)} %refs_9_.5, f32[2,128,1024]{2,1,0:T(8,128)} %refs_10_.5, f32[8,128,1024]{2,1,0:T(8,128)} %refs_11_.5, f32[128,1024]{1,0:T(8,128)} %refs_6_.5, ...), custom_call_target="tpu_custom_call" | custom-call | bytes 1179648 | tf_op jit(solution)/shard_map/pack_rows/pallas_call | solution.py:380
  2.8 0.0 copy-start.6
  2.8 0.0 copy-start.1
  2.8 0.0 copy-start.2
  2.8 2.7 %pack_columns.1 = f32[14,128,128]{2,1,0:T(8,128)} custom-call(f32[128,1024]{1,0:T(8,128)} %refs_6_.5, s32[128,1024]{1,0:T(8,128)} %refs_7_.5, f32[128,1024]{1,0:T(8,128)} %refs_8_.5, f32[128,1024]{1,0:T(8,128)} %refs_9_.5, f32[2,128,1024]{2,1,0:T(8,128)} %refs_10_.5, f32[8,128,1024]{2,1,0:T(8,128)} %refs_11_.5, f32[128,1024]{1,0:T(8,128)} %refs_6_.5, ...), custom_call_target="tpu_custom_call" | custom-call | bytes 2752512 | tf_op jit(solution)/shard_map/pack_columns/pallas_call | solution.py:395
  5.5 0.5 %collective-permute-start = (f32[14,128,128]{2,1,0:T(8,128)}, f32[14,128,128]{2,1,0:T(8,128)S(1)}, u32[]{:S(2)}, u32[]{:S(2)}) collective-permute-start(f32[14,128,128]{2,1,0:T(8,128)} %pack_columns.1), channel_id=1, source_target_pairs={{0,1},{1,0},{2,3},{3,2},{4,5},{5,4},{6,7},{7,6},{8,9},{9,8},{10,11... | collective-permute-start | bytes 2752520 | tf_op jit(solution)/shard_map/ppermute | solution.py:407
  5.9 0.0 copy-done.6
  5.9 4.4 %collective-permute-start.1 = (f32[72,1024]{1,0:T(8,128)S(1)}, f32[72,1024]{1,0:T(8,128)S(1)}, u32[]{:S(2)}, u32[]{:S(2)}) collective-permute-start(f32[72,1024]{1,0:T(8,128)S(1)} %copy-done.6), channel_id=1, source_target_pairs={{0,2},{2,4},{4,6},{6,8},{8,10},{10,12},{12,14},{1,3},{3,5},{5,7},{... | collective-permute-start | bytes 884744 | tf_op jit(solution)/shard_map/ppermute | solution.py:391
  10.4 1.3 %collective-permute-start.2 = (f32[72,1024]{1,0:T(8,128)}, f32[72,1024]{1,0:T(8,128)S(1)}, u32[]{:S(2)}, u32[]{:S(2)}) collective-permute-start(f32[72,1024]{1,0:T(8,128)} %get-tuple-element.13), channel_id=1, source_target_pairs={{2,0},{4,2},{6,4},{8,6},{10,8},{12,10},{14,12},{3,1},{5,3},{7,5},{... | collective-permute-start | bytes 884744 | tf_op jit(solution)/shard_map/ppermute | solution.py:392
  11.7 0.0 collective-permute-done.refs_6_.refs_12_.refs_13_
  11.7 0.0 copy-done.1
  11.7 0.0 copy-done.2
  11.7 0.0 copy-start
  11.7 2.2 %copy-done = f32[8,128,1024]{2,1,0:T(8,128)S(1)} copy-done((f32[8,128,1024]{2,1,0:T(8,128)S(1)}, f32[8,128,1024]{2,1,0:T(8,128)}, u32[]{:S(2)}) %copy-start) | copy-done | bytes 4194328
  13.9 1.0 %copy-done.3 = s32[128,1024]{1,0:T(8,128)S(1)} copy-done((s32[128,1024]{1,0:T(8,128)S(1)}, s32[128,1024]{1,0:T(8,128)}, u32[]{:S(2)}) %copy-start.3) | copy-done | bytes 524312
  14.9 1.0 %copy-done.4 = f32[128,1024]{1,0:T(8,128)S(1)} copy-done((f32[128,1024]{1,0:T(8,128)S(1)}, f32[128,1024]{1,0:T(8,128)}, u32[]{:S(2)}) %copy-start.4) | copy-done | bytes 524312
  16.0 1.0 %copy-done.5 = f32[128,1024]{1,0:T(8,128)S(1)} copy-done((f32[128,1024]{1,0:T(8,128)S(1)}, f32[128,1024]{1,0:T(8,128)}, u32[]{:S(2)}) %copy-start.5) | copy-done | bytes 524312
  17.0 5.1 %tile.1 = (f32[7,128,1152]{2,1,0:T(8,128)S(1)}, f32[12,8,128]{2,1,0:T(8,128)S(1)}) custom-call(f32[128,1024]{1,0:T(8,128)S(1)} %copy-done.2, s32[128,1024]{1,0:T(8,128)S(1)} %copy-done.3, f32[128,1024]{1,0:T(8,128)S(1)} %copy-done.4, f32[128,1024]{1,0:T(8,128)S(1)} %copy-done.5, f32[2,128,1024]{2,1,0:T(8,128)S(1)} %copy-done.1, f32[8,128,1024]{2,1,0:T(8,128)S(1)} %copy-done, ...), custom_call_target="tpu_custom_call" | custom-call | flops 14745600000 | bytes 12386304 | tf_op jit(solution)/shard_map/tile/pallas_call | solution.py:410
  22.1 0.0 collective-permute-done.2.refs_15_
  22.1 1.4 %collective-permute-done.1.refs_14_ = f32[72,1024]{1,0:T(8,128)S(1)} collective-permute-done((f32[72,1024]{1,0:T(8,128)S(1)}, f32[72,1024]{1,0:T(8,128)S(1)}, u32[]{:S(2)}, u32[]{:S(2)}) %collective-permute-start.1) | collective-permute-done | bytes 294944 | tf_op jit(solution)/shard_map/ppermute | solution.py:391
  23.6 0.1 collective-permute-start.3
  23.7 1.3 %collective-permute-done.3.refs_16_ = f32[144,128]{1,0:T(8,128)S(1)} collective-permute-done((f32[144,128]{1,0:T(8,128)S(1)}, f32[144,128]{1,0:T(8,128)S(1)}, u32[]{:S(2)}, u32[]{:S(2)}) %collective-permute-start.3) | collective-permute-done | bytes 73760 | tf_op jit(solution)/shard_map/ppermute | solution.py:429
  24.9 1.9 %edge.1 = (f32[7,48,1152]{2,1,0:T(8,128)S(1)}, f32[16,128]{1,0:T(8,128)S(1)}) custom-call(f32[128,1024]{1,0:T(8,128)S(1)} %copy-done.2, s32[128,1024]{1,0:T(8,128)S(1)} %copy-done.3, f32[128,1024]{1,0:T(8,128)S(1)} %copy-done.4, f32[128,1024]{1,0:T(8,128)S(1)} %copy-done.5, f32[2,128,1024]{2,1,0:T(8,128)S(1)} %copy-done.1, f32[8,128,1024]{2,1,0:T(8,128)S(1)} %copy-done, ...), custom_call_target="tpu_custom_call" | custom-call | flops 5529600 | bytes 4644864 | tf_op jit(solution)/shard_map/edge/pallas_call | solution.py:432
  26.8 0.2 collective-permute-start.4
  27.0 1.0 %collective-permute-done.4 = f32[16,128]{1,0:T(8,128)S(1)} collective-permute-done((f32[16,128]{1,0:T(8,128)S(1)}, f32[16,128]{1,0:T(8,128)S(1)}, u32[]{:S(2)}, u32[]{:S(2)}) %collective-permute-start.4) | collective-permute-done | bytes 8224 | tf_op jit(solution)/shard_map/ppermute | solution.py:454
  28.0 2.5 %collective-permute-start.5 = (f32[16,128]{1,0:T(8,128)S(1)}, f32[16,128]{1,0:T(8,128)S(1)}, u32[]{:S(2)}, u32[]{:S(2)}) collective-permute-start(f32[16,128]{1,0:T(8,128)S(1)} %add.12), channel_id=1, source_target_pairs={{0,2},{2,0},{4,6},{6,4},{8,10},{10,8},{12,14},{14,12},{1,3},{3,1},... | collective-permute-start | bytes 24584 | tf_op jit(solution)/shard_map/ppermute | solution.py:457
  30.5 1.6 %collective-permute-done.5 = f32[16,128]{1,0:T(8,128)S(1)} collective-permute-done((f32[16,128]{1,0:T(8,128)S(1)}, f32[16,128]{1,0:T(8,128)S(1)}, u32[]{:S(2)}, u32[]{:S(2)}) %collective-permute-start.5) | collective-permute-done | bytes 8224 | tf_op jit(solution)/shard_map/ppermute | solution.py:457
  32.2 3.0 %collective-permute-start.6 = (f32[16,128]{1,0:T(8,128)S(1)}, f32[16,128]{1,0:T(8,128)S(1)}, u32[]{:S(2)}, u32[]{:S(2)}) collective-permute-start(f32[16,128]{1,0:T(8,128)S(1)} %add.13), channel_id=1, source_target_pairs={{0,4},{2,6},{4,0},{6,2},{8,12},{10,14},{12,8},{14,10},{1,5},{3,7},... | collective-permute-start | bytes 24584 | tf_op jit(solution)/shard_map/ppermute | solution.py:457
  35.1 1.6 %collective-permute-done.6 = f32[16,128]{1,0:T(8,128)S(1)} collective-permute-done((f32[16,128]{1,0:T(8,128)S(1)}, f32[16,128]{1,0:T(8,128)S(1)}, u32[]{:S(2)}, u32[]{:S(2)}) %collective-permute-start.6) | collective-permute-done | bytes 8224 | tf_op jit(solution)/shard_map/ppermute | solution.py:457
  36.8 3.0 %collective-permute-start.7 = (f32[16,128]{1,0:T(8,128)S(1)}, f32[16,128]{1,0:T(8,128)S(1)}, u32[]{:S(2)}, u32[]{:S(2)}) collective-permute-start(f32[16,128]{1,0:T(8,128)S(1)} %add.14), channel_id=1, source_target_pairs={{0,8},{2,10},{4,12},{6,14},{8,0},{10,2},{12,4},{14,6},{1,9},{3,11}... | collective-permute-start | bytes 24584 | tf_op jit(solution)/shard_map/ppermute | solution.py:457
  39.8 1.6 %collective-permute-done.7 = f32[16,128]{1,0:T(8,128)S(1)} collective-permute-done((f32[16,128]{1,0:T(8,128)S(1)}, f32[16,128]{1,0:T(8,128)S(1)}, u32[]{:S(2)}, u32[]{:S(2)}) %collective-permute-start.7) | collective-permute-done | bytes 8224 | tf_op jit(solution)/shard_map/ppermute | solution.py:457
  41.4 1.3 %combine.1 = (f32[128,1024]{1,0:T(8,128)}, f32[128,1024]{1,0:T(8,128)}) custom-call(f32[16,128]{1,0:T(8,128)S(1)} %add.15.gram_ref, f32[7,128,1152]{2,1,0:T(8,128)S(1)} %get-tuple-element.18.kept, f32[7,48,1152]{2,1,0:T(8,128)S(1)} %get-tuple-element.19.edges), custom_call_target="tpu_custom_call" | custom-call | flops 1835008 | bytes 4718592 | tf_op jit(solution)/shard_map/combine/pallas_call | solution.py:461
  (10 shorter events, 0.0 us)
Async XLA Ops:
  2.8 3.1 %copy-start.6 = (f32[72,1024]{1,0:T(8,128)S(1)}, f32[72,1024]{1,0:T(8,128)}, u32[]{:S(2)}) copy-start(f32[72,1024]{1,0:T(8,128)} %get-tuple-element.11.refs_12_) | copy-start | bytes 884740
  2.8 8.9 %copy-start.1 = (f32[2,128,1024]{2,1,0:T(8,128)S(1)}, f32[2,128,1024]{2,1,0:T(8,128)}, u32[]{:S(2)}) copy-start(f32[2,128,1024]{2,1,0:T(8,128)} %refs_10_.5) | copy-start | bytes 3145732
  2.8 8.9 %copy-start.2 = (f32[128,1024]{1,0:T(8,128)S(1)}, f32[128,1024]{1,0:T(8,128)}, u32[]{:S(2)}) copy-start(f32[128,1024]{1,0:T(8,128)} %refs_6_.5) | copy-start | bytes 1572868
  5.5 6.2 %collective-permute-start = (f32[14,128,128]{2,1,0:T(8,128)}, f32[14,128,128]{2,1,0:T(8,128)S(1)}, u32[]{:S(2)}, u32[]{:S(2)}) collective-permute-start(f32[14,128,128]{2,1,0:T(8,128)} %pack_columns.1), channel_id=1, source_target_pairs={{0,1},{1,0},{2,3},{3,2},{4,5},{5,4},{6,7},{7,6},{8,9},{9,8},{10,11... | collective-permute-start | bytes 2752520 | tf_op jit(solution)/shard_map/ppermute | solution.py:407
  5.9 17.7 %collective-permute-start.1 = (f32[72,1024]{1,0:T(8,128)S(1)}, f32[72,1024]{1,0:T(8,128)S(1)}, u32[]{:S(2)}, u32[]{:S(2)}) collective-permute-start(f32[72,1024]{1,0:T(8,128)S(1)} %copy-done.6), channel_id=1, source_target_pairs={{0,2},{2,4},{4,6},{6,8},{8,10},{10,12},{12,14},{1,3},{3,5},{5,7},{... | collective-permute-start | bytes 884744 | tf_op jit(solution)/shard_map/ppermute | solution.py:391
  10.4 11.8 %collective-permute-start.2 = (f32[72,1024]{1,0:T(8,128)}, f32[72,1024]{1,0:T(8,128)S(1)}, u32[]{:S(2)}, u32[]{:S(2)}) collective-permute-start(f32[72,1024]{1,0:T(8,128)} %get-tuple-element.13), channel_id=1, source_target_pairs={{2,0},{4,2},{6,4},{8,6},{10,8},{12,10},{14,12},{3,1},{5,3},{7,5},{... | collective-permute-start | bytes 884744 | tf_op jit(solution)/shard_map/ppermute | solution.py:392
  11.7 2.2 %copy-start = (f32[8,128,1024]{2,1,0:T(8,128)S(1)}, f32[8,128,1024]{2,1,0:T(8,128)}, u32[]{:S(2)}) copy-start(f32[8,128,1024]{2,1,0:T(8,128)} %refs_11_.5) | copy-start | bytes 12582916
  13.9 1.0 %copy-start.3 = (s32[128,1024]{1,0:T(8,128)S(1)}, s32[128,1024]{1,0:T(8,128)}, u32[]{:S(2)}) copy-start(s32[128,1024]{1,0:T(8,128)} %refs_7_.5) | copy-start | bytes 1572868
  14.9 1.0 %copy-start.4 = (f32[128,1024]{1,0:T(8,128)S(1)}, f32[128,1024]{1,0:T(8,128)}, u32[]{:S(2)}) copy-start(f32[128,1024]{1,0:T(8,128)} %refs_8_.5) | copy-start | bytes 1572868
  16.0 1.0 %copy-start.5 = (f32[128,1024]{1,0:T(8,128)S(1)}, f32[128,1024]{1,0:T(8,128)}, u32[]{:S(2)}) copy-start(f32[128,1024]{1,0:T(8,128)} %refs_9_.5) | copy-start | bytes 1572868
  23.6 1.3 %collective-permute-start.3 = (f32[144,128]{1,0:T(8,128)S(1)}, f32[144,128]{1,0:T(8,128)S(1)}, u32[]{:S(2)}, u32[]{:S(2)}) collective-permute-start(f32[144,128]{1,0:T(8,128)S(1)} %pad_maximum_fusion), channel_id=1, source_target_pairs={{0,1},{1,0},{2,3},{3,2},{4,5},{5,4},{6,7},{7,6},{8,9},{9,8},{10,11... | collective-permute-start | bytes 221192 | tf_op jit(solution)/shard_map/ppermute | solution.py:429
  26.8 1.2 %collective-permute-start.4 = (f32[16,128]{1,0:T(8,128)S(1)}, f32[16,128]{1,0:T(8,128)S(1)}, u32[]{:S(2)}, u32[]{:S(2)}) collective-permute-start(f32[16,128]{1,0:T(8,128)S(1)} %get-tuple-element.17), channel_id=1, source_target_pairs={{0,1},{1,0},{2,3},{3,2},{4,5},{5,4},{6,7},{7,6},{8,9},{9,8},{10,11... | collective-permute-start | bytes 24584 | tf_op jit(solution)/shard_map/ppermute | solution.py:454
  28.0 4.1 %collective-permute-start.5 = (f32[16,128]{1,0:T(8,128)S(1)}, f32[16,128]{1,0:T(8,128)S(1)}, u32[]{:S(2)}, u32[]{:S(2)}) collective-permute-start(f32[16,128]{1,0:T(8,128)S(1)} %add.12), channel_id=1, source_target_pairs={{0,2},{2,0},{4,6},{6,4},{8,10},{10,8},{12,14},{14,12},{1,3},{3,1},... | collective-permute-start | bytes 24584 | tf_op jit(solution)/shard_map/ppermute | solution.py:457
  32.2 4.6 %collective-permute-start.6 = (f32[16,128]{1,0:T(8,128)S(1)}, f32[16,128]{1,0:T(8,128)S(1)}, u32[]{:S(2)}, u32[]{:S(2)}) collective-permute-start(f32[16,128]{1,0:T(8,128)S(1)} %add.13), channel_id=1, source_target_pairs={{0,4},{2,6},{4,0},{6,2},{8,12},{10,14},{12,8},{14,10},{1,5},{3,7},... | collective-permute-start | bytes 24584 | tf_op jit(solution)/shard_map/ppermute | solution.py:457
  36.8 4.7 %collective-permute-start.7 = (f32[16,128]{1,0:T(8,128)S(1)}, f32[16,128]{1,0:T(8,128)S(1)}, u32[]{:S(2)}, u32[]{:S(2)}) collective-permute-start(f32[16,128]{1,0:T(8,128)S(1)} %add.14), channel_id=1, source_target_pairs={{0,8},{2,10},{4,12},{6,14},{8,0},{10,2},{12,4},{14,6},{1,9},{3,11}... | collective-permute-start | bytes 24584 | tf_op jit(solution)/shard_map/ppermute | solution.py:457

commit v3 on v2

v3 whole, which is shorter than its diff:
```python
import functools

import jax
import jax.numpy as jnp
from jax import lax
from jax.experimental import pallas as pl
from jax.experimental.pallas import tpu as pltpu
from jax.sharding import PartitionSpec as P

ITERS = 3
SHIFT = 1.0
SCALE = 4.0
LANES = 128
STRIP = 8

neighbour_steps = [(-1, -1), (-1, 0), (-1, 1), (0, -1), (0, 1), (1, -1), (1, 0), (1, 1)]

FIELDS = 6 + len(neighbour_steps)
REACH = 2 * ITERS
LOW_ROWS = [REACH, REACH - 1, REACH - 1, REACH - 2, REACH - 2, REACH - 2] + [
    REACH - 1 + down for down, _ in neighbour_steps
]
HIGH_ROWS = [REACH, REACH - 1, REACH - 1, REACH - 2, REACH - 2, REACH - 1] + [
    REACH - 1 - down for down, _ in neighbour_steps
]
PACKED = -(-max(sum(LOW_ROWS), sum(HIGH_ROWS)) // STRIP) * STRIP
PRODUCTS = (ITERS + 1) * ITERS
KEPT = 2 * ITERS + 1
SLOT = 8
COEFFICIENTS = 15
NEAR = 2 * COEFFICIENTS
SOUTH = NEAR + 6
FIRST = SOUTH + 1
BASIS = FIRST + 2
HANDED = BASIS + 2 * KEPT
TILE_VMEM_BYTES = 40 * 1024 * 1024
VMEM_BYTES = 32 * 1024 * 1024
PACK_VMEM_BYTES = 62 * 1024 * 1024


def field(refs, which, rows):
    right_side, mask, centre, ratio, faces, offdiag = refs
    if which == 0:
        return mask[rows, :].astype(jnp.float32) * right_side[rows, :]
    if which == 1:
        return mask[rows, :].astype(jnp.float32)
    if which == 2:
        return centre[rows, :]
    if which == 3:
        return ratio[rows, :]
    if which < 6:
        return faces[which - 4, rows, :]
    return offdiag[which - 6, rows, :]


def trimmed(out, refs, counts, at_end):
    place = 0
    for which, count in enumerate(counts):
        rows = slice(STRIP - count, STRIP) if at_end else slice(0, count)
        out[place : place + count, :] = field(refs, which, rows)
        place += count
    if place < PACKED:
        out[place:PACKED, :] = jnp.zeros((PACKED - place, out.shape[1]), jnp.float32)


def lanes_of(shape):
    return lax.broadcasted_iota(jnp.int32, shape, len(shape) - 1)


def squeezed(near, side):
    start = jnp.where(side == 0, SLOT, 0)
    total = None
    for which in range(FIELDS):
        block = pltpu.roll(near(which), start + SLOT * which, 1)
        if total is None:
            lane = lanes_of(block.shape)
            total = jnp.zeros(block.shape, jnp.float32)
        inside = (lane >= SLOT * which) & (lane < SLOT * (which + 1))
        total = jnp.where(inside, block, total)
    return total


def spread(block, side):
    lane = lanes_of(block.shape)
    start = jnp.where(side == 0, LANES, LANES - SLOT)
    first = jnp.where(side == 0, 0, LANES - SLOT)
    inside = ((lane >= first) & (lane < first + SLOT)).astype(jnp.float32)
    return [
        pltpu.roll(block, start - SLOT * which, 1) * inside for which in range(FIELDS)
    ]


def pack_kernel(*refs):
    args = refs[0:6]
    even, odd, even_corner, odd_corner, columns = refs[6:11]
    ends, sides, end_arrived, side_arrived = refs[11:17], refs[17:23], refs[23], refs[24]
    height, breadth = args[0].shape
    side = lax.axis_index("gx")
    parity = lax.rem(lax.axis_index("gy"), 2)
    beside = pl.multiple_of(jnp.where(side == 0, breadth - LANES, 0), LANES)
    copies, more = [], []
    for index, (arg, end, edge) in enumerate(zip(args, ends, sides)):
        lead = (slice(None),) * (len(arg.shape) - 2)
        for which, start in enumerate((0, height - STRIP)):
            copies.append(
                pltpu.make_async_copy(
                    arg.at[lead + (pl.ds(start, STRIP), slice(None))],
                    end.at[which],
                    end_arrived.at[index, which],
                )
            )
        more.append(
            pltpu.make_async_copy(
                arg.at[lead + (slice(None), pl.ds(beside, LANES))],
                edge,
                side_arrived.at[index],
            )
        )
    for copy in copies + more:
        copy.start()
    for copy in copies:
        copy.wait()
    first = [end.at[0] for end in ends]
    last = [end.at[1] for end in ends]

    @pl.when(parity == 0)
    def _():
        trimmed(even, last, LOW_ROWS, True)
        trimmed(odd, first, HIGH_ROWS, False)

    @pl.when(parity != 0)
    def _():
        trimmed(even, first, HIGH_ROWS, False)
        trimmed(odd, last, LOW_ROWS, True)

    for copy in more:
        copy.wait()
    packed = squeezed(lambda which: field(sides, which, slice(None)), side)
    columns[...] = packed
    corner_first, corner_last = packed[0:STRIP, :], packed[height - STRIP : height, :]
    even_corner[...] = jnp.where(parity == 0, corner_last, corner_first)
    odd_corner[...] = jnp.where(parity == 0, corner_first, corner_last)


def row_above(block, before):
    row = lax.broadcasted_iota(jnp.int32, block.shape, 0)
    return jnp.where(row == 0, pltpu.roll(before, 1, 0), pltpu.roll(block, 1, 0))


def row_below(block, after):
    row = lax.broadcasted_iota(jnp.int32, block.shape, 0)
    last = STRIP - 1
    return jnp.where(row == last, pltpu.roll(after, last, 0), pltpu.roll(block, last, 0))


def strip_rows(strip):
    return pl.ds(pl.multiple_of(strip * STRIP, STRIP), STRIP)


def west_of(block):
    return pltpu.roll(block, 1, 1)


def east_of(block):
    return pltpu.roll(block, block.shape[1] - 1, 1)


def coefficients(get, south_after):
    result = [None] * COEFFICIENTS
    wet = get(1)
    result[4] = get(2)
    for index, (down, across) in enumerate(neighbour_steps):
        weight = get(6 + index)
        if across == 1:
            weight = west_of(weight)
        elif across == -1:
            weight = east_of(weight)
        result[(down + 1) * 3 + across + 1] = weight
    west = get(4)
    south = get(5)
    east = east_of(west)
    north = row_below(south, south_after)
    scaled = wet * (1.0 / SCALE)
    result[9] = wet
    result[10] = scaled * (west + east + south + north + get(3))
    result[11] = scaled * west
    result[12] = scaled * east
    result[13] = scaled * south
    result[14] = scaled * north
    return result, south


def weighted(get, block, downs=(0, 1, 2)):
    left, right = east_of(block), west_of(block)
    return [
        get(down * 3) * left + get(down * 3 + 1) * block + get(down * 3 + 2) * right
        for down in downs
    ]


def applied(get, block, before, after, old):
    return (
        get(10) * block
        - get(11) * west_of(block)
        - get(12) * east_of(block)
        - get(13) * row_above(block, before)
        - get(14) * row_below(block, after)
        - (SHIFT / SCALE) * old
    )


def gathered(totals, kept, rows, breadth):
    result = list(totals)
    for start in range(0, breadth, LANES):
        bases = [kept[i, rows, start : start + LANES] for i in range(KEPT)]
        for i in range(ITERS + 1):
            for j in range(ITERS):
                result[i * ITERS + j] += bases[i] * bases[ITERS + 1 + j]
    return tuple(result)


def krylov(load, strips, coef, kept, arrive):
    width = kept.shape[2]
    zero = jnp.zeros((STRIP, width), jnp.float32)

    def prepare(step, south_after):
        strip = strips - 1 - step
        rows = strip_rows(strip)
        kept[0, rows, :] = load(0, strip)
        values, south = coefficients(lambda which: load(which, strip), south_after)
        for index, value in enumerate(values):
            coef[index, rows, :] = value
        return south

    south = zero
    half = strips // 2
    for start in (0, half):
        arrive(start)
        south = lax.fori_loop(start, start + half, prepare, south, unroll=half)

    for order in range(ITERS):
        smoothed = ITERS + 1 + order

        def smooth(strip, carried):
            above, partial = carried
            rows = strip_rows(strip)
            totals = weighted(lambda k: coef[k, rows, :], kept[order, rows, :])
            row = lax.broadcasted_iota(jnp.int32, totals[0].shape, 0)
            rising = pltpu.roll(totals[0], STRIP - 1, 0)
            falling = pltpu.roll(totals[2], 1, 0)
            done = strip_rows(jnp.maximum(strip - 1, 0))
            kept[smoothed, done, :] = coef[9, done, :] * (
                partial + jnp.where(row == STRIP - 1, rising, 0.0)
            )
            partial = (
                totals[1]
                + jnp.where(row == 0, above, falling)
                + jnp.where(row == STRIP - 1, 0.0, rising)
            )
            return falling, partial

        _, partial = lax.fori_loop(0, strips, smooth, (zero, zero), unroll=strips)
        done = slice((strips - 1) * STRIP, strips * STRIP)
        kept[smoothed, done, :] = coef[9, done, :] * partial

        def operate(strip, carried):
            rows = strip_rows(strip)
            kept[order + 1, rows, :] = applied(
                lambda k: coef[k, rows, :],
                kept[smoothed, rows, :],
                kept[smoothed, strip_rows(jnp.maximum(strip - 1, 0)), :],
                kept[smoothed, strip_rows(jnp.minimum(strip + 1, strips - 1)), :],
                kept[order, rows, :],
            )
            return carried

        lax.fori_loop(0, strips, operate, 0, unroll=strips)


def tile_kernel(*refs):
    args, columns, kept, sums, handed, coef, wide = refs[0:6], *refs[6:12]
    own, arrived = refs[12:18], refs[18]
    strips = kept.shape[1] // STRIP
    half = strips // 2 * STRIP
    side = lax.axis_index("gx")
    copies = []
    for part in (1, 0):
        rows = pl.ds(part * half, half)
        for index, (arg, buffer) in enumerate(zip(args, own)):
            place = (slice(None),) * (len(arg.shape) - 2) + (rows, slice(None))
            copies.append(
                pltpu.make_async_copy(
                    arg.at[place], buffer.at[place], arrived.at[index, part]
                )
            )
    for copy in copies:
        copy.start()

    def arrive(start):
        for copy in copies[:6] if start == 0 else copies[6:]:
            copy.wait()

    for which, block in enumerate(spread(columns[...], side)):
        wide[which] = block

    def load(which, strip):
        rows = strip_rows(strip)
        return jnp.concatenate([field(own, which, rows), wide[which, rows, :]], axis=1)

    krylov(load, strips, coef, kept, arrive)
    zero = jnp.zeros((STRIP, LANES), jnp.float32)
    breadth = kept.shape[2] - LANES
    totals = lax.fori_loop(
        1,
        strips - 1,
        lambda strip, totals: gathered(totals, kept, strip_rows(strip), breadth),
        (zero,) * PRODUCTS,
        unroll=2,
    )
    for index in range(PRODUCTS):
        sums[index] = totals[index]
    first, last = slice(0, STRIP), slice((strips - 1) * STRIP, strips * STRIP)
    second, third = slice(STRIP, 2 * STRIP), slice((strips - 2) * STRIP, (strips - 1) * STRIP)
    for index in range(COEFFICIENTS):
        handed[index] = coef[index, first, :]
        handed[COEFFICIENTS + index] = coef[index, last, :]
    for index in range(3):
        handed[NEAR + index] = coef[index, second, :]
        handed[NEAR + 3 + index] = coef[6 + index, third, :]
    handed[SOUTH] = load(5, 0)
    handed[FIRST] = kept[0, first, :]
    handed[FIRST + 1] = kept[0, last, :]
    for index in range(KEPT):
        handed[BASIS + index] = kept[index, second, :]
        handed[BASIS + KEPT + index] = kept[index, third, :]


def edge_kernel(
    handed, even, odd, even_corner, odd_corner, sums, kept, gram, joined, coef, outer
):
    breadth = even.shape[1]
    width = breadth + LANES
    side = lax.axis_index("gx")
    parity = lax.rem(lax.axis_index("gy"), 2)
    low_corner = spread(jnp.where(parity == 0, odd_corner[...], even_corner[...]), side)
    high_corner = spread(jnp.where(parity == 0, even_corner[...], odd_corner[...]), side)
    low_rows, high_rows = slice(0, STRIP), slice(STRIP, 2 * STRIP)
    place_low, place_high = 0, 0
    for which in range(FIELDS):
        joined[which, :, 0:breadth] = jnp.zeros((2 * STRIP, breadth), jnp.float32)
        joined[which, low_rows, breadth:width] = low_corner[which]
        joined[which, high_rows, breadth:width] = high_corner[which]
        count = LOW_ROWS[which]
        place = slice(place_low, place_low + count)
        joined[which, STRIP - count : STRIP, 0:breadth] = jnp.where(
            parity == 0, odd[place, :], even[place, :]
        )
        place_low += count
        count = HIGH_ROWS[which]
        place = slice(place_high, place_high + count)
        joined[which, STRIP : STRIP + count, 0:breadth] = jnp.where(
            parity == 0, even[place, :], odd[place, :]
        )
        place_high += count

    zero = jnp.zeros((STRIP, width), jnp.float32)
    values, _ = coefficients(lambda which: joined[which, low_rows, :], handed[SOUTH])
    for index, value in enumerate(values):
        coef[index, low_rows, :] = value
    values, south = coefficients(lambda which: joined[which, high_rows, :], zero)
    for index, value in enumerate(values):
        coef[index, high_rows, :] = value
    row = lax.broadcasted_iota(jnp.int32, zero.shape, 0)
    missing = (
        handed[COEFFICIENTS + 9]
        * (1.0 / SCALE)
        * jnp.where(row == STRIP - 1, pltpu.roll(south, STRIP - 1, 0), 0.0)
    )

    def getter(strip):
        if strip == 0:
            return lambda k: coef[k, low_rows, :]
        if strip == 3:
            return lambda k: coef[k, high_rows, :]
        if strip == 1:
            return lambda k: handed[k]
        return lambda k: handed[COEFFICIENTS + k] + (missing if k in (10, 14) else 0.0)

    getters = [getter(strip) for strip in range(4)]
    inner = [slice(0, STRIP), slice(STRIP, 2 * STRIP)]

    def write(index, strip, value):
        if strip in (1, 2):
            kept[index, inner[strip - 1], :] = value
        else:
            outer[index, low_rows if strip == 0 else high_rows, :] = value

    def read(index, strip):
        if strip in (1, 2):
            return kept[index, inner[strip - 1], :]
        return outer[index, low_rows if strip == 0 else high_rows, :]

    write(0, 0, joined[0, low_rows, :])
    write(0, 3, joined[0, high_rows, :])
    write(0, 1, handed[FIRST])
    write(0, 2, handed[FIRST + 1])
    for order in range(ITERS):
        smoothed = ITERS + 1 + order
        totals = [weighted(getters[strip], read(order, strip)) for strip in range(4)]
        rising = weighted(lambda k: handed[NEAR + k], handed[BASIS + order], (0,))[0]
        falling = weighted(
            lambda k: handed[NEAR + 3 + k], handed[BASIS + KEPT + order], (0,)
        )[0]
        above = [zero, totals[0][2], falling, totals[2][2]]
        below = [totals[1][0], rising, totals[3][0], zero]
        for strip in range(4):
            write(
                smoothed,
                strip,
                getters[strip](9)
                * (
                    totals[strip][1]
                    + row_above(totals[strip][2], above[strip])
                    + row_below(totals[strip][0], below[strip])
                ),
            )
        blocks = [read(smoothed, strip) for strip in range(4)]
        before = [zero, blocks[0], handed[BASIS + KEPT + smoothed], blocks[2]]
        after = [blocks[1], handed[BASIS + smoothed], blocks[3], zero]
        for strip in range(4) if order < ITERS - 1 else (1, 2):
            write(
                order + 1,
                strip,
                applied(
                    getters[strip],
                    blocks[strip],
                    before[strip],
                    after[strip],
                    read(order, strip),
                ),
            )
    totals = tuple(sums[i] for i in range(PRODUCTS))
    for rows in inner:
        totals = gathered(totals, kept, rows, breadth)
    gram[...] = jnp.zeros(gram.shape, jnp.float32)
    for index in range(PRODUCTS):
        total = jnp.sum(jnp.sum(totals[index], axis=0, keepdims=True), axis=1, keepdims=True)
        gram[index : index + 1, :] = jnp.broadcast_to(total, (1, LANES))


def recurrences(gram):
    shift, scale = SHIFT, SCALE
    residual = [1.0]
    direction = []
    steps = [0.0] * ITERS
    rz_before = None
    for order in range(ITERS):
        rz = None
        for i in range(order + 1):
            inner = None
            for j in range(order + 1):
                term = residual[j] * gram[i][j]
                inner = term if inner is None else inner + term
            inner = residual[i] * inner
            rz = inner if rz is None else rz + inner
        if order == 0:
            direction = [1.0]
        else:
            ratio = rz / rz_before
            direction = [
                residual[i] + ratio * direction[i] if i < order else residual[i]
                for i in range(order + 1)
            ]
        image = [0.0] * (order + 2)
        for i in range(order + 1):
            image[i] = image[i] + shift * direction[i]
            image[i + 1] = image[i + 1] + scale * direction[i]
        curvature = None
        for i in range(order + 2):
            inner = None
            for j in range(order + 1):
                term = direction[j] * gram[i][j]
                inner = term if inner is None else inner + term
            inner = image[i] * inner
            curvature = inner if curvature is None else curvature + inner
        step = rz / curvature
        for i in range(order + 1):
            steps[i] = steps[i] + step * direction[i]
        residual = [
            (residual[i] if i < order + 1 else 0.0) - step * image[i]
            for i in range(order + 2)
        ]
        rz_before = rz
    return steps, residual


def combine_kernel(gram_ref, kept, edges, solution_ref, residual_ref):
    height, breadth = solution_ref.shape
    gram = [
        [gram_ref[i * ITERS + j : i * ITERS + j + 1, :] for j in range(ITERS)]
        for i in range(ITERS + 1)
    ]
    steps, residual = recurrences(gram)

    def wide(value):
        value = jnp.broadcast_to(value, (STRIP, LANES))
        return jnp.concatenate([value] * (breadth // LANES), axis=1)

    def put(source, rows_from, rows_to):
        total = None
        for j in range(ITERS):
            term = wide(steps[j]) * source[ITERS + 1 + j, rows_from, 0:breadth]
            total = term if total is None else total + term
        solution_ref[rows_to, :] = total
        total = None
        for i in range(ITERS + 1):
            term = wide(residual[i]) * source[i, rows_from, 0:breadth]
            total = term if total is None else total + term
        residual_ref[rows_to, :] = total

    put(edges, slice(0, STRIP), slice(0, STRIP))
    put(edges, slice(STRIP, 2 * STRIP), slice(height - STRIP, height))

    def middle(strip, carried):
        rows = strip_rows(strip)
        put(kept, rows, rows)
        return carried

    lax.fori_loop(1, height // STRIP - 1, middle, 0)


def params(limit=VMEM_BYTES):
    return pltpu.CompilerParams(vmem_limit_bytes=limit)


def cost(flops, moved):
    return pl.CostEstimate(flops=flops, bytes_accessed=moved, transcendentals=0)


def whole(*shapes):
    return [pl.BlockSpec(shape, lambda step, n=len(shape): (0,) * n) for shape in shapes]


def body(right_side, faces, ratio, centre, offdiag, mask):
    height, breadth = right_side.shape
    width = breadth + LANES
    args = (right_side, mask, centre, ratio, faces, offdiag)
    f32 = jnp.float32
    gy = lax.axis_size("gy")
    swap = [(0, 1), (1, 0)]
    pairs = [(i, i ^ 1) for i in range(gy) if i ^ 1 < gy]
    between = [(i, (i + 1 ^ 1) - 1) for i in range(1, gy) if (i + 1 ^ 1) - 1 < gy]

    def diagonal(partners):
        return [(2 * a + c, 2 * b + 1 - c) for a, b in partners for c in (0, 1)]

    packed = jax.ShapeDtypeStruct((PACKED, breadth), f32)
    corner = jax.ShapeDtypeStruct((STRIP, LANES), f32)
    columns = jax.ShapeDtypeStruct((height, LANES), f32)
    even, odd, even_corner, odd_corner, columns = pl.pallas_call(
        pack_kernel,
        in_specs=[pl.BlockSpec(memory_space=pltpu.HBM)] * len(args),
        out_shape=(packed, packed, corner, corner, columns),
        scratch_shapes=[
            pltpu.VMEM((2,) + a.shape[:-2] + (STRIP, breadth), a.dtype) for a in args
        ]
        + [pltpu.VMEM(a.shape[:-1] + (LANES,), a.dtype) for a in args]
        + [
            pltpu.SemaphoreType.DMA((len(args), 2)),
            pltpu.SemaphoreType.DMA((len(args),)),
        ],
        compiler_params=params(PACK_VMEM_BYTES),
        cost_estimate=cost(0, 4 * 4 * PACKED * breadth),
        name="pack",
    )(*args)
    columns = lax.ppermute(columns, "gx", swap)
    even_in = lax.ppermute(even, "gy", pairs)
    even_corner = lax.ppermute(even_corner, ("gy", "gx"), diagonal(pairs))
    odd_in = lax.ppermute(odd, "gy", between)
    odd_corner = lax.ppermute(odd_corner, ("gy", "gx"), diagonal(between))

    cells = height * width
    kept, sums, handed = pl.pallas_call(
        tile_kernel,
        in_specs=[pl.BlockSpec(memory_space=pltpu.HBM)] * len(args)
        + [pl.BlockSpec(memory_space=pltpu.VMEM)],
        out_shape=(
            jax.ShapeDtypeStruct((KEPT, height, width), f32),
            jax.ShapeDtypeStruct((PRODUCTS, STRIP, LANES), f32),
            jax.ShapeDtypeStruct((HANDED, STRIP, width), f32),
        ),
        scratch_shapes=[
            pltpu.VMEM((COEFFICIENTS, height, width), f32),
            pltpu.VMEM((FIELDS, height, LANES), f32),
        ]
        + [pltpu.VMEM(a.shape, a.dtype) for a in args]
        + [pltpu.SemaphoreType.DMA((len(args), 2))],
        compiler_params=params(TILE_VMEM_BYTES),
        cost_estimate=cost(100 * cells, 4 * cells * (FIELDS + KEPT)),
        name="tile",
    )(*args, columns)

    sums, even_in, odd_in, even_corner, odd_corner = lax.optimization_barrier(
        (sums, even_in, odd_in, even_corner, odd_corner)
    )
    rows = 2 * STRIP
    edges, gram = pl.pallas_call(
        edge_kernel,
        out_shape=(
            jax.ShapeDtypeStruct((KEPT, rows, width), f32),
            jax.ShapeDtypeStruct((2 * STRIP, LANES), f32),
        ),
        scratch_shapes=[
            pltpu.VMEM((FIELDS, rows, width), f32),
            pltpu.VMEM((COEFFICIENTS, rows, width), f32),
            pltpu.VMEM((KEPT, rows, width), f32),
        ],
        compiler_params=params(),
        cost_estimate=cost(200 * rows * width, 4 * rows * width * (FIELDS + KEPT)),
        name="edge",
    )(handed, even_in, odd_in, even_corner, odd_corner, sums)

    gram = gram + lax.ppermute(gram, "gx", swap)
    reach = 1
    while reach < gy:
        gram = gram + lax.ppermute(gram, "gy", [(i, i ^ reach) for i in range(gy)])
        reach *= 2

    tile = jax.ShapeDtypeStruct((height, breadth), f32)
    return pl.pallas_call(
        combine_kernel,
        grid=(1,),
        in_specs=whole(gram.shape, kept.shape, edges.shape),
        out_specs=whole(tile.shape, tile.shape),
        out_shape=(tile, tile),
        compiler_params=params(),
        cost_estimate=cost(14 * height * breadth, 4 * height * breadth * (KEPT + 2)),
        name="combine",
    )(gram, kept, edges)


def solution(mesh):
    return jax.shard_map(
        body,
        mesh=mesh,
        in_specs=(
            P(("members", "gy"), "gx"),
            P(None, "gy", "gx"),
            P("gy", "gx"),
            P("gy", "gx"),
            P(None, "gy", "gx"),
            P("gy", "gx"),
        ),
        out_specs=(P(("members", "gy"), "gx"), P(("members", "gy"), "gx")),
        check_vma=False,
    )
```

time: 43.1 us -> 41.3 us (0.958)
  Pallas kernels: 13.1 us -> 11 us
  starting transfers between devices: 14.9 us -> 16.3 us
  waiting for transfers between devices: 8.61 us -> 7.56 us
    ppermute x3 -> x4, starting transfers between devices: 5.8 us -> 8.73 us  [the longest x1 4.38 us: body(): even_corner = lax.ppermute(even_corner, ('gy', 'gx'), diagonal(pairs))]
    ppermute x3 -> x4, waiting for transfers between devices: 2.7 us -> 0.01 us  [the longest x1 0.01 us: body(): even_corner = lax.ppermute(even_corner, ('gy', 'gx'), diagonal(pairs))]
    pallas_call x4 -> x3, Pallas kernels: 11.8 us -> 9.72 us  [the longest x1 5.69 us: body(): pl.pallas_call(tile_kernel, in_specs=[pl.BlockSpec(memory_space=pltpu.HBM...]
    ppermute x3, waiting for transfers between devices: 4.88 us -> 6.44 us  [body(): gram = gram + lax.ppermute(gram, 'gy', [(i, i ^ reach) for i in range(gy)])]
    ppermute x3, starting transfers between devices: 8.5 us -> 7.45 us  [body(): gram = gram + lax.ppermute(gram, 'gy', [(i, i ^ reach) for i in range(gy)])]
    unnamed x14 -> x12, local copies, waits for them, and re-layouts: 5.32 us -> 5.31 us
  transfers between devices with their start and end apart: 8 -> 9, of which waited for: 6 -> 4; matrix products, arithmetic and copies ran while one was open for 0% -> 0% of each run, Pallas kernels for 12% -> 14%
where the time goes in v3:
time: 41.3 us; the launch traced here: 41 us
  starting transfers between devices  16.3 us (39%)
  Pallas kernels  11 us (27%)
  waiting for transfers between devices  7.56 us (18%)
  local copies, waits for them, and re-layouts  5.31 us (13%)
  between operations  0.76 us (2%)
    ppermute x3, starting transfers between devices, body(): gram = gram + lax.ppermute(gram, 'gy', [(i, i ^ reach) for i in range(gy)])  7.45 us
    ppermute x3, waiting for transfers between devices, body(): gram = gram + lax.ppermute(gram, 'gy', [(i, i ^ reach) for i in range(gy)])  6.44 us
    pallas_call x1, Pallas kernels, body(): pl.pallas_call(tile_kernel, in_specs=[pl.BlockSpec(memory_space=pltpu.HBM...  5.69 us
    unnamed x12, local copies, waits for them, and re-layouts  5.31 us
    ppermute x1, starting transfers between devices, body(): even_corner = lax.ppermute(even_corner, ('gy', 'gx'), diagonal(pairs))  4.38 us
    ppermute x1, starting transfers between devices, body(): even_in = lax.ppermute(even, 'gy', pairs)  3.03 us
    pallas_call x1, Pallas kernels, body(): pl.pallas_call(pack_kernel, in_specs=[pl.BlockSpec(memory_space=pltpu.HBM...  2.76 us
    pallas_call x1, Pallas kernels, body(): pl.pallas_call(combine_kernel, grid=(1,), in_specs=whole(gram.shape, kept...  1.32 us
  transfers between devices with their start and end apart: 9, of which 4 were waited for; matrix products, arithmetic and copies ran while one was open for 0% of the time, Pallas kernels for 14%

profile of v3, /device:TPU:0, one launch (start us, length us, event | category | flops | bytes accessed | tf_op | source)
XLA Modules:
  0.0 41.0 jit_solution(4412229703600500056)
XLA Ops:
  0.6 0.0 copy-start.1
  0.6 0.0 copy-start.2
  0.6 2.8 %pack.1 = (f32[72,1024]{1,0:T(8,128)}, f32[72,1024]{1,0:T(8,128)}, f32[8,128]{1,0:T(8,128)}, f32[8,128]{1,0:T(8,128)}, f32[128,128]{1,0:T(8,128)}) custom-call(f32[128,1024]{1,0:T(8,128)} %refs_0_.3, s32[128,1024]{1,0:T(8,128)} %refs_1_.3, f32[128,1024]{1,0:T(8,128)} %refs_2_.3, f32[128,1024]{1,0:T(8,128)} %refs_3_.3, f32[2,128,1024]{2,1,0:T(8,128)} %refs_4_.3, ...), custom_call_target="tpu_custom_call" | custom-call | bytes 1179648 | tf_op jit(solution)/shard_map/pack/pallas_call | solution.py:560
  3.4 3.0 %collective-permute-start.1 = (f32[72,1024]{1,0:T(8,128)}, f32[72,1024]{1,0:T(8,128)S(1)}, u32[]{:S(2)}, u32[]{:S(2)}) collective-permute-start(f32[72,1024]{1,0:T(8,128)} %get-tuple-element.20), channel_id=1, source_target_pairs={{0,2},{2,0},{4,6},{6,4},{8,10},{10,8},{12,14},{14,12},{1,3},{3,1},... | collective-permute-start | bytes 884744 | tf_op jit(solution)/shard_map/ppermute | solution.py:577
  6.5 0.7 %collective-permute-start.2 = (f32[72,1024]{1,0:T(8,128)}, f32[72,1024]{1,0:T(8,128)S(1)}, u32[]{:S(2)}, u32[]{:S(2)}) collective-permute-start(f32[72,1024]{1,0:T(8,128)} %get-tuple-element.21), channel_id=1, source_target_pairs={{2,4},{4,2},{6,8},{8,6},{10,12},{12,10},{3,5},{5,3},{7,9},{9,7},{1... | collective-permute-start | bytes 884744 | tf_op jit(solution)/shard_map/ppermute | solution.py:579
  7.1 0.1 collective-permute-start
  7.2 4.4 %collective-permute-start.3 = (f32[8,128]{1,0:T(8,128)}, f32[8,128]{1,0:T(8,128)S(1)}, u32[]{:S(2)}, u32[]{:S(2)}) collective-permute-start(f32[8,128]{1,0:T(8,128)} %get-tuple-element.22), channel_id=1, source_target_pairs={{0,3},{1,2},{2,1},{3,0},{4,7},{5,6},{6,5},{7,4},{8,11},{9,10},{10,... | collective-permute-start | bytes 12296 | tf_op jit(solution)/shard_map/ppermute | solution.py:578
  11.6 0.6 %collective-permute-start.4 = (f32[8,128]{1,0:T(8,128)}, f32[8,128]{1,0:T(8,128)S(1)}, u32[]{:S(2)}, u32[]{:S(2)}) collective-permute-start(f32[8,128]{1,0:T(8,128)} %get-tuple-element.23), channel_id=1, source_target_pairs={{2,5},{3,4},{4,3},{5,2},{6,9},{7,8},{8,7},{9,6},{10,13},{11,12},{1... | collective-permute-start | bytes 12296 | tf_op jit(solution)/shard_map/ppermute | solution.py:580
  12.2 0.0 collective-permute-done.refs_6_
  12.3 0.0 copy-done.1
  12.3 0.0 copy-done.2
  12.3 0.0 copy-start
  12.3 2.2 %copy-done = f32[8,128,1024]{2,1,0:T(8,128)S(1)} copy-done((f32[8,128,1024]{2,1,0:T(8,128)S(1)}, f32[8,128,1024]{2,1,0:T(8,128)}, u32[]{:S(2)}) %copy-start) | copy-done | bytes 4194328
  14.5 0.0 copy-start.3
  14.5 1.0 %copy-done.3 = s32[128,1024]{1,0:T(8,128)S(1)} copy-done((s32[128,1024]{1,0:T(8,128)S(1)}, s32[128,1024]{1,0:T(8,128)}, u32[]{:S(2)}) %copy-start.3) | copy-done | bytes 524312
  15.5 1.0 %copy-done.4 = f32[128,1024]{1,0:T(8,128)S(1)} copy-done((f32[128,1024]{1,0:T(8,128)S(1)}, f32[128,1024]{1,0:T(8,128)}, u32[]{:S(2)}) %copy-start.4) | copy-done | bytes 524312
  16.6 1.0 %copy-done.5 = f32[128,1024]{1,0:T(8,128)S(1)} copy-done((f32[128,1024]{1,0:T(8,128)S(1)}, f32[128,1024]{1,0:T(8,128)}, u32[]{:S(2)}) %copy-start.5) | copy-done | bytes 524312
  17.6 5.7 %tile.1 = (f32[7,128,1152]{2,1,0:T(8,128)S(1)}, f32[12,8,128]{2,1,0:T(8,128)S(1)}, f32[53,8,1152]{2,1,0:T(8,128)S(1)}) custom-call(f32[128,1024]{1,0:T(8,128)S(1)} %copy-done.2, s32[128,1024]{1,0:T(8,128)S(1)} %copy-done.3, f32[128,1024]{1,0:T(8,128)S(1)} %copy-done.4, f32[128,1024]{1,0:T(8,128)S(1)} %copy-done.5, f32[2,128,1024]{2,1,0:T(8,128)S(1)} %copy-done.1, ...), custom_call_target="tpu_custom_call" | custom-call | flops 14745600 | bytes 12386304 | tf_op jit(solution)/shard_map/tile/pallas_call | solution.py:583
  23.3 0.0 collective-permute-done.3.even_corner
  23.3 0.0 collective-permute-done.4.odd_corner
  23.3 0.0 collective-permute-done.1.even
  23.3 0.0 collective-permute-done.2.odd
  23.3 1.3 %edge.1 = (f32[7,16,1152]{2,1,0:T(8,128)S(1)}, f32[16,128]{1,0:T(8,128)S(1)}) custom-call(f32[53,8,1152]{2,1,0:T(8,128)S(1)} %get-tuple-element.18.handed, f32[72,1024]{1,0:T(8,128)S(1)} %collective-permute-done.1.even, f32[72,1024]{1,0:T(8,128)S(1)} %collective-permute-done.2.odd, f32[8,128]{1,0:T(8,128)S(1)} %collective-permute-done.3.even_corner, ...), custom_call_target="tpu_custom_call" | custom-call | flops 3686400 | bytes 1548288 | tf_op jit(solution)/shard_map/edge/pallas_call | solution.py:607
  24.6 0.1 collective-permute-start.5
  24.7 1.1 %collective-permute-done.5 = f32[16,128]{1,0:T(8,128)S(1)} collective-permute-done((f32[16,128]{1,0:T(8,128)S(1)}, f32[16,128]{1,0:T(8,128)S(1)}, u32[]{:S(2)}, u32[]{:S(2)}) %collective-permute-start.5) | collective-permute-done | bytes 8224 | tf_op jit(solution)/shard_map/ppermute | solution.py:623
  25.8 4.1 %collective-permute-start.6 = (f32[16,128]{1,0:T(8,128)S(1)}, f32[16,128]{1,0:T(8,128)S(1)}, u32[]{:S(2)}, u32[]{:S(2)}) collective-permute-start(f32[16,128]{1,0:T(8,128)S(1)} %add.12), channel_id=1, source_target_pairs={{0,2},{2,0},{4,6},{6,4},{8,10},{10,8},{12,14},{14,12},{1,3},{3,1},... | collective-permute-start | bytes 24584 | tf_op jit(solution)/shard_map/ppermute | solution.py:626
  29.9 1.6 %collective-permute-done.6 = f32[16,128]{1,0:T(8,128)S(1)} collective-permute-done((f32[16,128]{1,0:T(8,128)S(1)}, f32[16,128]{1,0:T(8,128)S(1)}, u32[]{:S(2)}, u32[]{:S(2)}) %collective-permute-start.6) | collective-permute-done | bytes 8224 | tf_op jit(solution)/shard_map/ppermute | solution.py:626
  31.5 1.6 %collective-permute-start.7 = (f32[16,128]{1,0:T(8,128)S(1)}, f32[16,128]{1,0:T(8,128)S(1)}, u32[]{:S(2)}, u32[]{:S(2)}) collective-permute-start(f32[16,128]{1,0:T(8,128)S(1)} %add.13), channel_id=1, source_target_pairs={{0,4},{2,6},{4,0},{6,2},{8,12},{10,14},{12,8},{14,10},{1,5},{3,7},... | collective-permute-start | bytes 24584 | tf_op jit(solution)/shard_map/ppermute | solution.py:626
  33.1 2.1 %collective-permute-done.7 = f32[16,128]{1,0:T(8,128)S(1)} collective-permute-done((f32[16,128]{1,0:T(8,128)S(1)}, f32[16,128]{1,0:T(8,128)S(1)}, u32[]{:S(2)}, u32[]{:S(2)}) %collective-permute-start.7) | collective-permute-done | bytes 8224 | tf_op jit(solution)/shard_map/ppermute | solution.py:626
  35.1 1.8 %collective-permute-start.8 = (f32[16,128]{1,0:T(8,128)S(1)}, f32[16,128]{1,0:T(8,128)S(1)}, u32[]{:S(2)}, u32[]{:S(2)}) collective-permute-start(f32[16,128]{1,0:T(8,128)S(1)} %add.14), channel_id=1, source_target_pairs={{0,8},{2,10},{4,12},{6,14},{8,0},{10,2},{12,4},{14,6},{1,9},{3,11}... | collective-permute-start | bytes 24584 | tf_op jit(solution)/shard_map/ppermute | solution.py:626
  37.0 2.7 %collective-permute-done.8 = f32[16,128]{1,0:T(8,128)S(1)} collective-permute-done((f32[16,128]{1,0:T(8,128)S(1)}, f32[16,128]{1,0:T(8,128)S(1)}, u32[]{:S(2)}, u32[]{:S(2)}) %collective-permute-start.8) | collective-permute-done | bytes 8224 | tf_op jit(solution)/shard_map/ppermute | solution.py:626
  39.7 1.3 %combine.1 = (f32[128,1024]{1,0:T(8,128)}, f32[128,1024]{1,0:T(8,128)}) custom-call(f32[16,128]{1,0:T(8,128)S(1)} %add.15.gram_ref, f32[7,128,1152]{2,1,0:T(8,128)S(1)} %get-tuple-element.30.kept, f32[7,16,1152]{2,1,0:T(8,128)S(1)} %get-tuple-element.31.edges), custom_call_target="tpu_custom_call" | custom-call | flops 1835008 | bytes 4718592 | tf_op jit(solution)/shard_map/combine/pallas_call | solution.py:630
  (6 shorter events, 0.0 us)
Async XLA Ops:
  0.6 11.6 %copy-start.1 = (f32[2,128,1024]{2,1,0:T(8,128)S(1)}, f32[2,128,1024]{2,1,0:T(8,128)}, u32[]{:S(2)}) copy-start(f32[2,128,1024]{2,1,0:T(8,128)} %refs_4_.3) | copy-start | bytes 3145732
  0.6 11.6 %copy-start.2 = (f32[128,1024]{1,0:T(8,128)S(1)}, f32[128,1024]{1,0:T(8,128)}, u32[]{:S(2)}) copy-start(f32[128,1024]{1,0:T(8,128)} %refs_0_.3) | copy-start | bytes 1572868
  3.4 19.9 %collective-permute-start.1 = (f32[72,1024]{1,0:T(8,128)}, f32[72,1024]{1,0:T(8,128)S(1)}, u32[]{:S(2)}, u32[]{:S(2)}) collective-permute-start(f32[72,1024]{1,0:T(8,128)} %get-tuple-element.20), channel_id=1, source_target_pairs={{0,2},{2,0},{4,6},{6,4},{8,10},{10,8},{12,14},{14,12},{1,3},{3,1},... | collective-permute-start | bytes 884744 | tf_op jit(solution)/shard_map/ppermute | solution.py:577
  6.5 16.9 %collective-permute-start.2 = (f32[72,1024]{1,0:T(8,128)}, f32[72,1024]{1,0:T(8,128)S(1)}, u32[]{:S(2)}, u32[]{:S(2)}) collective-permute-start(f32[72,1024]{1,0:T(8,128)} %get-tuple-element.21), channel_id=1, source_target_pairs={{2,4},{4,2},{6,8},{8,6},{10,12},{12,10},{3,5},{5,3},{7,9},{9,7},{1... | collective-permute-start | bytes 884744 | tf_op jit(solution)/shard_map/ppermute | solution.py:579
  7.1 5.1 %collective-permute-start = (f32[128,128]{1,0:T(8,128)}, f32[128,128]{1,0:T(8,128)S(1)}, u32[]{:S(2)}, u32[]{:S(2)}) collective-permute-start(f32[128,128]{1,0:T(8,128)} %get-tuple-element.17), channel_id=1, source_target_pairs={{0,1},{1,0},{2,3},{3,2},{4,5},{5,4},{6,7},{7,6},{8,9},{9,8},{10,11... | collective-permute-start | bytes 196616 | tf_op jit(solution)/shard_map/ppermute | solution.py:576
  7.2 16.1 %collective-permute-start.3 = (f32[8,128]{1,0:T(8,128)}, f32[8,128]{1,0:T(8,128)S(1)}, u32[]{:S(2)}, u32[]{:S(2)}) collective-permute-start(f32[8,128]{1,0:T(8,128)} %get-tuple-element.22), channel_id=1, source_target_pairs={{0,3},{1,2},{2,1},{3,0},{4,7},{5,6},{6,5},{7,4},{8,11},{9,10},{10,... | collective-permute-start | bytes 12296 | tf_op jit(solution)/shard_map/ppermute | solution.py:578
  11.6 11.7 %collective-permute-start.4 = (f32[8,128]{1,0:T(8,128)}, f32[8,128]{1,0:T(8,128)S(1)}, u32[]{:S(2)}, u32[]{:S(2)}) collective-permute-start(f32[8,128]{1,0:T(8,128)} %get-tuple-element.23), channel_id=1, source_target_pairs={{2,5},{3,4},{4,3},{5,2},{6,9},{7,8},{8,7},{9,6},{10,13},{11,12},{1... | collective-permute-start | bytes 12296 | tf_op jit(solution)/shard_map/ppermute | solution.py:580
  12.3 2.2 %copy-start = (f32[8,128,1024]{2,1,0:T(8,128)S(1)}, f32[8,128,1024]{2,1,0:T(8,128)}, u32[]{:S(2)}) copy-start(f32[8,128,1024]{2,1,0:T(8,128)} %refs_5_.3) | copy-start | bytes 12582916
  14.5 1.0 %copy-start.3 = (s32[128,1024]{1,0:T(8,128)S(1)}, s32[128,1024]{1,0:T(8,128)}, u32[]{:S(2)}) copy-start(s32[128,1024]{1,0:T(8,128)} %refs_1_.3) | copy-start | bytes 1572868
  15.5 1.0 %copy-start.4 = (f32[128,1024]{1,0:T(8,128)S(1)}, f32[128,1024]{1,0:T(8,128)}, u32[]{:S(2)}) copy-start(f32[128,1024]{1,0:T(8,128)} %refs_2_.3) | copy-start | bytes 1572868
  16.6 1.0 %copy-start.5 = (f32[128,1024]{1,0:T(8,128)S(1)}, f32[128,1024]{1,0:T(8,128)}, u32[]{:S(2)}) copy-start(f32[128,1024]{1,0:T(8,128)} %refs_3_.3) | copy-start | bytes 1572868
  24.6 1.2 %collective-permute-start.5 = (f32[16,128]{1,0:T(8,128)S(1)}, f32[16,128]{1,0:T(8,128)S(1)}, u32[]{:S(2)}, u32[]{:S(2)}) collective-permute-start(f32[16,128]{1,0:T(8,128)S(1)} %get-tuple-element.29), channel_id=1, source_target_pairs={{0,1},{1,0},{2,3},{3,2},{4,5},{5,4},{6,7},{7,6},{8,9},{9,8},{10,11... | collective-permute-start | bytes 24584 | tf_op jit(solution)/shard_map/ppermute | solution.py:623
  25.8 5.7 %collective-permute-start.6 = (f32[16,128]{1,0:T(8,128)S(1)}, f32[16,128]{1,0:T(8,128)S(1)}, u32[]{:S(2)}, u32[]{:S(2)}) collective-permute-start(f32[16,128]{1,0:T(8,128)S(1)} %add.12), channel_id=1, source_target_pairs={{0,2},{2,0},{4,6},{6,4},{8,10},{10,8},{12,14},{14,12},{1,3},{3,1},... | collective-permute-start | bytes 24584 | tf_op jit(solution)/shard_map/ppermute | solution.py:626
  31.5 3.7 %collective-permute-start.7 = (f32[16,128]{1,0:T(8,128)S(1)}, f32[16,128]{1,0:T(8,128)S(1)}, u32[]{:S(2)}, u32[]{:S(2)}) collective-permute-start(f32[16,128]{1,0:T(8,128)S(1)} %add.13), channel_id=1, source_target_pairs={{0,4},{2,6},{4,0},{6,2},{8,12},{10,14},{12,8},{14,10},{1,5},{3,7},... | collective-permute-start | bytes 24584 | tf_op jit(solution)/shard_map/ppermute | solution.py:626
  35.1 4.5 %collective-permute-start.8 = (f32[16,128]{1,0:T(8,128)S(1)}, f32[16,128]{1,0:T(8,128)S(1)}, u32[]{:S(2)}, u32[]{:S(2)}) collective-permute-start(f32[16,128]{1,0:T(8,128)S(1)} %add.14), channel_id=1, source_target_pairs={{0,8},{2,10},{4,12},{6,14},{8,0},{10,2},{12,4},{14,6},{1,9},{3,11}... | collective-permute-start | bytes 24584 | tf_op jit(solution)/shard_map/ppermute | solution.py:626

commit v4 on v3

--- a/solution.py
+++ b/solution.py
@@ -35,7 +35,7 @@
 HANDED = BASIS + 2 * KEPT
 TILE_VMEM_BYTES = 40 * 1024 * 1024
 VMEM_BYTES = 32 * 1024 * 1024
-PACK_VMEM_BYTES = 62 * 1024 * 1024
+PACK_VMEM_BYTES = 16 * 1024 * 1024
 
 
 def field(refs, which, rows):
@@ -544,7 +544,10 @@
 def body(right_side, faces, ratio, centre, offdiag, mask):
     height, breadth = right_side.shape
     width = breadth + LANES
-    args = (right_side, mask, centre, ratio, faces, offdiag)
+    args = [
+        pltpu.with_memory_space_constraint(a, pltpu.HBM)
+        for a in (right_side, mask, centre, ratio, faces, offdiag)
+    ]
     f32 = jnp.float32
     gy = lax.axis_size("gy")
     swap = [(0, 1), (1, 0)]

time: 41.3 us -> 37 us (0.90)
  local copies, waits for them, and re-layouts: 5.31 us -> 0 us
  Pallas kernels: 11 us -> 12.2 us
    unnamed x12 -> x0, local copies, waits for them, and re-layouts: 5.31 us -> none
    pallas_call x1, Pallas kernels: 5.69 us -> 7.58 us  [body(): pl.pallas_call(tile_kernel, in_specs=[pl.BlockSpec(memory_space=pltpu.HBM...]
    pallas_call x1, Pallas kernels: 2.76 us -> 2.04 us  [body(): pl.pallas_call(pack_kernel, in_specs=[pl.BlockSpec(memory_space=pltpu.HBM...]
  transfers between devices with their start and end apart: 9 -> 9, of which waited for: 4 -> 4; matrix products, arithmetic and copies ran while one was open for 0% -> 0% of each run, Pallas kernels for 14% -> 21%
where the time goes in v4:
time: 37 us; the launch traced here: 36.9 us
  starting transfers between devices  16.3 us (44%)
  Pallas kernels  12.2 us (33%)
  waiting for transfers between devices  7.56 us (20%)
  between operations  0.72 us (2%)
    pallas_call x1, Pallas kernels, body(): pl.pallas_call(tile_kernel, in_specs=[pl.BlockSpec(memory_space=pltpu.HBM...  7.58 us
    ppermute x3, starting transfers between devices, body(): gram = gram + lax.ppermute(gram, 'gy', [(i, i ^ reach) for i in range(gy)])  7.45 us
    ppermute x3, waiting for transfers between devices, body(): gram = gram + lax.ppermute(gram, 'gy', [(i, i ^ reach) for i in range(gy)])  6.44 us
    ppermute x1, starting transfers between devices, body(): even_corner = lax.ppermute(even_corner, ('gy', 'gx'), diagonal(pairs))  4.38 us
    ppermute x1, starting transfers between devices, body(): even_in = lax.ppermute(even, 'gy', pairs)  3.03 us
    pallas_call x1, Pallas kernels, body(): pl.pallas_call(pack_kernel, in_specs=[pl.BlockSpec(memory_space=pltpu.HBM...  2.04 us
    pallas_call x1, Pallas kernels, body(): pl.pallas_call(combine_kernel, grid=(1,), in_specs=whole(gram.shape, kept...  1.32 us
    pallas_call x1, Pallas kernels, body(): pl.pallas_call(edge_kernel, out_shape=(jax.ShapeDtypeStruct((KEPT, rows,...  1.3 us
  transfers between devices with their start and end apart: 9, of which 4 were waited for; matrix products, arithmetic and copies ran while one was open for 0% of the time, Pallas kernels for 21%

profile of v4, /device:TPU:0, one launch (start us, length us, event | category | flops | bytes accessed | tf_op | source)
XLA Modules:
  0.0 36.9 jit_solution(16207048330563237792)
XLA Ops:
  0.6 2.0 %pack.1 = (f32[72,1024]{1,0:T(8,128)S(1)}, f32[72,1024]{1,0:T(8,128)S(1)}, f32[8,128]{1,0:T(8,128)S(1)}, f32[8,128]{1,0:T(8,128)S(1)}, f32[128,128]{1,0:T(8,128)S(1)}) custom-call(f32[128,1024]{1,0:T(8,128)} %refs_0_.3, s32[128,1024]{1,0:T(8,128)} %refs_1_.3, f32[128,1024]{1,0:T(8,128)} %refs_2_.3, f32[128,1024]{1,0:T(8,128)} %refs_3_.3, ...), custom_call_target="tpu_custom_call" | custom-call | bytes 1179648 | tf_op jit(solution)/shard_map/pack/pallas_call | solution.py:563
  2.7 3.0 %collective-permute-start.1 = (f32[72,1024]{1,0:T(8,128)S(1)}, f32[72,1024]{1,0:T(8,128)S(1)}, u32[]{:S(2)}, u32[]{:S(2)}) collective-permute-start(f32[72,1024]{1,0:T(8,128)S(1)} %get-tuple-element.20), channel_id=1, source_target_pairs={{0,2},{2,0},{4,6},{6,4},{8,10},{10,8},{12,14},{14,12},{1,3},{3,1},... | collective-permute-start | bytes 884744 | tf_op jit(solution)/shard_map/ppermute | solution.py:580
  5.7 0.7 %collective-permute-start.2 = (f32[72,1024]{1,0:T(8,128)S(1)}, f32[72,1024]{1,0:T(8,128)S(1)}, u32[]{:S(2)}, u32[]{:S(2)}) collective-permute-start(f32[72,1024]{1,0:T(8,128)S(1)} %get-tuple-element.21), channel_id=1, source_target_pairs={{2,4},{4,2},{6,8},{8,6},{10,12},{12,10},{3,5},{5,3},{7,9},{9,7},{1... | collective-permute-start | bytes 884744 | tf_op jit(solution)/shard_map/ppermute | solution.py:582
  6.4 0.1 collective-permute-start
  6.5 4.4 %collective-permute-start.3 = (f32[8,128]{1,0:T(8,128)S(1)}, f32[8,128]{1,0:T(8,128)S(1)}, u32[]{:S(2)}, u32[]{:S(2)}) collective-permute-start(f32[8,128]{1,0:T(8,128)S(1)} %get-tuple-element.22), channel_id=1, source_target_pairs={{0,3},{1,2},{2,1},{3,0},{4,7},{5,6},{6,5},{7,4},{8,11},{9,10},{10,... | collective-permute-start | bytes 12296 | tf_op jit(solution)/shard_map/ppermute | solution.py:581
  10.8 0.6 %collective-permute-start.4 = (f32[8,128]{1,0:T(8,128)S(1)}, f32[8,128]{1,0:T(8,128)S(1)}, u32[]{:S(2)}, u32[]{:S(2)}) collective-permute-start(f32[8,128]{1,0:T(8,128)S(1)} %get-tuple-element.23), channel_id=1, source_target_pairs={{2,5},{3,4},{4,3},{5,2},{6,9},{7,8},{8,7},{9,6},{10,13},{11,12},{1... | collective-permute-start | bytes 12296 | tf_op jit(solution)/shard_map/ppermute | solution.py:583
  11.5 0.0 collective-permute-done.refs_6_
  11.5 7.6 %tile.1 = (f32[7,128,1152]{2,1,0:T(8,128)S(1)}, f32[12,8,128]{2,1,0:T(8,128)S(1)}, f32[53,8,1152]{2,1,0:T(8,128)S(1)}) custom-call(f32[128,1024]{1,0:T(8,128)} %refs_0_.3, s32[128,1024]{1,0:T(8,128)} %refs_1_.3, f32[128,1024]{1,0:T(8,128)} %refs_2_.3, f32[128,1024]{1,0:T(8,128)} %refs_3_.3, f32[2,128,1024]{2,1,0:T(8,128)} %refs_4_.3, ...), custom_call_target="tpu_custom_call" | custom-call | flops 14745600 | bytes 12386304 | tf_op jit(solution)/shard_map/tile/pallas_call | solution.py:586
  19.1 0.0 collective-permute-done.3.even_corner
  19.1 0.0 collective-permute-done.4.odd_corner
  19.1 0.0 collective-permute-done.1.even
  19.1 0.0 collective-permute-done.2.odd
  19.1 1.3 %edge.1 = (f32[7,16,1152]{2,1,0:T(8,128)S(1)}, f32[16,128]{1,0:T(8,128)S(1)}) custom-call(f32[53,8,1152]{2,1,0:T(8,128)S(1)} %get-tuple-element.18.handed, f32[72,1024]{1,0:T(8,128)S(1)} %collective-permute-done.1.even, f32[72,1024]{1,0:T(8,128)S(1)} %collective-permute-done.2.odd, f32[8,128]{1,0:T(8,128)S(1)} %collective-permute-done.3.even_corner, ...), custom_call_target="tpu_custom_call" | custom-call | flops 3686400 | bytes 1548288 | tf_op jit(solution)/shard_map/edge/pallas_call | solution.py:610
  20.4 0.1 collective-permute-start.5
  20.5 1.1 %collective-permute-done.5 = f32[16,128]{1,0:T(8,128)S(1)} collective-permute-done((f32[16,128]{1,0:T(8,128)S(1)}, f32[16,128]{1,0:T(8,128)S(1)}, u32[]{:S(2)}, u32[]{:S(2)}) %collective-permute-start.5) | collective-permute-done | bytes 8224 | tf_op jit(solution)/shard_map/ppermute | solution.py:626
  21.6 4.1 %collective-permute-start.6 = (f32[16,128]{1,0:T(8,128)S(1)}, f32[16,128]{1,0:T(8,128)S(1)}, u32[]{:S(2)}, u32[]{:S(2)}) collective-permute-start(f32[16,128]{1,0:T(8,128)S(1)} %add.12), channel_id=1, source_target_pairs={{0,2},{2,0},{4,6},{6,4},{8,10},{10,8},{12,14},{14,12},{1,3},{3,1},... | collective-permute-start | bytes 24584 | tf_op jit(solution)/shard_map/ppermute | solution.py:629
  25.7 1.6 %collective-permute-done.6 = f32[16,128]{1,0:T(8,128)S(1)} collective-permute-done((f32[16,128]{1,0:T(8,128)S(1)}, f32[16,128]{1,0:T(8,128)S(1)}, u32[]{:S(2)}, u32[]{:S(2)}) %collective-permute-start.6) | collective-permute-done | bytes 8224 | tf_op jit(solution)/shard_map/ppermute | solution.py:629
  27.3 1.6 %collective-permute-start.7 = (f32[16,128]{1,0:T(8,128)S(1)}, f32[16,128]{1,0:T(8,128)S(1)}, u32[]{:S(2)}, u32[]{:S(2)}) collective-permute-start(f32[16,128]{1,0:T(8,128)S(1)} %add.13), channel_id=1, source_target_pairs={{0,4},{2,6},{4,0},{6,2},{8,12},{10,14},{12,8},{14,10},{1,5},{3,7},... | collective-permute-start | bytes 24584 | tf_op jit(solution)/shard_map/ppermute | solution.py:629
  28.9 2.1 %collective-permute-done.7 = f32[16,128]{1,0:T(8,128)S(1)} collective-permute-done((f32[16,128]{1,0:T(8,128)S(1)}, f32[16,128]{1,0:T(8,128)S(1)}, u32[]{:S(2)}, u32[]{:S(2)}) %collective-permute-start.7) | collective-permute-done | bytes 8224 | tf_op jit(solution)/shard_map/ppermute | solution.py:629
  31.0 1.8 %collective-permute-start.8 = (f32[16,128]{1,0:T(8,128)S(1)}, f32[16,128]{1,0:T(8,128)S(1)}, u32[]{:S(2)}, u32[]{:S(2)}) collective-permute-start(f32[16,128]{1,0:T(8,128)S(1)} %add.14), channel_id=1, source_target_pairs={{0,8},{2,10},{4,12},{6,14},{8,0},{10,2},{12,4},{14,6},{1,9},{3,11}... | collective-permute-start | bytes 24584 | tf_op jit(solution)/shard_map/ppermute | solution.py:629
  32.8 2.7 %collective-permute-done.8 = f32[16,128]{1,0:T(8,128)S(1)} collective-permute-done((f32[16,128]{1,0:T(8,128)S(1)}, f32[16,128]{1,0:T(8,128)S(1)}, u32[]{:S(2)}, u32[]{:S(2)}) %collective-permute-start.8) | collective-permute-done | bytes 8224 | tf_op jit(solution)/shard_map/ppermute | solution.py:629
  35.5 1.3 %combine.1 = (f32[128,1024]{1,0:T(8,128)}, f32[128,1024]{1,0:T(8,128)}) custom-call(f32[16,128]{1,0:T(8,128)S(1)} %add.15.gram_ref, f32[7,128,1152]{2,1,0:T(8,128)S(1)} %get-tuple-element.30.kept, f32[7,16,1152]{2,1,0:T(8,128)S(1)} %get-tuple-element.31.edges), custom_call_target="tpu_custom_call" | custom-call | flops 1835008 | bytes 4718592 | tf_op jit(solution)/shard_map/combine/pallas_call | solution.py:633
  (4 shorter events, 0.0 us)
Async XLA Ops:
  2.7 16.5 %collective-permute-start.1 = (f32[72,1024]{1,0:T(8,128)S(1)}, f32[72,1024]{1,0:T(8,128)S(1)}, u32[]{:S(2)}, u32[]{:S(2)}) collective-permute-start(f32[72,1024]{1,0:T(8,128)S(1)} %get-tuple-element.20), channel_id=1, source_target_pairs={{0,2},{2,0},{4,6},{6,4},{8,10},{10,8},{12,14},{14,12},{1,3},{3,1},... | collective-permute-start | bytes 884744 | tf_op jit(solution)/shard_map/ppermute | solution.py:580
  5.7 13.4 %collective-permute-start.2 = (f32[72,1024]{1,0:T(8,128)S(1)}, f32[72,1024]{1,0:T(8,128)S(1)}, u32[]{:S(2)}, u32[]{:S(2)}) collective-permute-start(f32[72,1024]{1,0:T(8,128)S(1)} %get-tuple-element.21), channel_id=1, source_target_pairs={{2,4},{4,2},{6,8},{8,6},{10,12},{12,10},{3,5},{5,3},{7,9},{9,7},{1... | collective-permute-start | bytes 884744 | tf_op jit(solution)/shard_map/ppermute | solution.py:582
  6.4 5.1 %collective-permute-start = (f32[128,128]{1,0:T(8,128)S(1)}, f32[128,128]{1,0:T(8,128)S(1)}, u32[]{:S(2)}, u32[]{:S(2)}) collective-permute-start(f32[128,128]{1,0:T(8,128)S(1)} %get-tuple-element.17), channel_id=1, source_target_pairs={{0,1},{1,0},{2,3},{3,2},{4,5},{5,4},{6,7},{7,6},{8,9},{9,8},{10,11... | collective-permute-start | bytes 196616 | tf_op jit(solution)/shard_map/ppermute | solution.py:579
  6.5 12.6 %collective-permute-start.3 = (f32[8,128]{1,0:T(8,128)S(1)}, f32[8,128]{1,0:T(8,128)S(1)}, u32[]{:S(2)}, u32[]{:S(2)}) collective-permute-start(f32[8,128]{1,0:T(8,128)S(1)} %get-tuple-element.22), channel_id=1, source_target_pairs={{0,3},{1,2},{2,1},{3,0},{4,7},{5,6},{6,5},{7,4},{8,11},{9,10},{10,... | collective-permute-start | bytes 12296 | tf_op jit(solution)/shard_map/ppermute | solution.py:581
  10.8 8.3 %collective-permute-start.4 = (f32[8,128]{1,0:T(8,128)S(1)}, f32[8,128]{1,0:T(8,128)S(1)}, u32[]{:S(2)}, u32[]{:S(2)}) collective-permute-start(f32[8,128]{1,0:T(8,128)S(1)} %get-tuple-element.23), channel_id=1, source_target_pairs={{2,5},{3,4},{4,3},{5,2},{6,9},{7,8},{8,7},{9,6},{10,13},{11,12},{1... | collective-permute-start | bytes 12296 | tf_op jit(solution)/shard_map/ppermute | solution.py:583
  20.4 1.2 %collective-permute-start.5 = (f32[16,128]{1,0:T(8,128)S(1)}, f32[16,128]{1,0:T(8,128)S(1)}, u32[]{:S(2)}, u32[]{:S(2)}) collective-permute-start(f32[16,128]{1,0:T(8,128)S(1)} %get-tuple-element.29), channel_id=1, source_target_pairs={{0,1},{1,0},{2,3},{3,2},{4,5},{5,4},{6,7},{7,6},{8,9},{9,8},{10,11... | collective-permute-start | bytes 24584 | tf_op jit(solution)/shard_map/ppermute | solution.py:626
  21.6 5.7 %collective-permute-start.6 = (f32[16,128]{1,0:T(8,128)S(1)}, f32[16,128]{1,0:T(8,128)S(1)}, u32[]{:S(2)}, u32[]{:S(2)}) collective-permute-start(f32[16,128]{1,0:T(8,128)S(1)} %add.12), channel_id=1, source_target_pairs={{0,2},{2,0},{4,6},{6,4},{8,10},{10,8},{12,14},{14,12},{1,3},{3,1},... | collective-permute-start | bytes 24584 | tf_op jit(solution)/shard_map/ppermute | solution.py:629
  27.3 3.7 %collective-permute-start.7 = (f32[16,128]{1,0:T(8,128)S(1)}, f32[16,128]{1,0:T(8,128)S(1)}, u32[]{:S(2)}, u32[]{:S(2)}) collective-permute-start(f32[16,128]{1,0:T(8,128)S(1)} %add.13), channel_id=1, source_target_pairs={{0,4},{2,6},{4,0},{6,2},{8,12},{10,14},{12,8},{14,10},{1,5},{3,7},... | collective-permute-start | bytes 24584 | tf_op jit(solution)/shard_map/ppermute | solution.py:629
  31.0 4.5 %collective-permute-start.8 = (f32[16,128]{1,0:T(8,128)S(1)}, f32[16,128]{1,0:T(8,128)S(1)}, u32[]{:S(2)}, u32[]{:S(2)}) collective-permute-start(f32[16,128]{1,0:T(8,128)S(1)} %add.14), channel_id=1, source_target_pairs={{0,8},{2,10},{4,12},{6,14},{8,0},{10,2},{12,4},{14,6},{1,9},{3,11}... | collective-permute-start | bytes 24584 | tf_op jit(solution)/shard_map/ppermute | solution.py:629

commit v5 on v3

--- a/solution.py
+++ b/solution.py
@@ -35,7 +35,7 @@
 HANDED = BASIS + 2 * KEPT
 TILE_VMEM_BYTES = 40 * 1024 * 1024
 VMEM_BYTES = 32 * 1024 * 1024
-PACK_VMEM_BYTES = 62 * 1024 * 1024
+PACK_VMEM_BYTES = 16 * 1024 * 1024
 
 
 def field(refs, which, rows):
@@ -219,7 +219,7 @@
     return tuple(result)
 
 
-def krylov(load, strips, coef, kept, arrive):
+def krylov(load, strips, coef, kept):
     width = kept.shape[2]
     zero = jnp.zeros((STRIP, width), jnp.float32)
 
@@ -232,11 +232,7 @@
             coef[index, rows, :] = value
         return south
 
-    south = zero
-    half = strips // 2
-    for start in (0, half):
-        arrive(start)
-        south = lax.fori_loop(start, start + half, prepare, south, unroll=half)
+    lax.fori_loop(0, strips, prepare, zero, unroll=strips)
 
     for order in range(ITERS):
         smoothed = ITERS + 1 + order
@@ -278,28 +274,9 @@
 
 
 def tile_kernel(*refs):
-    args, columns, kept, sums, handed, coef, wide = refs[0:6], *refs[6:12]
-    own, arrived = refs[12:18], refs[18]
+    own, columns, kept, sums, handed, coef, wide = refs[0:6], *refs[6:12]
     strips = kept.shape[1] // STRIP
-    half = strips // 2 * STRIP
     side = lax.axis_index("gx")
-    copies = []
-    for part in (1, 0):
-        rows = pl.ds(part * half, half)
-        for index, (arg, buffer) in enumerate(zip(args, own)):
-            place = (slice(None),) * (len(arg.shape) - 2) + (rows, slice(None))
-            copies.append(
-                pltpu.make_async_copy(
-                    arg.at[place], buffer.at[place], arrived.at[index, part]
-                )
-            )
-    for copy in copies:
-        copy.start()
-
-    def arrive(start):
-        for copy in copies[:6] if start == 0 else copies[6:]:
-            copy.wait()
-
     for which, block in enumerate(spread(columns[...], side)):
         wide[which] = block
 
@@ -307,7 +284,7 @@
         rows = strip_rows(strip)
         return jnp.concatenate([field(own, which, rows), wide[which, rows, :]], axis=1)
 
-    krylov(load, strips, coef, kept, arrive)
+    krylov(load, strips, coef, kept)
     zero = jnp.zeros((STRIP, LANES), jnp.float32)
     breadth = kept.shape[2] - LANES
     totals = lax.fori_loop(
@@ -545,6 +522,7 @@
     height, breadth = right_side.shape
     width = breadth + LANES
     args = (right_side, mask, centre, ratio, faces, offdiag)
+    held = [pltpu.with_memory_space_constraint(a, pltpu.HBM) for a in args]
     f32 = jnp.float32
     gy = lax.axis_size("gy")
     swap = [(0, 1), (1, 0)]
@@ -572,7 +550,7 @@
         compiler_params=params(PACK_VMEM_BYTES),
         cost_estimate=cost(0, 4 * 4 * PACKED * breadth),
         name="pack",
-    )(*args)
+    )(*held)
     columns = lax.ppermute(columns, "gx", swap)
     even_in = lax.ppermute(even, "gy", pairs)
     even_corner = lax.ppermute(even_corner, ("gy", "gx"), diagonal(pairs))
@@ -582,8 +560,6 @@
     cells = height * width
     kept, sums, handed = pl.pallas_call(
         tile_kernel,
-        in_specs=[pl.BlockSpec(memory_space=pltpu.HBM)] * len(args)
-        + [pl.BlockSpec(memory_space=pltpu.VMEM)],
         out_shape=(
             jax.ShapeDtypeStruct((KEPT, height, width), f32),
             jax.ShapeDtypeStruct((PRODUCTS, STRIP, LANES), f32),
@@ -592,9 +568,7 @@
         scratch_shapes=[
             pltpu.VMEM((COEFFICIENTS, height, width), f32),
             pltpu.VMEM((FIELDS, height, LANES), f32),
-        ]
-        + [pltpu.VMEM(a.shape, a.dtype) for a in args]
-        + [pltpu.SemaphoreType.DMA((len(args), 2))],
+        ],
         compiler_params=params(TILE_VMEM_BYTES),
         cost_estimate=cost(100 * cells, 4 * cells * (FIELDS + KEPT)),
         name="tile",

time: 41.3 us -> 35.1 us (0.85)
  local copies, waits for them, and re-layouts: 5.31 us -> 0.03 us
  Pallas kernels: 11 us -> 9.7 us
  waiting for transfers between devices: 7.56 us -> 8.01 us
    unnamed x12, local copies, waits for them, and re-layouts: 5.31 us -> 0.03 us
    ppermute x1, waiting for transfers between devices: 0.01 us -> 1.96 us  [body(): even_corner = lax.ppermute(even_corner, ('gy', 'gx'), diagonal(pairs))]
    ppermute x3, waiting for transfers between devices: 6.44 us -> 4.88 us  [body(): gram = gram + lax.ppermute(gram, 'gy', [(i, i ^ reach) for i in range(gy)])]
    pallas_call x1, Pallas kernels: 5.69 us -> 4.93 us  [body(): pl.pallas_call(tile_kernel, out_shape=(jax.ShapeDtypeStruct((KEPT, height...]
    pallas_call x1, Pallas kernels: 2.76 us -> 2.15 us  [body(): pl.pallas_call(pack_kernel, in_specs=[pl.BlockSpec(memory_space=pltpu.HBM...]
  transfers between devices with their start and end apart: 9 -> 9, of which waited for: 4 -> 5; matrix products, arithmetic and copies ran while one was open for 0% -> 0% of each run, Pallas kernels for 14% -> 14%
where the time goes in v5:
time: 35.1 us; the launch traced here: 34.9 us
  starting transfers between devices  16.4 us (47%)
  Pallas kernels  9.7 us (28%)
  waiting for transfers between devices  8.01 us (23%)
  between operations  0.79 us (2%)
    ppermute x3, starting transfers between devices, body(): gram = gram + lax.ppermute(gram, 'gy', [(i, i ^ reach) for i in range(gy)])  7.54 us
    pallas_call x1, Pallas kernels, body(): pl.pallas_call(tile_kernel, out_shape=(jax.ShapeDtypeStruct((KEPT, height...  4.93 us
    ppermute x3, waiting for transfers between devices, body(): gram = gram + lax.ppermute(gram, 'gy', [(i, i ^ reach) for i in range(gy)])  4.88 us
    ppermute x1, starting transfers between devices, body(): even_corner = lax.ppermute(even_corner, ('gy', 'gx'), diagonal(pairs))  4.38 us
    ppermute x1, starting transfers between devices, body(): even_in = lax.ppermute(even, 'gy', pairs)  3.03 us
    pallas_call x1, Pallas kernels, body(): pl.pallas_call(pack_kernel, in_specs=[pl.BlockSpec(memory_space=pltpu.HBM...  2.15 us
    ppermute x1, waiting for transfers between devices, body(): even_corner = lax.ppermute(even_corner, ('gy', 'gx'), diagonal(pairs))  1.96 us
    pallas_call x1, Pallas kernels, body(): pl.pallas_call(combine_kernel, grid=(1,), in_specs=whole(gram.shape, kept...  1.32 us
  transfers between devices with their start and end apart: 9, of which 5 were waited for; matrix products, arithmetic and copies ran while one was open for 0% of the time, Pallas kernels for 14%

profile of v5, /device:TPU:0, one launch (start us, length us, event | category | flops | bytes accessed | tf_op | source)
XLA Modules:
  0.0 34.9 jit_solution(15384383438769959332)
XLA Ops:
  0.6 0.0 copy-start.3
  0.6 0.0 copy-start
  0.7 0.0 copy-start.4
  0.7 0.0 copy-start.5
  0.7 0.0 copy-start.1
  0.7 0.0 copy-start.2
  0.7 2.2 %pack.1 = (f32[72,1024]{1,0:T(8,128)S(1)}, f32[72,1024]{1,0:T(8,128)S(1)}, f32[8,128]{1,0:T(8,128)S(1)}, f32[8,128]{1,0:T(8,128)S(1)}, f32[128,128]{1,0:T(8,128)S(1)}) custom-call(f32[128,1024]{1,0:T(8,128)} %refs_0_.3, s32[128,1024]{1,0:T(8,128)} %refs_1_.3, f32[128,1024]{1,0:T(8,128)} %refs_2_.3, f32[128,1024]{1,0:T(8,128)} %refs_3_.3, ...), custom_call_target="tpu_custom_call" | custom-call | bytes 1179648 | tf_op jit(solution)/shard_map/pack/pallas_call | solution.py:538
  2.9 3.0 %collective-permute-start.1 = (f32[72,1024]{1,0:T(8,128)S(1)}, f32[72,1024]{1,0:T(8,128)S(1)}, u32[]{:S(2)}, u32[]{:S(2)}) collective-permute-start(f32[72,1024]{1,0:T(8,128)S(1)} %get-tuple-element.20), channel_id=1, source_target_pairs={{0,2},{2,0},{4,6},{6,4},{8,10},{10,8},{12,14},{14,12},{1,3},{3,1},... | collective-permute-start | bytes 884744 | tf_op jit(solution)/shard_map/ppermute | solution.py:555
  5.9 0.7 %collective-permute-start.2 = (f32[72,1024]{1,0:T(8,128)S(1)}, f32[72,1024]{1,0:T(8,128)S(1)}, u32[]{:S(2)}, u32[]{:S(2)}) collective-permute-start(f32[72,1024]{1,0:T(8,128)S(1)} %get-tuple-element.21), channel_id=1, source_target_pairs={{2,4},{4,2},{6,8},{8,6},{10,12},{12,10},{3,5},{5,3},{7,9},{9,7},{1... | collective-permute-start | bytes 884744 | tf_op jit(solution)/shard_map/ppermute | solution.py:557
  6.6 0.1 collective-permute-start
  6.6 4.4 %collective-permute-start.3 = (f32[8,128]{1,0:T(8,128)S(1)}, f32[8,128]{1,0:T(8,128)S(1)}, u32[]{:S(2)}, u32[]{:S(2)}) collective-permute-start(f32[8,128]{1,0:T(8,128)S(1)} %get-tuple-element.22), channel_id=1, source_target_pairs={{0,3},{1,2},{2,1},{3,0},{4,7},{5,6},{6,5},{7,4},{8,11},{9,10},{10,... | collective-permute-start | bytes 12296 | tf_op jit(solution)/shard_map/ppermute | solution.py:556
  11.0 0.6 %collective-permute-start.4 = (f32[8,128]{1,0:T(8,128)S(1)}, f32[8,128]{1,0:T(8,128)S(1)}, u32[]{:S(2)}, u32[]{:S(2)}) collective-permute-start(f32[8,128]{1,0:T(8,128)S(1)} %get-tuple-element.23), channel_id=1, source_target_pairs={{2,5},{3,4},{4,3},{5,2},{6,9},{7,8},{8,7},{9,6},{10,13},{11,12},{1... | collective-permute-start | bytes 12296 | tf_op jit(solution)/shard_map/ppermute | solution.py:558
  11.7 0.0 collective-permute-done.refs_6_
  11.7 0.0 copy-done.3
  11.7 0.0 copy-done
  11.7 0.0 copy-done.4
  11.7 0.0 copy-done.5
  11.8 4.9 %tile.1 = (f32[7,128,1152]{2,1,0:T(8,128)S(1)}, f32[12,8,128]{2,1,0:T(8,128)S(1)}, f32[53,8,1152]{2,1,0:T(8,128)S(1)}) custom-call(f32[128,1024]{1,0:T(8,128)S(1)} %copy-done.2, s32[128,1024]{1,0:T(8,128)S(1)} %copy-done.3, f32[128,1024]{1,0:T(8,128)S(1)} %copy-done.4, f32[128,1024]{1,0:T(8,128)S(1)} %copy-done.5, f32[2,128,1024]{2,1,0:T(8,128)S(1)} %copy-done.1, ...), custom_call_target="tpu_custom_call" | custom-call | flops 14745600 | bytes 12386304 | tf_op jit(solution)/shard_map/tile/pallas_call | solution.py:561
  16.7 2.0 %collective-permute-done.3.even_corner = f32[8,128]{1,0:T(8,128)S(1)} collective-permute-done((f32[8,128]{1,0:T(8,128)S(1)}, f32[8,128]{1,0:T(8,128)S(1)}, u32[]{:S(2)}, u32[]{:S(2)}) %collective-permute-start.3) | collective-permute-done | bytes 4128 | tf_op jit(solution)/shard_map/ppermute | solution.py:556
  18.6 0.0 collective-permute-done.4.odd_corner
  18.7 0.0 collective-permute-done.1.even
  18.7 0.0 collective-permute-done.2.odd
  18.7 1.3 %edge.1 = (f32[7,16,1152]{2,1,0:T(8,128)S(1)}, f32[16,128]{1,0:T(8,128)S(1)}) custom-call(f32[53,8,1152]{2,1,0:T(8,128)S(1)} %get-tuple-element.18.handed, f32[72,1024]{1,0:T(8,128)S(1)} %collective-permute-done.1.even, f32[72,1024]{1,0:T(8,128)S(1)} %collective-permute-done.2.odd, f32[8,128]{1,0:T(8,128)S(1)} %collective-permute-done.3.even_corner, ...), custom_call_target="tpu_custom_call" | custom-call | flops 3686400 | bytes 1548288 | tf_op jit(solution)/shard_map/edge/pallas_call | solution.py:581
  20.0 0.0 collective-permute-start.5
  20.0 1.2 %collective-permute-done.5 = f32[16,128]{1,0:T(8,128)S(1)} collective-permute-done((f32[16,128]{1,0:T(8,128)S(1)}, f32[16,128]{1,0:T(8,128)S(1)}, u32[]{:S(2)}, u32[]{:S(2)}) %collective-permute-start.5) | collective-permute-done | bytes 8224 | tf_op jit(solution)/shard_map/ppermute | solution.py:597
  21.1 2.4 %collective-permute-start.6 = (f32[16,128]{1,0:T(8,128)S(1)}, f32[16,128]{1,0:T(8,128)S(1)}, u32[]{:S(2)}, u32[]{:S(2)}) collective-permute-start(f32[16,128]{1,0:T(8,128)S(1)} %add.12), channel_id=1, source_target_pairs={{0,2},{2,0},{4,6},{6,4},{8,10},{10,8},{12,14},{14,12},{1,3},{3,1},... | collective-permute-start | bytes 24584 | tf_op jit(solution)/shard_map/ppermute | solution.py:600
  23.6 1.6 %collective-permute-done.6 = f32[16,128]{1,0:T(8,128)S(1)} collective-permute-done((f32[16,128]{1,0:T(8,128)S(1)}, f32[16,128]{1,0:T(8,128)S(1)}, u32[]{:S(2)}, u32[]{:S(2)}) %collective-permute-start.6) | collective-permute-done | bytes 8224 | tf_op jit(solution)/shard_map/ppermute | solution.py:600
  25.2 2.1 %collective-permute-start.7 = (f32[16,128]{1,0:T(8,128)S(1)}, f32[16,128]{1,0:T(8,128)S(1)}, u32[]{:S(2)}, u32[]{:S(2)}) collective-permute-start(f32[16,128]{1,0:T(8,128)S(1)} %add.13), channel_id=1, source_target_pairs={{0,4},{2,6},{4,0},{6,2},{8,12},{10,14},{12,8},{14,10},{1,5},{3,7},... | collective-permute-start | bytes 24584 | tf_op jit(solution)/shard_map/ppermute | solution.py:600
  27.3 1.6 %collective-permute-done.7 = f32[16,128]{1,0:T(8,128)S(1)} collective-permute-done((f32[16,128]{1,0:T(8,128)S(1)}, f32[16,128]{1,0:T(8,128)S(1)}, u32[]{:S(2)}, u32[]{:S(2)}) %collective-permute-start.7) | collective-permute-done | bytes 8224 | tf_op jit(solution)/shard_map/ppermute | solution.py:600
  28.9 3.0 %collective-permute-start.8 = (f32[16,128]{1,0:T(8,128)S(1)}, f32[16,128]{1,0:T(8,128)S(1)}, u32[]{:S(2)}, u32[]{:S(2)}) collective-permute-start(f32[16,128]{1,0:T(8,128)S(1)} %add.14), channel_id=1, source_target_pairs={{0,8},{2,10},{4,12},{6,14},{8,0},{10,2},{12,4},{14,6},{1,9},{3,11}... | collective-permute-start | bytes 24584 | tf_op jit(solution)/shard_map/ppermute | solution.py:600
  32.0 1.6 %collective-permute-done.8 = f32[16,128]{1,0:T(8,128)S(1)} collective-permute-done((f32[16,128]{1,0:T(8,128)S(1)}, f32[16,128]{1,0:T(8,128)S(1)}, u32[]{:S(2)}, u32[]{:S(2)}) %collective-permute-start.8) | collective-permute-done | bytes 8224 | tf_op jit(solution)/shard_map/ppermute | solution.py:600
  33.6 1.3 %combine.1 = (f32[128,1024]{1,0:T(8,128)}, f32[128,1024]{1,0:T(8,128)}) custom-call(f32[16,128]{1,0:T(8,128)S(1)} %add.15.gram_ref, f32[7,128,1152]{2,1,0:T(8,128)S(1)} %get-tuple-element.30.kept, f32[7,16,1152]{2,1,0:T(8,128)S(1)} %get-tuple-element.31.edges), custom_call_target="tpu_custom_call" | custom-call | flops 1835008 | bytes 4718592 | tf_op jit(solution)/shard_map/combine/pallas_call | solution.py:604
  (6 shorter events, 0.0 us)
Async XLA Ops:
  0.6 11.1 %copy-start.3 = (s32[128,1024]{1,0:T(8,128)S(1)}, s32[128,1024]{1,0:T(8,128)}, u32[]{:S(2)}) copy-start(s32[128,1024]{1,0:T(8,128)} %refs_1_.3) | copy-start | bytes 1572868
  0.6 11.1 %copy-start = (f32[8,128,1024]{2,1,0:T(8,128)S(1)}, f32[8,128,1024]{2,1,0:T(8,128)}, u32[]{:S(2)}) copy-start(f32[8,128,1024]{2,1,0:T(8,128)} %refs_5_.3) | copy-start | bytes 12582916
  0.7 11.1 %copy-start.4 = (f32[128,1024]{1,0:T(8,128)S(1)}, f32[128,1024]{1,0:T(8,128)}, u32[]{:S(2)}) copy-start(f32[128,1024]{1,0:T(8,128)} %refs_2_.3) | copy-start | bytes 1572868
  0.7 11.1 %copy-start.5 = (f32[128,1024]{1,0:T(8,128)S(1)}, f32[128,1024]{1,0:T(8,128)}, u32[]{:S(2)}) copy-start(f32[128,1024]{1,0:T(8,128)} %refs_3_.3) | copy-start | bytes 1572868
  0.7 11.1 %copy-start.1 = (f32[2,128,1024]{2,1,0:T(8,128)S(1)}, f32[2,128,1024]{2,1,0:T(8,128)}, u32[]{:S(2)}) copy-start(f32[2,128,1024]{2,1,0:T(8,128)} %refs_4_.3) | copy-start | bytes 3145732
  0.7 11.1 %copy-start.2 = (f32[128,1024]{1,0:T(8,128)S(1)}, f32[128,1024]{1,0:T(8,128)}, u32[]{:S(2)}) copy-start(f32[128,1024]{1,0:T(8,128)} %refs_0_.3) | copy-start | bytes 1572868
  2.9 15.8 %collective-permute-start.1 = (f32[72,1024]{1,0:T(8,128)S(1)}, f32[72,1024]{1,0:T(8,128)S(1)}, u32[]{:S(2)}, u32[]{:S(2)}) collective-permute-start(f32[72,1024]{1,0:T(8,128)S(1)} %get-tuple-element.20), channel_id=1, source_target_pairs={{0,2},{2,0},{4,6},{6,4},{8,10},{10,8},{12,14},{14,12},{1,3},{3,1},... | collective-permute-start | bytes 884744 | tf_op jit(solution)/shard_map/ppermute | solution.py:555
  5.9 12.8 %collective-permute-start.2 = (f32[72,1024]{1,0:T(8,128)S(1)}, f32[72,1024]{1,0:T(8,128)S(1)}, u32[]{:S(2)}, u32[]{:S(2)}) collective-permute-start(f32[72,1024]{1,0:T(8,128)S(1)} %get-tuple-element.21), channel_id=1, source_target_pairs={{2,4},{4,2},{6,8},{8,6},{10,12},{12,10},{3,5},{5,3},{7,9},{9,7},{1... | collective-permute-start | bytes 884744 | tf_op jit(solution)/shard_map/ppermute | solution.py:557
  6.6 5.1 %collective-permute-start = (f32[128,128]{1,0:T(8,128)S(1)}, f32[128,128]{1,0:T(8,128)S(1)}, u32[]{:S(2)}, u32[]{:S(2)}) collective-permute-start(f32[128,128]{1,0:T(8,128)S(1)} %get-tuple-element.17), channel_id=1, source_target_pairs={{0,1},{1,0},{2,3},{3,2},{4,5},{5,4},{6,7},{7,6},{8,9},{9,8},{10,11... | collective-permute-start | bytes 196616 | tf_op jit(solution)/shard_map/ppermute | solution.py:554
  6.6 12.0 %collective-permute-start.3 = (f32[8,128]{1,0:T(8,128)S(1)}, f32[8,128]{1,0:T(8,128)S(1)}, u32[]{:S(2)}, u32[]{:S(2)}) collective-permute-start(f32[8,128]{1,0:T(8,128)S(1)} %get-tuple-element.22), channel_id=1, source_target_pairs={{0,3},{1,2},{2,1},{3,0},{4,7},{5,6},{6,5},{7,4},{8,11},{9,10},{10,... | collective-permute-start | bytes 12296 | tf_op jit(solution)/shard_map/ppermute | solution.py:556
  11.0 7.6 %collective-permute-start.4 = (f32[8,128]{1,0:T(8,128)S(1)}, f32[8,128]{1,0:T(8,128)S(1)}, u32[]{:S(2)}, u32[]{:S(2)}) collective-permute-start(f32[8,128]{1,0:T(8,128)S(1)} %get-tuple-element.23), channel_id=1, source_target_pairs={{2,5},{3,4},{4,3},{5,2},{6,9},{7,8},{8,7},{9,6},{10,13},{11,12},{1... | collective-permute-start | bytes 12296 | tf_op jit(solution)/shard_map/ppermute | solution.py:558
  20.0 1.2 %collective-permute-start.5 = (f32[16,128]{1,0:T(8,128)S(1)}, f32[16,128]{1,0:T(8,128)S(1)}, u32[]{:S(2)}, u32[]{:S(2)}) collective-permute-start(f32[16,128]{1,0:T(8,128)S(1)} %get-tuple-element.29), channel_id=1, source_target_pairs={{0,1},{1,0},{2,3},{3,2},{4,5},{5,4},{6,7},{7,6},{8,9},{9,8},{10,11... | collective-permute-start | bytes 24584 | tf_op jit(solution)/shard_map/ppermute | solution.py:597
  21.1 4.1 %collective-permute-start.6 = (f32[16,128]{1,0:T(8,128)S(1)}, f32[16,128]{1,0:T(8,128)S(1)}, u32[]{:S(2)}, u32[]{:S(2)}) collective-permute-start(f32[16,128]{1,0:T(8,128)S(1)} %add.12), channel_id=1, source_target_pairs={{0,2},{2,0},{4,6},{6,4},{8,10},{10,8},{12,14},{14,12},{1,3},{3,1},... | collective-permute-start | bytes 24584 | tf_op jit(solution)/shard_map/ppermute | solution.py:600
  25.2 3.7 %collective-permute-start.7 = (f32[16,128]{1,0:T(8,128)S(1)}, f32[16,128]{1,0:T(8,128)S(1)}, u32[]{:S(2)}, u32[]{:S(2)}) collective-permute-start(f32[16,128]{1,0:T(8,128)S(1)} %add.13), channel_id=1, source_target_pairs={{0,4},{2,6},{4,0},{6,2},{8,12},{10,14},{12,8},{14,10},{1,5},{3,7},... | collective-permute-start | bytes 24584 | tf_op jit(solution)/shard_map/ppermute | solution.py:600
  28.9 4.7 %collective-permute-start.8 = (f32[16,128]{1,0:T(8,128)S(1)}, f32[16,128]{1,0:T(8,128)S(1)}, u32[]{:S(2)}, u32[]{:S(2)}) collective-permute-start(f32[16,128]{1,0:T(8,128)S(1)} %add.14), channel_id=1, source_target_pairs={{0,8},{2,10},{4,12},{6,14},{8,0},{10,2},{12,4},{14,6},{1,9},{3,11}... | collective-permute-start | bytes 24584 | tf_op jit(solution)/shard_map/ppermute | solution.py:600

commit v6 on v5

--- a/solution.py
+++ b/solution.py
@@ -27,6 +27,7 @@
 PRODUCTS = (ITERS + 1) * ITERS
 KEPT = 2 * ITERS + 1
 SLOT = 8
+PARTS = 4
 COEFFICIENTS = 15
 NEAR = 2 * COEFFICIENTS
 SOUTH = NEAR + 6
@@ -67,6 +68,13 @@
     return lax.broadcasted_iota(jnp.int32, shape, len(shape) - 1)
 
 
+def beside(refs, which, rows, side):
+    breadth = refs[0].shape[1]
+    west = field([ref.at[..., 0:LANES] for ref in refs], which, rows)
+    east = field([ref.at[..., breadth - LANES : breadth] for ref in refs], which, rows)
+    return jnp.where(side == 0, east, west)
+
+
 def squeezed(near, side):
     start = jnp.where(side == 0, SLOT, 0)
     total = None
@@ -92,36 +100,33 @@
 
 def pack_kernel(*refs):
     args = refs[0:6]
-    even, odd, even_corner, odd_corner, columns = refs[6:11]
-    ends, sides, end_arrived, side_arrived = refs[11:17], refs[17:23], refs[23], refs[24]
+    even, odd, even_corner, odd_corner = refs[6:10]
+    ends, arrived = refs[10:16], refs[16]
     height, breadth = args[0].shape
     side = lax.axis_index("gx")
     parity = lax.rem(lax.axis_index("gy"), 2)
-    beside = pl.multiple_of(jnp.where(side == 0, breadth - LANES, 0), LANES)
-    copies, more = [], []
-    for index, (arg, end, edge) in enumerate(zip(args, ends, sides)):
+    copies = []
+    for index, (arg, end) in enumerate(zip(args, ends)):
         lead = (slice(None),) * (len(arg.shape) - 2)
         for which, start in enumerate((0, height - STRIP)):
             copies.append(
                 pltpu.make_async_copy(
                     arg.at[lead + (pl.ds(start, STRIP), slice(None))],
                     end.at[which],
-                    end_arrived.at[index, which],
+                    arrived.at[index, which],
                 )
             )
-        more.append(
-            pltpu.make_async_copy(
-                arg.at[lead + (slice(None), pl.ds(beside, LANES))],
-                edge,
-                side_arrived.at[index],
-            )
-        )
-    for copy in copies + more:
+    for copy in copies:
         copy.start()
     for copy in copies:
         copy.wait()
     first = [end.at[0] for end in ends]
     last = [end.at[1] for end in ends]
+    rows = slice(0, STRIP)
+    corner_first = squeezed(lambda which: beside(first, which, rows, side), side)
+    corner_last = squeezed(lambda which: beside(last, which, rows, side), side)
+    even_corner[...] = jnp.where(parity == 0, corner_last, corner_first)
+    odd_corner[...] = jnp.where(parity == 0, corner_first, corner_last)
 
     @pl.when(parity == 0)
     def _():
@@ -133,13 +138,11 @@
         trimmed(even, first, HIGH_ROWS, False)
         trimmed(odd, last, LOW_ROWS, True)
 
-    for copy in more:
-        copy.wait()
-    packed = squeezed(lambda which: field(sides, which, slice(None)), side)
-    columns[...] = packed
-    corner_first, corner_last = packed[0:STRIP, :], packed[height - STRIP : height, :]
-    even_corner[...] = jnp.where(parity == 0, corner_last, corner_first)
-    odd_corner[...] = jnp.where(parity == 0, corner_first, corner_last)
+
+def columns_kernel(*refs):
+    args, columns = refs[0:6], refs[7]
+    side = lax.axis_index("gx")
+    columns[...] = squeezed(lambda which: beside(args, which, slice(None), side), side)
 
 
 def row_above(block, before):
@@ -471,8 +474,10 @@
     return steps, residual
 
 
-def combine_kernel(gram_ref, kept, edges, solution_ref, residual_ref):
+def combine_kernel(gram_ref, kept, edges, solution_out, residual_out, *scratch):
+    solution_ref, residual_ref, left = scratch
     height, breadth = solution_ref.shape
+    part = height // PARTS
     gram = [
         [gram_ref[i * ITERS + j : i * ITERS + j + 1, :] for j in range(ITERS)]
         for i in range(ITERS + 1)
@@ -495,15 +500,27 @@
             total = term if total is None else total + term
         residual_ref[rows_to, :] = total
 
-    put(edges, slice(0, STRIP), slice(0, STRIP))
-    put(edges, slice(STRIP, 2 * STRIP), slice(height - STRIP, height))
-
-    def middle(strip, carried):
-        rows = strip_rows(strip)
-        put(kept, rows, rows)
-        return carried
-
-    lax.fori_loop(1, height // STRIP - 1, middle, 0)
+    copies = []
+    for step in range(PARTS):
+        for strip in range(step * part // STRIP, (step + 1) * part // STRIP):
+            rows = slice(strip * STRIP, (strip + 1) * STRIP)
+            if strip == 0:
+                put(edges, slice(0, STRIP), rows)
+            elif strip == height // STRIP - 1:
+                put(edges, slice(STRIP, 2 * STRIP), rows)
+            else:
+                put(kept, rows, rows)
+        rows = pl.ds(step * part, part)
+        for index, (source, target) in enumerate(
+            ((solution_ref, solution_out), (residual_ref, residual_out))
+        ):
+            copy = pltpu.make_async_copy(
+                source.at[rows, :], target.at[rows, :], left.at[index, step]
+            )
+            copy.start()
+            copies.append(copy)
+    for copy in copies:
+        copy.wait()
 
 
 def params(limit=VMEM_BYTES):
@@ -512,10 +529,6 @@
 
 def cost(flops, moved):
     return pl.CostEstimate(flops=flops, bytes_accessed=moved, transcendentals=0)
-
-
-def whole(*shapes):
-    return [pl.BlockSpec(shape, lambda step, n=len(shape): (0,) * n) for shape in shapes]
 
 
 def body(right_side, faces, ratio, centre, offdiag, mask):
@@ -535,22 +548,27 @@
     packed = jax.ShapeDtypeStruct((PACKED, breadth), f32)
     corner = jax.ShapeDtypeStruct((STRIP, LANES), f32)
     columns = jax.ShapeDtypeStruct((height, LANES), f32)
-    even, odd, even_corner, odd_corner, columns = pl.pallas_call(
+    even, odd, even_corner, odd_corner = pl.pallas_call(
         pack_kernel,
         in_specs=[pl.BlockSpec(memory_space=pltpu.HBM)] * len(args),
-        out_shape=(packed, packed, corner, corner, columns),
+        out_shape=(packed, packed, corner, corner),
         scratch_shapes=[
             pltpu.VMEM((2,) + a.shape[:-2] + (STRIP, breadth), a.dtype) for a in args
         ]
-        + [pltpu.VMEM(a.shape[:-1] + (LANES,), a.dtype) for a in args]
-        + [
-            pltpu.SemaphoreType.DMA((len(args), 2)),
-            pltpu.SemaphoreType.DMA((len(args),)),
-        ],
+        + [pltpu.SemaphoreType.DMA((len(args), 2))],
         compiler_params=params(PACK_VMEM_BYTES),
         cost_estimate=cost(0, 4 * 4 * PACKED * breadth),
         name="pack",
     )(*held)
+    columns = pl.pallas_call(
+        columns_kernel,
+        in_specs=[pl.BlockSpec(memory_space=pltpu.VMEM)] * len(args)
+        + [pl.BlockSpec(memory_space=pl.ANY)],
+        out_shape=columns,
+        compiler_params=params(PACK_VMEM_BYTES),
+        cost_estimate=cost(0, 4 * FIELDS * height * LANES),
+        name="columns",
+    )(*args, odd_corner)
     columns = lax.ppermute(columns, "gx", swap)
     even_in = lax.ppermute(even, "gy", pairs)
     even_corner = lax.ppermute(even_corner, ("gy", "gx"), diagonal(pairs))
@@ -603,10 +621,10 @@
     tile = jax.ShapeDtypeStruct((height, breadth), f32)
     return pl.pallas_call(
         combine_kernel,
-        grid=(1,),
-        in_specs=whole(gram.shape, kept.shape, edges.shape),
-        out_specs=whole(tile.shape, tile.shape),
+        out_specs=(pl.BlockSpec(memory_space=pltpu.HBM),) * 2,
         out_shape=(tile, tile),
+        scratch_shapes=[pltpu.VMEM(tile.shape, f32)] * 2
+        + [pltpu.SemaphoreType.DMA((2, PARTS))],
         compiler_params=params(),
         cost_estimate=cost(14 * height * breadth, 4 * height * breadth * (KEPT + 2)),
         name="combine",

time: 35.1 us -> 34.4 us (0.980)
    pallas_call x1, Pallas kernels: 2.15 us -> 1.66 us  [body(): pl.pallas_call(pack_kernel, in_specs=[pl.BlockSpec(memory_space=pltpu.HBM...]
    ppermute x1, waiting for transfers between devices: 1.96 us -> 1.55 us  [body(): even_corner = lax.ppermute(even_corner, ('gy', 'gx'), diagonal(pairs))]
    pallas_call x1 -> x2, Pallas kernels: 1.32 us -> 1.43 us  [the longest x1 1.11 us: body(): pl.pallas_call(combine_kernel, out_specs=(pl.BlockSpec(memory_space=pltpu...]
  transfers between devices with their start and end apart: 9 -> 9, of which waited for: 5 -> 5; matrix products, arithmetic and copies ran while one was open for 0% -> 0% of each run, Pallas kernels for 14% -> 16%
where the time goes in v6:
time: 34.4 us; the launch traced here: 34.2 us
  starting transfers between devices  16.3 us (47%)
  Pallas kernels  9.38 us (27%)
  waiting for transfers between devices  7.67 us (22%)
  between operations  0.8 us (2%)
    ppermute x3, starting transfers between devices, body(): gram = gram + lax.ppermute(gram, 'gy', [(i, i ^ reach) for i in range(gy)])  7.46 us
    pallas_call x1, Pallas kernels, body(): pl.pallas_call(tile_kernel, out_shape=(jax.ShapeDtypeStruct((KEPT, height...  5.01 us
    ppermute x3, waiting for transfers between devices, body(): gram = gram + lax.ppermute(gram, 'gy', [(i, i ^ reach) for i in range(gy)])  4.95 us
    ppermute x1, starting transfers between devices, body(): even_corner = lax.ppermute(even_corner, ('gy', 'gx'), diagonal(pairs))  4.38 us
    ppermute x1, starting transfers between devices, body(): even_in = lax.ppermute(even, 'gy', pairs)  3.05 us
    pallas_call x1, Pallas kernels, body(): pl.pallas_call(pack_kernel, in_specs=[pl.BlockSpec(memory_space=pltpu.HBM...  1.66 us
    ppermute x1, waiting for transfers between devices, body(): even_corner = lax.ppermute(even_corner, ('gy', 'gx'), diagonal(pairs))  1.55 us
    pallas_call x1, Pallas kernels, body(): pl.pallas_call(edge_kernel, out_shape=(jax.ShapeDtypeStruct((KEPT, rows,...  1.28 us
  transfers between devices with their start and end apart: 9, of which 5 were waited for; matrix products, arithmetic and copies ran while one was open for 0% of the time, Pallas kernels for 16%

profile of v6, /device:TPU:0, one launch (start us, length us, event | category | flops | bytes accessed | tf_op | source)
XLA Modules:
  0.0 34.2 jit_solution(15462204622270749876)
XLA Ops:
  0.6 0.0 copy-start.3
  0.6 0.0 copy-start
  0.7 0.0 copy-start.4
  0.7 0.0 copy-start.5
  0.7 0.0 copy-start.1
  0.7 0.0 copy-start.2
  0.7 1.7 %pack.1 = (f32[72,1024]{1,0:T(8,128)S(1)}, f32[72,1024]{1,0:T(8,128)S(1)}, f32[8,128]{1,0:T(8,128)S(1)}, f32[8,128]{1,0:T(8,128)S(1)}) custom-call(f32[128,1024]{1,0:T(8,128)} %refs_0_.5, s32[128,1024]{1,0:T(8,128)} %refs_1_.5, f32[128,1024]{1,0:T(8,128)} %refs_2_.5, f32[128,1024]{1,0:T(8,128)} %refs_3_.5, f32[2,128,1024]{2,1,0:T(8,128)} %refs_4_.5, ...), custom_call_target="tpu_custom_call" | custom-call | bytes 1179648 | tf_op jit(solution)/shard_map/pack/pallas_call | solution.py:551
  2.4 3.1 %collective-permute-start.1 = (f32[72,1024]{1,0:T(8,128)S(1)}, f32[72,1024]{1,0:T(8,128)S(1)}, u32[]{:S(2)}, u32[]{:S(2)}) collective-permute-start(f32[72,1024]{1,0:T(8,128)S(1)} %get-tuple-element.19), channel_id=1, source_target_pairs={{0,2},{2,0},{4,6},{6,4},{8,10},{10,8},{12,14},{14,12},{1,3},{3,1},... | collective-permute-start | bytes 884744 | tf_op jit(solution)/shard_map/ppermute | solution.py:573
  5.4 0.7 %collective-permute-start.2 = (f32[72,1024]{1,0:T(8,128)S(1)}, f32[72,1024]{1,0:T(8,128)S(1)}, u32[]{:S(2)}, u32[]{:S(2)}) collective-permute-start(f32[72,1024]{1,0:T(8,128)S(1)} %get-tuple-element.20), channel_id=1, source_target_pairs={{2,4},{4,2},{6,8},{8,6},{10,12},{12,10},{3,5},{5,3},{7,9},{9,7},{1... | collective-permute-start | bytes 884744 | tf_op jit(solution)/shard_map/ppermute | solution.py:575
  6.1 0.0 copy-done.3
  6.1 0.0 copy-done
  6.1 0.0 copy-done.4
  6.1 0.3 columns.1
  6.5 0.1 collective-permute-start
  6.6 4.4 %collective-permute-start.3 = (f32[8,128]{1,0:T(8,128)S(1)}, f32[8,128]{1,0:T(8,128)S(1)}, u32[]{:S(2)}, u32[]{:S(2)}) collective-permute-start(f32[8,128]{1,0:T(8,128)S(1)} %get-tuple-element.21), channel_id=1, source_target_pairs={{0,3},{1,2},{2,1},{3,0},{4,7},{5,6},{6,5},{7,4},{8,11},{9,10},{10,... | collective-permute-start | bytes 12296 | tf_op jit(solution)/shard_map/ppermute | solution.py:574
  10.9 0.6 %collective-permute-start.4 = (f32[8,128]{1,0:T(8,128)S(1)}, f32[8,128]{1,0:T(8,128)S(1)}, u32[]{:S(2)}, u32[]{:S(2)}) collective-permute-start(f32[8,128]{1,0:T(8,128)S(1)} %get-tuple-element.16.refs_6_), channel_id=1, source_target_pairs={{2,5},{3,4},{4,3},{5,2},{6,9},{7,8},{8,7},{9,6},{10,13},{11,12},{1... | collective-permute-start | bytes 12296 | tf_op jit(solution)/shard_map/ppermute | solution.py:576
  11.6 0.0 collective-permute-done.refs_6_
  11.6 5.0 %tile.1 = (f32[7,128,1152]{2,1,0:T(8,128)S(1)}, f32[12,8,128]{2,1,0:T(8,128)S(1)}, f32[53,8,1152]{2,1,0:T(8,128)S(1)}) custom-call(f32[128,1024]{1,0:T(8,128)S(1)} %copy-done.2, s32[128,1024]{1,0:T(8,128)S(1)} %copy-done.3, f32[128,1024]{1,0:T(8,128)S(1)} %copy-done.4, f32[128,1024]{1,0:T(8,128)S(1)} %copy-done.5, f32[2,128,1024]{2,1,0:T(8,128)S(1)} %copy-done.1, ...), custom_call_target="tpu_custom_call" | custom-call | flops 14745600 | bytes 12386304 | tf_op jit(solution)/shard_map/tile/pallas_call | solution.py:579
  16.6 1.6 %collective-permute-done.3.even_corner = f32[8,128]{1,0:T(8,128)S(1)} collective-permute-done((f32[8,128]{1,0:T(8,128)S(1)}, f32[8,128]{1,0:T(8,128)S(1)}, u32[]{:S(2)}, u32[]{:S(2)}) %collective-permute-start.3) | collective-permute-done | bytes 4128 | tf_op jit(solution)/shard_map/ppermute | solution.py:574
  18.2 0.0 collective-permute-done.4.odd_corner
  18.2 0.0 collective-permute-done.1.even
  18.2 0.0 collective-permute-done.2.odd
  18.2 1.3 %edge.1 = (f32[7,16,1152]{2,1,0:T(8,128)S(1)}, f32[16,128]{1,0:T(8,128)S(1)}) custom-call(f32[53,8,1152]{2,1,0:T(8,128)S(1)} %get-tuple-element.17.handed, f32[72,1024]{1,0:T(8,128)S(1)} %collective-permute-done.1.even, f32[72,1024]{1,0:T(8,128)S(1)} %collective-permute-done.2.odd, f32[8,128]{1,0:T(8,128)S(1)} %collective-permute-done.3.even_corner, ...), custom_call_target="tpu_custom_call" | custom-call | flops 3686400 | bytes 1548288 | tf_op jit(solution)/shard_map/edge/pallas_call | solution.py:599
  19.5 0.0 collective-permute-start.5
  19.5 1.2 %collective-permute-done.5 = f32[16,128]{1,0:T(8,128)S(1)} collective-permute-done((f32[16,128]{1,0:T(8,128)S(1)}, f32[16,128]{1,0:T(8,128)S(1)}, u32[]{:S(2)}, u32[]{:S(2)}) %collective-permute-start.5) | collective-permute-done | bytes 8224 | tf_op jit(solution)/shard_map/ppermute | solution.py:615
  20.7 2.5 %collective-permute-start.6 = (f32[16,128]{1,0:T(8,128)S(1)}, f32[16,128]{1,0:T(8,128)S(1)}, u32[]{:S(2)}, u32[]{:S(2)}) collective-permute-start(f32[16,128]{1,0:T(8,128)S(1)} %add.12), channel_id=1, source_target_pairs={{0,2},{2,0},{4,6},{6,4},{8,10},{10,8},{12,14},{14,12},{1,3},{3,1},... | collective-permute-start | bytes 24584 | tf_op jit(solution)/shard_map/ppermute | solution.py:618
  23.2 1.6 %collective-permute-done.6 = f32[16,128]{1,0:T(8,128)S(1)} collective-permute-done((f32[16,128]{1,0:T(8,128)S(1)}, f32[16,128]{1,0:T(8,128)S(1)}, u32[]{:S(2)}, u32[]{:S(2)}) %collective-permute-start.6) | collective-permute-done | bytes 8224 | tf_op jit(solution)/shard_map/ppermute | solution.py:618
  24.8 2.0 %collective-permute-start.7 = (f32[16,128]{1,0:T(8,128)S(1)}, f32[16,128]{1,0:T(8,128)S(1)}, u32[]{:S(2)}, u32[]{:S(2)}) collective-permute-start(f32[16,128]{1,0:T(8,128)S(1)} %add.13), channel_id=1, source_target_pairs={{0,4},{2,6},{4,0},{6,2},{8,12},{10,14},{12,8},{14,10},{1,5},{3,7},... | collective-permute-start | bytes 24584 | tf_op jit(solution)/shard_map/ppermute | solution.py:618
  26.8 1.7 %collective-permute-done.7 = f32[16,128]{1,0:T(8,128)S(1)} collective-permute-done((f32[16,128]{1,0:T(8,128)S(1)}, f32[16,128]{1,0:T(8,128)S(1)}, u32[]{:S(2)}, u32[]{:S(2)}) %collective-permute-start.7) | collective-permute-done | bytes 8224 | tf_op jit(solution)/shard_map/ppermute | solution.py:618
  28.5 3.0 %collective-permute-start.8 = (f32[16,128]{1,0:T(8,128)S(1)}, f32[16,128]{1,0:T(8,128)S(1)}, u32[]{:S(2)}, u32[]{:S(2)}) collective-permute-start(f32[16,128]{1,0:T(8,128)S(1)} %add.14), channel_id=1, source_target_pairs={{0,8},{2,10},{4,12},{6,14},{8,0},{10,2},{12,4},{14,6},{1,9},{3,11}... | collective-permute-start | bytes 24584 | tf_op jit(solution)/shard_map/ppermute | solution.py:618
  31.4 1.6 %collective-permute-done.8 = f32[16,128]{1,0:T(8,128)S(1)} collective-permute-done((f32[16,128]{1,0:T(8,128)S(1)}, f32[16,128]{1,0:T(8,128)S(1)}, u32[]{:S(2)}, u32[]{:S(2)}) %collective-permute-start.8) | collective-permute-done | bytes 8224 | tf_op jit(solution)/shard_map/ppermute | solution.py:618
  33.1 1.1 %combine.1 = (f32[128,1024]{1,0:T(8,128)}, f32[128,1024]{1,0:T(8,128)}) custom-call(f32[16,128]{1,0:T(8,128)S(1)} %add.15.gram_ref, f32[7,128,1152]{2,1,0:T(8,128)S(1)} %get-tuple-element.28.kept, f32[7,16,1152]{2,1,0:T(8,128)S(1)} %get-tuple-element.29.edges), custom_call_target="tpu_custom_call" | custom-call | flops 1835008 | bytes 4718592 | tf_op jit(solution)/shard_map/combine/pallas_call | solution.py:622
  (7 shorter events, 0.0 us)
Async XLA Ops:
  0.6 5.5 %copy-start.3 = (s32[128,1024]{1,0:T(8,128)S(1)}, s32[128,1024]{1,0:T(8,128)}, u32[]{:S(2)}) copy-start(s32[128,1024]{1,0:T(8,128)} %refs_1_.5) | copy-start | bytes 1572868
  0.6 5.5 %copy-start = (f32[8,128,1024]{2,1,0:T(8,128)S(1)}, f32[8,128,1024]{2,1,0:T(8,128)}, u32[]{:S(2)}) copy-start(f32[8,128,1024]{2,1,0:T(8,128)} %refs_5_.5) | copy-start | bytes 12582916
  0.7 5.5 %copy-start.4 = (f32[128,1024]{1,0:T(8,128)S(1)}, f32[128,1024]{1,0:T(8,128)}, u32[]{:S(2)}) copy-start(f32[128,1024]{1,0:T(8,128)} %refs_2_.5) | copy-start | bytes 1572868
  0.7 5.5 %copy-start.5 = (f32[128,1024]{1,0:T(8,128)S(1)}, f32[128,1024]{1,0:T(8,128)}, u32[]{:S(2)}) copy-start(f32[128,1024]{1,0:T(8,128)} %refs_3_.5) | copy-start | bytes 1572868
  0.7 5.5 %copy-start.1 = (f32[2,128,1024]{2,1,0:T(8,128)S(1)}, f32[2,128,1024]{2,1,0:T(8,128)}, u32[]{:S(2)}) copy-start(f32[2,128,1024]{2,1,0:T(8,128)} %refs_4_.5) | copy-start | bytes 3145732
  0.7 5.5 %copy-start.2 = (f32[128,1024]{1,0:T(8,128)S(1)}, f32[128,1024]{1,0:T(8,128)}, u32[]{:S(2)}) copy-start(f32[128,1024]{1,0:T(8,128)} %refs_0_.5) | copy-start | bytes 1572868
  2.4 15.8 %collective-permute-start.1 = (f32[72,1024]{1,0:T(8,128)S(1)}, f32[72,1024]{1,0:T(8,128)S(1)}, u32[]{:S(2)}, u32[]{:S(2)}) collective-permute-start(f32[72,1024]{1,0:T(8,128)S(1)} %get-tuple-element.19), channel_id=1, source_target_pairs={{0,2},{2,0},{4,6},{6,4},{8,10},{10,8},{12,14},{14,12},{1,3},{3,1},... | collective-permute-start | bytes 884744 | tf_op jit(solution)/shard_map/ppermute | solution.py:573
  5.4 12.8 %collective-permute-start.2 = (f32[72,1024]{1,0:T(8,128)S(1)}, f32[72,1024]{1,0:T(8,128)S(1)}, u32[]{:S(2)}, u32[]{:S(2)}) collective-permute-start(f32[72,1024]{1,0:T(8,128)S(1)} %get-tuple-element.20), channel_id=1, source_target_pairs={{2,4},{4,2},{6,8},{8,6},{10,12},{12,10},{3,5},{5,3},{7,9},{9,7},{1... | collective-permute-start | bytes 884744 | tf_op jit(solution)/shard_map/ppermute | solution.py:575
  6.5 5.1 %collective-permute-start = (f32[128,128]{1,0:T(8,128)S(1)}, f32[128,128]{1,0:T(8,128)S(1)}, u32[]{:S(2)}, u32[]{:S(2)}) collective-permute-start(f32[128,128]{1,0:T(8,128)S(1)} %columns.1), channel_id=1, source_target_pairs={{0,1},{1,0},{2,3},{3,2},{4,5},{5,4},{6,7},{7,6},{8,9},{9,8},{10,11... | collective-permute-start | bytes 196616 | tf_op jit(solution)/shard_map/ppermute | solution.py:572
  6.6 11.6 %collective-permute-start.3 = (f32[8,128]{1,0:T(8,128)S(1)}, f32[8,128]{1,0:T(8,128)S(1)}, u32[]{:S(2)}, u32[]{:S(2)}) collective-permute-start(f32[8,128]{1,0:T(8,128)S(1)} %get-tuple-element.21), channel_id=1, source_target_pairs={{0,3},{1,2},{2,1},{3,0},{4,7},{5,6},{6,5},{7,4},{8,11},{9,10},{10,... | collective-permute-start | bytes 12296 | tf_op jit(solution)/shard_map/ppermute | solution.py:574
  10.9 7.2 %collective-permute-start.4 = (f32[8,128]{1,0:T(8,128)S(1)}, f32[8,128]{1,0:T(8,128)S(1)}, u32[]{:S(2)}, u32[]{:S(2)}) collective-permute-start(f32[8,128]{1,0:T(8,128)S(1)} %get-tuple-element.16.refs_6_), channel_id=1, source_target_pairs={{2,5},{3,4},{4,3},{5,2},{6,9},{7,8},{8,7},{9,6},{10,13},{11,12},{1... | collective-permute-start | bytes 12296 | tf_op jit(solution)/shard_map/ppermute | solution.py:576
  19.5 1.2 %collective-permute-start.5 = (f32[16,128]{1,0:T(8,128)S(1)}, f32[16,128]{1,0:T(8,128)S(1)}, u32[]{:S(2)}, u32[]{:S(2)}) collective-permute-start(f32[16,128]{1,0:T(8,128)S(1)} %get-tuple-element.27), channel_id=1, source_target_pairs={{0,1},{1,0},{2,3},{3,2},{4,5},{5,4},{6,7},{7,6},{8,9},{9,8},{10,11... | collective-permute-start | bytes 24584 | tf_op jit(solution)/shard_map/ppermute | solution.py:615
  20.7 4.2 %collective-permute-start.6 = (f32[16,128]{1,0:T(8,128)S(1)}, f32[16,128]{1,0:T(8,128)S(1)}, u32[]{:S(2)}, u32[]{:S(2)}) collective-permute-start(f32[16,128]{1,0:T(8,128)S(1)} %add.12), channel_id=1, source_target_pairs={{0,2},{2,0},{4,6},{6,4},{8,10},{10,8},{12,14},{14,12},{1,3},{3,1},... | collective-permute-start | bytes 24584 | tf_op jit(solution)/shard_map/ppermute | solution.py:618
  24.8 3.7 %collective-permute-start.7 = (f32[16,128]{1,0:T(8,128)S(1)}, f32[16,128]{1,0:T(8,128)S(1)}, u32[]{:S(2)}, u32[]{:S(2)}) collective-permute-start(f32[16,128]{1,0:T(8,128)S(1)} %add.13), channel_id=1, source_target_pairs={{0,4},{2,6},{4,0},{6,2},{8,12},{10,14},{12,8},{14,10},{1,5},{3,7},... | collective-permute-start | bytes 24584 | tf_op jit(solution)/shard_map/ppermute | solution.py:618
  28.5 4.6 %collective-permute-start.8 = (f32[16,128]{1,0:T(8,128)S(1)}, f32[16,128]{1,0:T(8,128)S(1)}, u32[]{:S(2)}, u32[]{:S(2)}) collective-permute-start(f32[16,128]{1,0:T(8,128)S(1)} %add.14), channel_id=1, source_target_pairs={{0,8},{2,10},{4,12},{6,14},{8,0},{10,2},{12,4},{14,6},{1,9},{3,11}... | collective-permute-start | bytes 24584 | tf_op jit(solution)/shard_map/ppermute | solution.py:618

commit v7 on v6

--- a/solution.py
+++ b/solution.py
@@ -23,7 +23,7 @@
 HIGH_ROWS = [REACH, REACH - 1, REACH - 1, REACH - 2, REACH - 2, REACH - 1] + [
     REACH - 1 - down for down, _ in neighbour_steps
 ]
-PACKED = -(-max(sum(LOW_ROWS), sum(HIGH_ROWS)) // STRIP) * STRIP
+PACKED = max(sum(LOW_ROWS), sum(HIGH_ROWS))
 PRODUCTS = (ITERS + 1) * ITERS
 KEPT = 2 * ITERS + 1
 SLOT = 8
@@ -54,14 +54,25 @@
     return offdiag[which - 6, rows, :]
 
 
+def stacked(place, count, breadth):
+    for block in range(breadth // LANES):
+        start = block * PACKED + place
+        yield slice(start, start + count), slice(block * LANES, (block + 1) * LANES)
+
+
 def trimmed(out, refs, counts, at_end):
+    breadth = out.shape[0] // PACKED * LANES
     place = 0
     for which, count in enumerate(counts):
         rows = slice(STRIP - count, STRIP) if at_end else slice(0, count)
-        out[place : place + count, :] = field(refs, which, rows)
+        value = field(refs, which, rows)
+        for target, lanes in stacked(place, count, breadth):
+            out[target, :] = value[:, lanes]
         place += count
     if place < PACKED:
-        out[place:PACKED, :] = jnp.zeros((PACKED - place, out.shape[1]), jnp.float32)
+        zero = jnp.zeros((PACKED - place, LANES), jnp.float32)
+        for target, _ in stacked(place, PACKED - place, breadth):
+            out[target, :] = zero
 
 
 def lanes_of(shape):
@@ -295,7 +306,7 @@
         strips - 1,
         lambda strip, totals: gathered(totals, kept, strip_rows(strip), breadth),
         (zero,) * PRODUCTS,
-        unroll=2,
+        unroll=7,
     )
     for index in range(PRODUCTS):
         sums[index] = totals[index]
@@ -318,7 +329,7 @@
 def edge_kernel(
     handed, even, odd, even_corner, odd_corner, sums, kept, gram, joined, coef, outer
 ):
-    breadth = even.shape[1]
+    breadth = even.shape[0] // PACKED * LANES
     width = breadth + LANES
     side = lax.axis_index("gx")
     parity = lax.rem(lax.axis_index("gy"), 2)
@@ -331,16 +342,16 @@
         joined[which, low_rows, breadth:width] = low_corner[which]
         joined[which, high_rows, breadth:width] = high_corner[which]
         count = LOW_ROWS[which]
-        place = slice(place_low, place_low + count)
-        joined[which, STRIP - count : STRIP, 0:breadth] = jnp.where(
-            parity == 0, odd[place, :], even[place, :]
-        )
+        for place, lanes in stacked(place_low, count, breadth):
+            joined[which, STRIP - count : STRIP, lanes] = jnp.where(
+                parity == 0, odd[place, :], even[place, :]
+            )
         place_low += count
         count = HIGH_ROWS[which]
-        place = slice(place_high, place_high + count)
-        joined[which, STRIP : STRIP + count, 0:breadth] = jnp.where(
-            parity == 0, even[place, :], odd[place, :]
-        )
+        for place, lanes in stacked(place_high, count, breadth):
+            joined[which, STRIP : STRIP + count, lanes] = jnp.where(
+                parity == 0, even[place, :], odd[place, :]
+            )
         place_high += count
 
     zero = jnp.zeros((STRIP, width), jnp.float32)
@@ -545,7 +556,7 @@
     def diagonal(partners):
         return [(2 * a + c, 2 * b + 1 - c) for a, b in partners for c in (0, 1)]
 
-    packed = jax.ShapeDtypeStruct((PACKED, breadth), f32)
+    packed = jax.ShapeDtypeStruct((breadth // LANES * PACKED, LANES), f32)
     corner = jax.ShapeDtypeStruct((STRIP, LANES), f32)
     columns = jax.ShapeDtypeStruct((height, LANES), f32)
     even, odd, even_corner, odd_corner = pl.pallas_call(

time: 34.4 us -> 34.2 us (level)
  starting transfers between devices: 16.3 us -> 15.9 us
    ppermute x3, waiting for transfers between devices: 4.95 us -> 5.78 us  [body(): gram = gram + lax.ppermute(gram, 'gy', [(i, i ^ reach) for i in range(gy)])]
    ppermute x1, waiting for transfers between devices: 1.55 us -> 1.06 us  [body(): even_corner = lax.ppermute(even_corner, ('gy', 'gx'), diagonal(pairs))]
    ppermute x3, starting transfers between devices: 7.46 us -> 7.07 us  [body(): gram = gram + lax.ppermute(gram, 'gy', [(i, i ^ reach) for i in range(gy)])]
where the time goes in v7:
time: 34.2 us; the launch traced here: 34.1 us
  starting transfers between devices  15.9 us (46%)
  Pallas kernels  9.3 us (27%)
  waiting for transfers between devices  8.01 us (23%)
  between operations  0.8 us (2%)
    ppermute x3, starting transfers between devices, body(): gram = gram + lax.ppermute(gram, 'gy', [(i, i ^ reach) for i in range(gy)])  7.07 us
    ppermute x3, waiting for transfers between devices, body(): gram = gram + lax.ppermute(gram, 'gy', [(i, i ^ reach) for i in range(gy)])  5.78 us
    pallas_call x1, Pallas kernels, body(): pl.pallas_call(tile_kernel, out_shape=(jax.ShapeDtypeStruct((KEPT, height...  4.97 us
    ppermute x1, starting transfers between devices, body(): even_corner = lax.ppermute(even_corner, ('gy', 'gx'), diagonal(pairs))  4.38 us
    ppermute x1, starting transfers between devices, body(): even_in = lax.ppermute(even, 'gy', pairs)  3.06 us
    pallas_call x1, Pallas kernels, body(): pl.pallas_call(pack_kernel, in_specs=[pl.BlockSpec(memory_space=pltpu.HBM...  1.64 us
    pallas_call x1, Pallas kernels, body(): pl.pallas_call(edge_kernel, out_shape=(jax.ShapeDtypeStruct((KEPT, rows,...  1.26 us
    ppermute x1, waiting for transfers between devices, body(): gram = gram + lax.ppermute(gram, 'gx', swap)  1.16 us
  transfers between devices with their start and end apart: 9, of which 5 were waited for; matrix products, arithmetic and copies ran while one was open for 0% of the time, Pallas kernels for 16%

profile of v7, /device:TPU:0, one launch (start us, length us, event | category | flops | bytes accessed | tf_op | source)
XLA Modules:
  0.0 34.1 jit_solution(3829898890873118993)
XLA Ops:
  0.6 0.0 copy-start.3
  0.6 0.0 copy-start
  0.7 0.0 copy-start.4
  0.7 0.0 copy-start.5
  0.7 0.0 copy-start.1
  0.7 0.0 copy-start.2
  0.7 1.6 %pack.1 = (f32[552,128]{1,0:T(8,128)S(1)}, f32[552,128]{1,0:T(8,128)S(1)}, f32[8,128]{1,0:T(8,128)S(1)}, f32[8,128]{1,0:T(8,128)S(1)}) custom-call(f32[128,1024]{1,0:T(8,128)} %refs_0_.5, s32[128,1024]{1,0:T(8,128)} %refs_1_.5, f32[128,1024]{1,0:T(8,128)} %refs_2_.5, f32[128,1024]{1,0:T(8,128)} %refs_3_.5, f32[2,128,1024]{2,1,0:T(8,128)} %refs_4_.5, ...), custom_call_target="tpu_custom_call" | custom-call | bytes 1130496 | tf_op jit(solution)/shard_map/pack/pallas_call | solution.py:562
  2.3 3.1 %collective-permute-start.1 = (f32[552,128]{1,0:T(8,128)S(1)}, f32[552,128]{1,0:T(8,128)S(1)}, u32[]{:S(2)}, u32[]{:S(2)}) collective-permute-start(f32[552,128]{1,0:T(8,128)S(1)} %get-tuple-element.19), channel_id=1, source_target_pairs={{0,2},{2,0},{4,6},{6,4},{8,10},{10,8},{12,14},{14,12},{1,3},{3,1},... | collective-permute-start | bytes 847880 | tf_op jit(solution)/shard_map/ppermute | solution.py:584
  5.4 0.7 %collective-permute-start.2 = (f32[552,128]{1,0:T(8,128)S(1)}, f32[552,128]{1,0:T(8,128)S(1)}, u32[]{:S(2)}, u32[]{:S(2)}) collective-permute-start(f32[552,128]{1,0:T(8,128)S(1)} %get-tuple-element.20), channel_id=1, source_target_pairs={{2,4},{4,2},{6,8},{8,6},{10,12},{12,10},{3,5},{5,3},{7,9},{9,7},{1... | collective-permute-start | bytes 847880 | tf_op jit(solution)/shard_map/ppermute | solution.py:586
  6.1 0.0 copy-done.3
  6.1 0.0 copy-done
  6.1 0.0 copy-done.4
  6.1 0.3 columns.1
  6.5 0.1 collective-permute-start
  6.5 4.4 %collective-permute-start.3 = (f32[8,128]{1,0:T(8,128)S(1)}, f32[8,128]{1,0:T(8,128)S(1)}, u32[]{:S(2)}, u32[]{:S(2)}) collective-permute-start(f32[8,128]{1,0:T(8,128)S(1)} %get-tuple-element.21), channel_id=1, source_target_pairs={{0,3},{1,2},{2,1},{3,0},{4,7},{5,6},{6,5},{7,4},{8,11},{9,10},{10,... | collective-permute-start | bytes 12296 | tf_op jit(solution)/shard_map/ppermute | solution.py:585
  10.9 0.6 %collective-permute-start.4 = (f32[8,128]{1,0:T(8,128)S(1)}, f32[8,128]{1,0:T(8,128)S(1)}, u32[]{:S(2)}, u32[]{:S(2)}) collective-permute-start(f32[8,128]{1,0:T(8,128)S(1)} %get-tuple-element.16.refs_6_), channel_id=1, source_target_pairs={{2,5},{3,4},{4,3},{5,2},{6,9},{7,8},{8,7},{9,6},{10,13},{11,12},{1... | collective-permute-start | bytes 12296 | tf_op jit(solution)/shard_map/ppermute | solution.py:587
  11.6 0.0 collective-permute-done.refs_6_
  11.6 5.0 %tile.1 = (f32[7,128,1152]{2,1,0:T(8,128)S(1)}, f32[12,8,128]{2,1,0:T(8,128)S(1)}, f32[53,8,1152]{2,1,0:T(8,128)S(1)}) custom-call(f32[128,1024]{1,0:T(8,128)S(1)} %copy-done.2, s32[128,1024]{1,0:T(8,128)S(1)} %copy-done.3, f32[128,1024]{1,0:T(8,128)S(1)} %copy-done.4, f32[128,1024]{1,0:T(8,128)S(1)} %copy-done.5, f32[2,128,1024]{2,1,0:T(8,128)S(1)} %copy-done.1, ...), custom_call_target="tpu_custom_call" | custom-call | flops 14745600 | bytes 12386304 | tf_op jit(solution)/shard_map/tile/pallas_call | solution.py:590
  16.6 1.1 %collective-permute-done.3.even_corner = f32[8,128]{1,0:T(8,128)S(1)} collective-permute-done((f32[8,128]{1,0:T(8,128)S(1)}, f32[8,128]{1,0:T(8,128)S(1)}, u32[]{:S(2)}, u32[]{:S(2)}) %collective-permute-start.3) | collective-permute-done | bytes 4128 | tf_op jit(solution)/shard_map/ppermute | solution.py:585
  17.6 0.0 collective-permute-done.4.odd_corner
  17.6 0.0 collective-permute-done.1.even
  17.6 0.0 collective-permute-done.2.odd
  17.6 1.3 %edge.1 = (f32[7,16,1152]{2,1,0:T(8,128)S(1)}, f32[16,128]{1,0:T(8,128)S(1)}) custom-call(f32[53,8,1152]{2,1,0:T(8,128)S(1)} %get-tuple-element.17.handed, f32[552,128]{1,0:T(8,128)S(1)} %collective-permute-done.1.even, f32[552,128]{1,0:T(8,128)S(1)} %collective-permute-done.2.odd, f32[8,128]{1,0:T(8,128)S(1)} %collective-permute-done.3.even_corner, ...), custom_call_target="tpu_custom_call" | custom-call | flops 3686400 | bytes 1548288 | tf_op jit(solution)/shard_map/edge/pallas_call | solution.py:610
  18.9 0.0 collective-permute-start.5
  18.9 1.2 %collective-permute-done.5 = f32[16,128]{1,0:T(8,128)S(1)} collective-permute-done((f32[16,128]{1,0:T(8,128)S(1)}, f32[16,128]{1,0:T(8,128)S(1)}, u32[]{:S(2)}, u32[]{:S(2)}) %collective-permute-start.5) | collective-permute-done | bytes 8224 | tf_op jit(solution)/shard_map/ppermute | solution.py:626
  20.1 3.0 %collective-permute-start.6 = (f32[16,128]{1,0:T(8,128)S(1)}, f32[16,128]{1,0:T(8,128)S(1)}, u32[]{:S(2)}, u32[]{:S(2)}) collective-permute-start(f32[16,128]{1,0:T(8,128)S(1)} %add.12), channel_id=1, source_target_pairs={{0,2},{2,0},{4,6},{6,4},{8,10},{10,8},{12,14},{14,12},{1,3},{3,1},... | collective-permute-start | bytes 24584 | tf_op jit(solution)/shard_map/ppermute | solution.py:629
  23.1 1.6 %collective-permute-done.6 = f32[16,128]{1,0:T(8,128)S(1)} collective-permute-done((f32[16,128]{1,0:T(8,128)S(1)}, f32[16,128]{1,0:T(8,128)S(1)}, u32[]{:S(2)}, u32[]{:S(2)}) %collective-permute-start.6) | collective-permute-done | bytes 8224 | tf_op jit(solution)/shard_map/ppermute | solution.py:629
  24.8 1.6 %collective-permute-start.7 = (f32[16,128]{1,0:T(8,128)S(1)}, f32[16,128]{1,0:T(8,128)S(1)}, u32[]{:S(2)}, u32[]{:S(2)}) collective-permute-start(f32[16,128]{1,0:T(8,128)S(1)} %add.13), channel_id=1, source_target_pairs={{0,4},{2,6},{4,0},{6,2},{8,12},{10,14},{12,8},{14,10},{1,5},{3,7},... | collective-permute-start | bytes 24584 | tf_op jit(solution)/shard_map/ppermute | solution.py:629
  26.3 2.1 %collective-permute-done.7 = f32[16,128]{1,0:T(8,128)S(1)} collective-permute-done((f32[16,128]{1,0:T(8,128)S(1)}, f32[16,128]{1,0:T(8,128)S(1)}, u32[]{:S(2)}, u32[]{:S(2)}) %collective-permute-start.7) | collective-permute-done | bytes 8224 | tf_op jit(solution)/shard_map/ppermute | solution.py:629
  28.4 2.5 %collective-permute-start.8 = (f32[16,128]{1,0:T(8,128)S(1)}, f32[16,128]{1,0:T(8,128)S(1)}, u32[]{:S(2)}, u32[]{:S(2)}) collective-permute-start(f32[16,128]{1,0:T(8,128)S(1)} %add.14), channel_id=1, source_target_pairs={{0,8},{2,10},{4,12},{6,14},{8,0},{10,2},{12,4},{14,6},{1,9},{3,11}... | collective-permute-start | bytes 24584 | tf_op jit(solution)/shard_map/ppermute | solution.py:629
  30.9 2.1 %collective-permute-done.8 = f32[16,128]{1,0:T(8,128)S(1)} collective-permute-done((f32[16,128]{1,0:T(8,128)S(1)}, f32[16,128]{1,0:T(8,128)S(1)}, u32[]{:S(2)}, u32[]{:S(2)}) %collective-permute-start.8) | collective-permute-done | bytes 8224 | tf_op jit(solution)/shard_map/ppermute | solution.py:629
  33.0 1.1 %combine.1 = (f32[128,1024]{1,0:T(8,128)}, f32[128,1024]{1,0:T(8,128)}) custom-call(f32[16,128]{1,0:T(8,128)S(1)} %add.15.gram_ref, f32[7,128,1152]{2,1,0:T(8,128)S(1)} %get-tuple-element.28.kept, f32[7,16,1152]{2,1,0:T(8,128)S(1)} %get-tuple-element.29.edges), custom_call_target="tpu_custom_call" | custom-call | flops 1835008 | bytes 4718592 | tf_op jit(solution)/shard_map/combine/pallas_call | solution.py:633
  (7 shorter events, 0.0 us)
Async XLA Ops:
  0.6 5.4 %copy-start.3 = (s32[128,1024]{1,0:T(8,128)S(1)}, s32[128,1024]{1,0:T(8,128)}, u32[]{:S(2)}) copy-start(s32[128,1024]{1,0:T(8,128)} %refs_1_.5) | copy-start | bytes 1572868
  0.6 5.4 %copy-start = (f32[8,128,1024]{2,1,0:T(8,128)S(1)}, f32[8,128,1024]{2,1,0:T(8,128)}, u32[]{:S(2)}) copy-start(f32[8,128,1024]{2,1,0:T(8,128)} %refs_5_.5) | copy-start | bytes 12582916
  0.7 5.4 %copy-start.4 = (f32[128,1024]{1,0:T(8,128)S(1)}, f32[128,1024]{1,0:T(8,128)}, u32[]{:S(2)}) copy-start(f32[128,1024]{1,0:T(8,128)} %refs_2_.5) | copy-start | bytes 1572868
  0.7 5.4 %copy-start.5 = (f32[128,1024]{1,0:T(8,128)S(1)}, f32[128,1024]{1,0:T(8,128)}, u32[]{:S(2)}) copy-start(f32[128,1024]{1,0:T(8,128)} %refs_3_.5) | copy-start | bytes 1572868
  0.7 5.4 %copy-start.1 = (f32[2,128,1024]{2,1,0:T(8,128)S(1)}, f32[2,128,1024]{2,1,0:T(8,128)}, u32[]{:S(2)}) copy-start(f32[2,128,1024]{2,1,0:T(8,128)} %refs_4_.5) | copy-start | bytes 3145732
  0.7 5.4 %copy-start.2 = (f32[128,1024]{1,0:T(8,128)S(1)}, f32[128,1024]{1,0:T(8,128)}, u32[]{:S(2)}) copy-start(f32[128,1024]{1,0:T(8,128)} %refs_0_.5) | copy-start | bytes 1572868
  2.3 15.3 %collective-permute-start.1 = (f32[552,128]{1,0:T(8,128)S(1)}, f32[552,128]{1,0:T(8,128)S(1)}, u32[]{:S(2)}, u32[]{:S(2)}) collective-permute-start(f32[552,128]{1,0:T(8,128)S(1)} %get-tuple-element.19), channel_id=1, source_target_pairs={{0,2},{2,0},{4,6},{6,4},{8,10},{10,8},{12,14},{14,12},{1,3},{3,1},... | collective-permute-start | bytes 847880 | tf_op jit(solution)/shard_map/ppermute | solution.py:584
  5.4 12.2 %collective-permute-start.2 = (f32[552,128]{1,0:T(8,128)S(1)}, f32[552,128]{1,0:T(8,128)S(1)}, u32[]{:S(2)}, u32[]{:S(2)}) collective-permute-start(f32[552,128]{1,0:T(8,128)S(1)} %get-tuple-element.20), channel_id=1, source_target_pairs={{2,4},{4,2},{6,8},{8,6},{10,12},{12,10},{3,5},{5,3},{7,9},{9,7},{1... | collective-permute-start | bytes 847880 | tf_op jit(solution)/shard_map/ppermute | solution.py:586
  6.5 5.1 %collective-permute-start = (f32[128,128]{1,0:T(8,128)S(1)}, f32[128,128]{1,0:T(8,128)S(1)}, u32[]{:S(2)}, u32[]{:S(2)}) collective-permute-start(f32[128,128]{1,0:T(8,128)S(1)} %columns.1), channel_id=1, source_target_pairs={{0,1},{1,0},{2,3},{3,2},{4,5},{5,4},{6,7},{7,6},{8,9},{9,8},{10,11... | collective-permute-start | bytes 196616 | tf_op jit(solution)/shard_map/ppermute | solution.py:583
  6.5 11.1 %collective-permute-start.3 = (f32[8,128]{1,0:T(8,128)S(1)}, f32[8,128]{1,0:T(8,128)S(1)}, u32[]{:S(2)}, u32[]{:S(2)}) collective-permute-start(f32[8,128]{1,0:T(8,128)S(1)} %get-tuple-element.21), channel_id=1, source_target_pairs={{0,3},{1,2},{2,1},{3,0},{4,7},{5,6},{6,5},{7,4},{8,11},{9,10},{10,... | collective-permute-start | bytes 12296 | tf_op jit(solution)/shard_map/ppermute | solution.py:585
  10.9 6.7 %collective-permute-start.4 = (f32[8,128]{1,0:T(8,128)S(1)}, f32[8,128]{1,0:T(8,128)S(1)}, u32[]{:S(2)}, u32[]{:S(2)}) collective-permute-start(f32[8,128]{1,0:T(8,128)S(1)} %get-tuple-element.16.refs_6_), channel_id=1, source_target_pairs={{2,5},{3,4},{4,3},{5,2},{6,9},{7,8},{8,7},{9,6},{10,13},{11,12},{1... | collective-permute-start | bytes 12296 | tf_op jit(solution)/shard_map/ppermute | solution.py:587
  18.9 1.2 %collective-permute-start.5 = (f32[16,128]{1,0:T(8,128)S(1)}, f32[16,128]{1,0:T(8,128)S(1)}, u32[]{:S(2)}, u32[]{:S(2)}) collective-permute-start(f32[16,128]{1,0:T(8,128)S(1)} %get-tuple-element.27), channel_id=1, source_target_pairs={{0,1},{1,0},{2,3},{3,2},{4,5},{5,4},{6,7},{7,6},{8,9},{9,8},{10,11... | collective-permute-start | bytes 24584 | tf_op jit(solution)/shard_map/ppermute | solution.py:626
  20.1 4.7 %collective-permute-start.6 = (f32[16,128]{1,0:T(8,128)S(1)}, f32[16,128]{1,0:T(8,128)S(1)}, u32[]{:S(2)}, u32[]{:S(2)}) collective-permute-start(f32[16,128]{1,0:T(8,128)S(1)} %add.12), channel_id=1, source_target_pairs={{0,2},{2,0},{4,6},{6,4},{8,10},{10,8},{12,14},{14,12},{1,3},{3,1},... | collective-permute-start | bytes 24584 | tf_op jit(solution)/shard_map/ppermute | solution.py:629
  24.8 3.7 %collective-permute-start.7 = (f32[16,128]{1,0:T(8,128)S(1)}, f32[16,128]{1,0:T(8,128)S(1)}, u32[]{:S(2)}, u32[]{:S(2)}) collective-permute-start(f32[16,128]{1,0:T(8,128)S(1)} %add.13), channel_id=1, source_target_pairs={{0,4},{2,6},{4,0},{6,2},{8,12},{10,14},{12,8},{14,10},{1,5},{3,7},... | collective-permute-start | bytes 24584 | tf_op jit(solution)/shard_map/ppermute | solution.py:629
  28.4 4.5 %collective-permute-start.8 = (f32[16,128]{1,0:T(8,128)S(1)}, f32[16,128]{1,0:T(8,128)S(1)}, u32[]{:S(2)}, u32[]{:S(2)}) collective-permute-start(f32[16,128]{1,0:T(8,128)S(1)} %add.14), channel_id=1, source_target_pairs={{0,8},{2,10},{4,12},{6,14},{8,0},{10,2},{12,4},{14,6},{1,9},{3,11}... | collective-permute-start | bytes 24584 | tf_op jit(solution)/shard_map/ppermute | solution.py:629

commit v8 on v7

--- a/solution.py
+++ b/solution.py
@@ -8,7 +8,7 @@
 from jax.sharding import PartitionSpec as P
 
 ITERS = 3
-SHIFT = 1.0
+SHIFT = 0.7
 SCALE = 4.0
 LANES = 128
 STRIP = 8

time: 34.2 us -> 34.2 us (level)
  no operation moved by 1% of the time
where the time goes in v8:
time: 34.2 us; the launch traced here: 34.1 us
  starting transfers between devices  15.9 us (46%)
  Pallas kernels  9.31 us (27%)
  waiting for transfers between devices  8.01 us (23%)
  between operations  0.8 us (2%)
    ppermute x3, starting transfers between devices, body(): gram = gram + lax.ppermute(gram, 'gy', [(i, i ^ reach) for i in range(gy)])  7.07 us
    ppermute x3, waiting for transfers between devices, body(): gram = gram + lax.ppermute(gram, 'gy', [(i, i ^ reach) for i in range(gy)])  5.79 us
    pallas_call x1, Pallas kernels, body(): pl.pallas_call(tile_kernel, out_shape=(jax.ShapeDtypeStruct((KEPT, height...  4.98 us
    ppermute x1, starting transfers between devices, body(): even_corner = lax.ppermute(even_corner, ('gy', 'gx'), diagonal(pairs))  4.38 us
    ppermute x1, starting transfers between devices, body(): even_in = lax.ppermute(even, 'gy', pairs)  3.06 us
    pallas_call x1, Pallas kernels, body(): pl.pallas_call(pack_kernel, in_specs=[pl.BlockSpec(memory_space=pltpu.HBM...  1.64 us
    pallas_call x1, Pallas kernels, body(): pl.pallas_call(edge_kernel, out_shape=(jax.ShapeDtypeStruct((KEPT, rows,...  1.27 us
    ppermute x1, waiting for transfers between devices, body(): gram = gram + lax.ppermute(gram, 'gx', swap)  1.16 us
  transfers between devices with their start and end apart: 9, of which 5 were waited for; matrix products, arithmetic and copies ran while one was open for 0% of the time, Pallas kernels for 16%

profile of v8, /device:TPU:0, one launch (start us, length us, event | category | flops | bytes accessed | tf_op | source)
XLA Modules:
  0.0 34.1 jit_solution(7539072106965448446)
XLA Ops:
  0.6 0.0 copy-start.3
  0.6 0.0 copy-start
  0.7 0.0 copy-start.4
  0.7 0.0 copy-start.5
  0.7 0.0 copy-start.1
  0.7 0.0 copy-start.2
  0.7 1.6 %pack.1 = (f32[552,128]{1,0:T(8,128)S(1)}, f32[552,128]{1,0:T(8,128)S(1)}, f32[8,128]{1,0:T(8,128)S(1)}, f32[8,128]{1,0:T(8,128)S(1)}) custom-call(f32[128,1024]{1,0:T(8,128)} %refs_0_.5, s32[128,1024]{1,0:T(8,128)} %refs_1_.5, f32[128,1024]{1,0:T(8,128)} %refs_2_.5, f32[128,1024]{1,0:T(8,128)} %refs_3_.5, f32[2,128,1024]{2,1,0:T(8,128)} %refs_4_.5, ...), custom_call_target="tpu_custom_call" | custom-call | bytes 1130496 | tf_op jit(solution)/shard_map/pack/pallas_call | solution.py:562
  2.3 3.1 %collective-permute-start.1 = (f32[552,128]{1,0:T(8,128)S(1)}, f32[552,128]{1,0:T(8,128)S(1)}, u32[]{:S(2)}, u32[]{:S(2)}) collective-permute-start(f32[552,128]{1,0:T(8,128)S(1)} %get-tuple-element.19), channel_id=1, source_target_pairs={{0,2},{2,0},{4,6},{6,4},{8,10},{10,8},{12,14},{14,12},{1,3},{3,1},... | collective-permute-start | bytes 847880 | tf_op jit(solution)/shard_map/ppermute | solution.py:584
  5.4 0.7 %collective-permute-start.2 = (f32[552,128]{1,0:T(8,128)S(1)}, f32[552,128]{1,0:T(8,128)S(1)}, u32[]{:S(2)}, u32[]{:S(2)}) collective-permute-start(f32[552,128]{1,0:T(8,128)S(1)} %get-tuple-element.20), channel_id=1, source_target_pairs={{2,4},{4,2},{6,8},{8,6},{10,12},{12,10},{3,5},{5,3},{7,9},{9,7},{1... | collective-permute-start | bytes 847880 | tf_op jit(solution)/shard_map/ppermute | solution.py:586
  6.1 0.0 copy-done.3
  6.1 0.0 copy-done
  6.1 0.0 copy-done.4
  6.1 0.3 columns.1
  6.5 0.1 collective-permute-start
  6.5 4.4 %collective-permute-start.3 = (f32[8,128]{1,0:T(8,128)S(1)}, f32[8,128]{1,0:T(8,128)S(1)}, u32[]{:S(2)}, u32[]{:S(2)}) collective-permute-start(f32[8,128]{1,0:T(8,128)S(1)} %get-tuple-element.21), channel_id=1, source_target_pairs={{0,3},{1,2},{2,1},{3,0},{4,7},{5,6},{6,5},{7,4},{8,11},{9,10},{10,... | collective-permute-start | bytes 12296 | tf_op jit(solution)/shard_map/ppermute | solution.py:585
  10.9 0.6 %collective-permute-start.4 = (f32[8,128]{1,0:T(8,128)S(1)}, f32[8,128]{1,0:T(8,128)S(1)}, u32[]{:S(2)}, u32[]{:S(2)}) collective-permute-start(f32[8,128]{1,0:T(8,128)S(1)} %get-tuple-element.16.refs_6_), channel_id=1, source_target_pairs={{2,5},{3,4},{4,3},{5,2},{6,9},{7,8},{8,7},{9,6},{10,13},{11,12},{1... | collective-permute-start | bytes 12296 | tf_op jit(solution)/shard_map/ppermute | solution.py:587
  11.6 0.0 collective-permute-done.refs_6_
  11.6 5.0 %tile.1 = (f32[7,128,1152]{2,1,0:T(8,128)S(1)}, f32[12,8,128]{2,1,0:T(8,128)S(1)}, f32[53,8,1152]{2,1,0:T(8,128)S(1)}) custom-call(f32[128,1024]{1,0:T(8,128)S(1)} %copy-done.2, s32[128,1024]{1,0:T(8,128)S(1)} %copy-done.3, f32[128,1024]{1,0:T(8,128)S(1)} %copy-done.4, f32[128,1024]{1,0:T(8,128)S(1)} %copy-done.5, f32[2,128,1024]{2,1,0:T(8,128)S(1)} %copy-done.1, ...), custom_call_target="tpu_custom_call" | custom-call | flops 14745600 | bytes 12386304 | tf_op jit(solution)/shard_map/tile/pallas_call | solution.py:590
  16.6 1.1 %collective-permute-done.3.even_corner = f32[8,128]{1,0:T(8,128)S(1)} collective-permute-done((f32[8,128]{1,0:T(8,128)S(1)}, f32[8,128]{1,0:T(8,128)S(1)}, u32[]{:S(2)}, u32[]{:S(2)}) %collective-permute-start.3) | collective-permute-done | bytes 4128 | tf_op jit(solution)/shard_map/ppermute | solution.py:585
  17.6 0.0 collective-permute-done.4.odd_corner
  17.6 0.0 collective-permute-done.1.even
  17.6 0.0 collective-permute-done.2.odd
  17.6 1.3 %edge.1 = (f32[7,16,1152]{2,1,0:T(8,128)S(1)}, f32[16,128]{1,0:T(8,128)S(1)}) custom-call(f32[53,8,1152]{2,1,0:T(8,128)S(1)} %get-tuple-element.17.handed, f32[552,128]{1,0:T(8,128)S(1)} %collective-permute-done.1.even, f32[552,128]{1,0:T(8,128)S(1)} %collective-permute-done.2.odd, f32[8,128]{1,0:T(8,128)S(1)} %collective-permute-done.3.even_corner, ...), custom_call_target="tpu_custom_call" | custom-call | flops 3686400 | bytes 1548288 | tf_op jit(solution)/shard_map/edge/pallas_call | solution.py:610
  18.9 0.0 collective-permute-start.5
  18.9 1.2 %collective-permute-done.5 = f32[16,128]{1,0:T(8,128)S(1)} collective-permute-done((f32[16,128]{1,0:T(8,128)S(1)}, f32[16,128]{1,0:T(8,128)S(1)}, u32[]{:S(2)}, u32[]{:S(2)}) %collective-permute-start.5) | collective-permute-done | bytes 8224 | tf_op jit(solution)/shard_map/ppermute | solution.py:626
  20.1 3.0 %collective-permute-start.6 = (f32[16,128]{1,0:T(8,128)S(1)}, f32[16,128]{1,0:T(8,128)S(1)}, u32[]{:S(2)}, u32[]{:S(2)}) collective-permute-start(f32[16,128]{1,0:T(8,128)S(1)} %add.12), channel_id=1, source_target_pairs={{0,2},{2,0},{4,6},{6,4},{8,10},{10,8},{12,14},{14,12},{1,3},{3,1},... | collective-permute-start | bytes 24584 | tf_op jit(solution)/shard_map/ppermute | solution.py:629
  23.1 1.6 %collective-permute-done.6 = f32[16,128]{1,0:T(8,128)S(1)} collective-permute-done((f32[16,128]{1,0:T(8,128)S(1)}, f32[16,128]{1,0:T(8,128)S(1)}, u32[]{:S(2)}, u32[]{:S(2)}) %collective-permute-start.6) | collective-permute-done | bytes 8224 | tf_op jit(solution)/shard_map/ppermute | solution.py:629
  24.8 1.6 %collective-permute-start.7 = (f32[16,128]{1,0:T(8,128)S(1)}, f32[16,128]{1,0:T(8,128)S(1)}, u32[]{:S(2)}, u32[]{:S(2)}) collective-permute-start(f32[16,128]{1,0:T(8,128)S(1)} %add.13), channel_id=1, source_target_pairs={{0,4},{2,6},{4,0},{6,2},{8,12},{10,14},{12,8},{14,10},{1,5},{3,7},... | collective-permute-start | bytes 24584 | tf_op jit(solution)/shard_map/ppermute | solution.py:629
  26.3 2.1 %collective-permute-done.7 = f32[16,128]{1,0:T(8,128)S(1)} collective-permute-done((f32[16,128]{1,0:T(8,128)S(1)}, f32[16,128]{1,0:T(8,128)S(1)}, u32[]{:S(2)}, u32[]{:S(2)}) %collective-permute-start.7) | collective-permute-done | bytes 8224 | tf_op jit(solution)/shard_map/ppermute | solution.py:629
  28.4 2.5 %collective-permute-start.8 = (f32[16,128]{1,0:T(8,128)S(1)}, f32[16,128]{1,0:T(8,128)S(1)}, u32[]{:S(2)}, u32[]{:S(2)}) collective-permute-start(f32[16,128]{1,0:T(8,128)S(1)} %add.14), channel_id=1, source_target_pairs={{0,8},{2,10},{4,12},{6,14},{8,0},{10,2},{12,4},{14,6},{1,9},{3,11}... | collective-permute-start | bytes 24584 | tf_op jit(solution)/shard_map/ppermute | solution.py:629
  30.9 2.1 %collective-permute-done.8 = f32[16,128]{1,0:T(8,128)S(1)} collective-permute-done((f32[16,128]{1,0:T(8,128)S(1)}, f32[16,128]{1,0:T(8,128)S(1)}, u32[]{:S(2)}, u32[]{:S(2)}) %collective-permute-start.8) | collective-permute-done | bytes 8224 | tf_op jit(solution)/shard_map/ppermute | solution.py:629
  33.0 1.1 %combine.1 = (f32[128,1024]{1,0:T(8,128)}, f32[128,1024]{1,0:T(8,128)}) custom-call(f32[16,128]{1,0:T(8,128)S(1)} %add.15.gram_ref, f32[7,128,1152]{2,1,0:T(8,128)S(1)} %get-tuple-element.28.kept, f32[7,16,1152]{2,1,0:T(8,128)S(1)} %get-tuple-element.29.edges), custom_call_target="tpu_custom_call" | custom-call | flops 1835008 | bytes 4718592 | tf_op jit(solution)/shard_map/combine/pallas_call | solution.py:633
  (7 shorter events, 0.0 us)
Async XLA Ops:
  0.6 5.4 %copy-start.3 = (s32[128,1024]{1,0:T(8,128)S(1)}, s32[128,1024]{1,0:T(8,128)}, u32[]{:S(2)}) copy-start(s32[128,1024]{1,0:T(8,128)} %refs_1_.5) | copy-start | bytes 1572868
  0.6 5.4 %copy-start = (f32[8,128,1024]{2,1,0:T(8,128)S(1)}, f32[8,128,1024]{2,1,0:T(8,128)}, u32[]{:S(2)}) copy-start(f32[8,128,1024]{2,1,0:T(8,128)} %refs_5_.5) | copy-start | bytes 12582916
  0.7 5.4 %copy-start.4 = (f32[128,1024]{1,0:T(8,128)S(1)}, f32[128,1024]{1,0:T(8,128)}, u32[]{:S(2)}) copy-start(f32[128,1024]{1,0:T(8,128)} %refs_2_.5) | copy-start | bytes 1572868
  0.7 5.4 %copy-start.5 = (f32[128,1024]{1,0:T(8,128)S(1)}, f32[128,1024]{1,0:T(8,128)}, u32[]{:S(2)}) copy-start(f32[128,1024]{1,0:T(8,128)} %refs_3_.5) | copy-start | bytes 1572868
  0.7 5.4 %copy-start.1 = (f32[2,128,1024]{2,1,0:T(8,128)S(1)}, f32[2,128,1024]{2,1,0:T(8,128)}, u32[]{:S(2)}) copy-start(f32[2,128,1024]{2,1,0:T(8,128)} %refs_4_.5) | copy-start | bytes 3145732
  0.7 5.4 %copy-start.2 = (f32[128,1024]{1,0:T(8,128)S(1)}, f32[128,1024]{1,0:T(8,128)}, u32[]{:S(2)}) copy-start(f32[128,1024]{1,0:T(8,128)} %refs_0_.5) | copy-start | bytes 1572868
  2.3 15.3 %collective-permute-start.1 = (f32[552,128]{1,0:T(8,128)S(1)}, f32[552,128]{1,0:T(8,128)S(1)}, u32[]{:S(2)}, u32[]{:S(2)}) collective-permute-start(f32[552,128]{1,0:T(8,128)S(1)} %get-tuple-element.19), channel_id=1, source_target_pairs={{0,2},{2,0},{4,6},{6,4},{8,10},{10,8},{12,14},{14,12},{1,3},{3,1},... | collective-permute-start | bytes 847880 | tf_op jit(solution)/shard_map/ppermute | solution.py:584
  5.4 12.2 %collective-permute-start.2 = (f32[552,128]{1,0:T(8,128)S(1)}, f32[552,128]{1,0:T(8,128)S(1)}, u32[]{:S(2)}, u32[]{:S(2)}) collective-permute-start(f32[552,128]{1,0:T(8,128)S(1)} %get-tuple-element.20), channel_id=1, source_target_pairs={{2,4},{4,2},{6,8},{8,6},{10,12},{12,10},{3,5},{5,3},{7,9},{9,7},{1... | collective-permute-start | bytes 847880 | tf_op jit(solution)/shard_map/ppermute | solution.py:586
  6.5 5.1 %collective-permute-start = (f32[128,128]{1,0:T(8,128)S(1)}, f32[128,128]{1,0:T(8,128)S(1)}, u32[]{:S(2)}, u32[]{:S(2)}) collective-permute-start(f32[128,128]{1,0:T(8,128)S(1)} %columns.1), channel_id=1, source_target_pairs={{0,1},{1,0},{2,3},{3,2},{4,5},{5,4},{6,7},{7,6},{8,9},{9,8},{10,11... | collective-permute-start | bytes 196616 | tf_op jit(solution)/shard_map/ppermute | solution.py:583
  6.5 11.1 %collective-permute-start.3 = (f32[8,128]{1,0:T(8,128)S(1)}, f32[8,128]{1,0:T(8,128)S(1)}, u32[]{:S(2)}, u32[]{:S(2)}) collective-permute-start(f32[8,128]{1,0:T(8,128)S(1)} %get-tuple-element.21), channel_id=1, source_target_pairs={{0,3},{1,2},{2,1},{3,0},{4,7},{5,6},{6,5},{7,4},{8,11},{9,10},{10,... | collective-permute-start | bytes 12296 | tf_op jit(solution)/shard_map/ppermute | solution.py:585
  10.9 6.7 %collective-permute-start.4 = (f32[8,128]{1,0:T(8,128)S(1)}, f32[8,128]{1,0:T(8,128)S(1)}, u32[]{:S(2)}, u32[]{:S(2)}) collective-permute-start(f32[8,128]{1,0:T(8,128)S(1)} %get-tuple-element.16.refs_6_), channel_id=1, source_target_pairs={{2,5},{3,4},{4,3},{5,2},{6,9},{7,8},{8,7},{9,6},{10,13},{11,12},{1... | collective-permute-start | bytes 12296 | tf_op jit(solution)/shard_map/ppermute | solution.py:587
  18.9 1.2 %collective-permute-start.5 = (f32[16,128]{1,0:T(8,128)S(1)}, f32[16,128]{1,0:T(8,128)S(1)}, u32[]{:S(2)}, u32[]{:S(2)}) collective-permute-start(f32[16,128]{1,0:T(8,128)S(1)} %get-tuple-element.27), channel_id=1, source_target_pairs={{0,1},{1,0},{2,3},{3,2},{4,5},{5,4},{6,7},{7,6},{8,9},{9,8},{10,11... | collective-permute-start | bytes 24584 | tf_op jit(solution)/shard_map/ppermute | solution.py:626
  20.1 4.7 %collective-permute-start.6 = (f32[16,128]{1,0:T(8,128)S(1)}, f32[16,128]{1,0:T(8,128)S(1)}, u32[]{:S(2)}, u32[]{:S(2)}) collective-permute-start(f32[16,128]{1,0:T(8,128)S(1)} %add.12), channel_id=1, source_target_pairs={{0,2},{2,0},{4,6},{6,4},{8,10},{10,8},{12,14},{14,12},{1,3},{3,1},... | collective-permute-start | bytes 24584 | tf_op jit(solution)/shard_map/ppermute | solution.py:629
  24.8 3.7 %collective-permute-start.7 = (f32[16,128]{1,0:T(8,128)S(1)}, f32[16,128]{1,0:T(8,128)S(1)}, u32[]{:S(2)}, u32[]{:S(2)}) collective-permute-start(f32[16,128]{1,0:T(8,128)S(1)} %add.13), channel_id=1, source_target_pairs={{0,4},{2,6},{4,0},{6,2},{8,12},{10,14},{12,8},{14,10},{1,5},{3,7},... | collective-permute-start | bytes 24584 | tf_op jit(solution)/shard_map/ppermute | solution.py:629
  28.4 4.5 %collective-permute-start.8 = (f32[16,128]{1,0:T(8,128)S(1)}, f32[16,128]{1,0:T(8,128)S(1)}, u32[]{:S(2)}, u32[]{:S(2)}) collective-permute-start(f32[16,128]{1,0:T(8,128)S(1)} %add.14), channel_id=1, source_target_pairs={{0,8},{2,10},{4,12},{6,14},{8,0},{10,2},{12,4},{14,6},{1,9},{3,11}... | collective-permute-start | bytes 24584 | tf_op jit(solution)/shard_map/ppermute | solution.py:629

commit v9 on v8

--- a/solution.py
+++ b/solution.py
@@ -623,11 +623,12 @@
         name="edge",
     )(handed, even_in, odd_in, even_corner, odd_corner, sums)
 
-    gram = gram + lax.ppermute(gram, "gx", swap)
     reach = 1
     while reach < gy:
         gram = gram + lax.ppermute(gram, "gy", [(i, i ^ reach) for i in range(gy)])
         reach *= 2
+
+    gram = gram + lax.ppermute(gram, "gx", swap)
 
     tile = jax.ShapeDtypeStruct((height, breadth), f32)
     return pl.pallas_call(

time: 34.2 us -> 34.1 us (level)
  no operation moved by 1% of the time
where the time goes in v9:
time: 34.1 us; the launch traced here: 34 us
  starting transfers between devices  15.9 us (47%)
  Pallas kernels  9.31 us (27%)
  waiting for transfers between devices  7.93 us (23%)
  between operations  0.79 us (2%)
    ppermute x3, starting transfers between devices, body(): gram = gram + lax.ppermute(gram, 'gy', [(i, i ^ reach) for i in range(gy)])  7.08 us
    ppermute x3, waiting for transfers between devices, body(): gram = gram + lax.ppermute(gram, 'gy', [(i, i ^ reach) for i in range(gy)])  5.69 us
    pallas_call x1, Pallas kernels, body(): pl.pallas_call(tile_kernel, out_shape=(jax.ShapeDtypeStruct((KEPT, height...  4.98 us
    ppermute x1, starting transfers between devices, body(): even_corner = lax.ppermute(even_corner, ('gy', 'gx'), diagonal(pairs))  4.38 us
    ppermute x1, starting transfers between devices, body(): even_in = lax.ppermute(even, 'gy', pairs)  3.06 us
    pallas_call x1, Pallas kernels, body(): pl.pallas_call(pack_kernel, in_specs=[pl.BlockSpec(memory_space=pltpu.HBM...  1.64 us
    pallas_call x1, Pallas kernels, body(): pl.pallas_call(edge_kernel, out_shape=(jax.ShapeDtypeStruct((KEPT, rows,...  1.27 us
    ppermute x1, waiting for transfers between devices, body(): gram = gram + lax.ppermute(gram, 'gx', swap)  1.17 us
  transfers between devices with their start and end apart: 9, of which 5 were waited for; matrix products, arithmetic and copies ran while one was open for 0% of the time, Pallas kernels for 16%

profile of v9, /device:TPU:0, one launch (start us, length us, event | category | flops | bytes accessed | tf_op | source)
XLA Modules:
  0.0 34.0 jit_solution(3349999728534248210)
XLA Ops:
  0.6 0.0 copy-start.3
  0.6 0.0 copy-start
  0.7 0.0 copy-start.4
  0.7 0.0 copy-start.5
  0.7 0.0 copy-start.1
  0.7 0.0 copy-start.2
  0.7 1.6 %pack.1 = (f32[552,128]{1,0:T(8,128)S(1)}, f32[552,128]{1,0:T(8,128)S(1)}, f32[8,128]{1,0:T(8,128)S(1)}, f32[8,128]{1,0:T(8,128)S(1)}) custom-call(f32[128,1024]{1,0:T(8,128)} %refs_0_.5, s32[128,1024]{1,0:T(8,128)} %refs_1_.5, f32[128,1024]{1,0:T(8,128)} %refs_2_.5, f32[128,1024]{1,0:T(8,128)} %refs_3_.5, f32[2,128,1024]{2,1,0:T(8,128)} %refs_4_.5, ...), custom_call_target="tpu_custom_call" | custom-call | bytes 1130496 | tf_op jit(solution)/shard_map/pack/pallas_call | solution.py:562
  2.3 3.1 %collective-permute-start.1 = (f32[552,128]{1,0:T(8,128)S(1)}, f32[552,128]{1,0:T(8,128)S(1)}, u32[]{:S(2)}, u32[]{:S(2)}) collective-permute-start(f32[552,128]{1,0:T(8,128)S(1)} %get-tuple-element.19), channel_id=1, source_target_pairs={{0,2},{2,0},{4,6},{6,4},{8,10},{10,8},{12,14},{14,12},{1,3},{3,1},... | collective-permute-start | bytes 847880 | tf_op jit(solution)/shard_map/ppermute | solution.py:584
  5.4 0.7 %collective-permute-start.2 = (f32[552,128]{1,0:T(8,128)S(1)}, f32[552,128]{1,0:T(8,128)S(1)}, u32[]{:S(2)}, u32[]{:S(2)}) collective-permute-start(f32[552,128]{1,0:T(8,128)S(1)} %get-tuple-element.20), channel_id=1, source_target_pairs={{2,4},{4,2},{6,8},{8,6},{10,12},{12,10},{3,5},{5,3},{7,9},{9,7},{1... | collective-permute-start | bytes 847880 | tf_op jit(solution)/shard_map/ppermute | solution.py:586
  6.1 0.0 copy-done.3
  6.1 0.0 copy-done
  6.1 0.0 copy-done.4
  6.1 0.3 columns.1
  6.5 0.1 collective-permute-start
  6.5 4.4 %collective-permute-start.3 = (f32[8,128]{1,0:T(8,128)S(1)}, f32[8,128]{1,0:T(8,128)S(1)}, u32[]{:S(2)}, u32[]{:S(2)}) collective-permute-start(f32[8,128]{1,0:T(8,128)S(1)} %get-tuple-element.21), channel_id=1, source_target_pairs={{0,3},{1,2},{2,1},{3,0},{4,7},{5,6},{6,5},{7,4},{8,11},{9,10},{10,... | collective-permute-start | bytes 12296 | tf_op jit(solution)/shard_map/ppermute | solution.py:585
  10.9 0.6 %collective-permute-start.4 = (f32[8,128]{1,0:T(8,128)S(1)}, f32[8,128]{1,0:T(8,128)S(1)}, u32[]{:S(2)}, u32[]{:S(2)}) collective-permute-start(f32[8,128]{1,0:T(8,128)S(1)} %get-tuple-element.16.refs_6_), channel_id=1, source_target_pairs={{2,5},{3,4},{4,3},{5,2},{6,9},{7,8},{8,7},{9,6},{10,13},{11,12},{1... | collective-permute-start | bytes 12296 | tf_op jit(solution)/shard_map/ppermute | solution.py:587
  11.6 0.0 collective-permute-done.refs_6_
  11.6 5.0 %tile.1 = (f32[7,128,1152]{2,1,0:T(8,128)S(1)}, f32[12,8,128]{2,1,0:T(8,128)S(1)}, f32[53,8,1152]{2,1,0:T(8,128)S(1)}) custom-call(f32[128,1024]{1,0:T(8,128)S(1)} %copy-done.2, s32[128,1024]{1,0:T(8,128)S(1)} %copy-done.3, f32[128,1024]{1,0:T(8,128)S(1)} %copy-done.4, f32[128,1024]{1,0:T(8,128)S(1)} %copy-done.5, f32[2,128,1024]{2,1,0:T(8,128)S(1)} %copy-done.1, ...), custom_call_target="tpu_custom_call" | custom-call | flops 14745600 | bytes 12386304 | tf_op jit(solution)/shard_map/tile/pallas_call | solution.py:590
  16.6 1.1 %collective-permute-done.3.even_corner = f32[8,128]{1,0:T(8,128)S(1)} collective-permute-done((f32[8,128]{1,0:T(8,128)S(1)}, f32[8,128]{1,0:T(8,128)S(1)}, u32[]{:S(2)}, u32[]{:S(2)}) %collective-permute-start.3) | collective-permute-done | bytes 4128 | tf_op jit(solution)/shard_map/ppermute | solution.py:585
  17.6 0.0 collective-permute-done.4.odd_corner
  17.6 0.0 collective-permute-done.1.even
  17.6 0.0 collective-permute-done.2.odd
  17.6 1.3 %edge.1 = (f32[7,16,1152]{2,1,0:T(8,128)S(1)}, f32[16,128]{1,0:T(8,128)S(1)}) custom-call(f32[53,8,1152]{2,1,0:T(8,128)S(1)} %get-tuple-element.17.handed, f32[552,128]{1,0:T(8,128)S(1)} %collective-permute-done.1.even, f32[552,128]{1,0:T(8,128)S(1)} %collective-permute-done.2.odd, f32[8,128]{1,0:T(8,128)S(1)} %collective-permute-done.3.even_corner, ...), custom_call_target="tpu_custom_call" | custom-call | flops 3686400 | bytes 1548288 | tf_op jit(solution)/shard_map/edge/pallas_call | solution.py:610
  18.9 2.9 %collective-permute-start.5 = (f32[16,128]{1,0:T(8,128)S(1)}, f32[16,128]{1,0:T(8,128)S(1)}, u32[]{:S(2)}, u32[]{:S(2)}) collective-permute-start(f32[16,128]{1,0:T(8,128)S(1)} %get-tuple-element.27), channel_id=1, source_target_pairs={{0,2},{2,0},{4,6},{6,4},{8,10},{10,8},{12,14},{14,12},{1,3},{3,1},... | collective-permute-start | bytes 24584 | tf_op jit(solution)/shard_map/ppermute | solution.py:628
  21.9 1.6 %collective-permute-done.5 = f32[16,128]{1,0:T(8,128)S(1)} collective-permute-done((f32[16,128]{1,0:T(8,128)S(1)}, f32[16,128]{1,0:T(8,128)S(1)}, u32[]{:S(2)}, u32[]{:S(2)}) %collective-permute-start.5) | collective-permute-done | bytes 8224 | tf_op jit(solution)/shard_map/ppermute | solution.py:628
  23.5 1.6 %collective-permute-start.6 = (f32[16,128]{1,0:T(8,128)S(1)}, f32[16,128]{1,0:T(8,128)S(1)}, u32[]{:S(2)}, u32[]{:S(2)}) collective-permute-start(f32[16,128]{1,0:T(8,128)S(1)} %add.12), channel_id=1, source_target_pairs={{0,4},{2,6},{4,0},{6,2},{8,12},{10,14},{12,8},{14,10},{1,5},{3,7},... | collective-permute-start | bytes 24584 | tf_op jit(solution)/shard_map/ppermute | solution.py:628
  25.1 2.1 %collective-permute-done.6 = f32[16,128]{1,0:T(8,128)S(1)} collective-permute-done((f32[16,128]{1,0:T(8,128)S(1)}, f32[16,128]{1,0:T(8,128)S(1)}, u32[]{:S(2)}, u32[]{:S(2)}) %collective-permute-start.6) | collective-permute-done | bytes 8224 | tf_op jit(solution)/shard_map/ppermute | solution.py:628
  27.1 2.6 %collective-permute-start.7 = (f32[16,128]{1,0:T(8,128)S(1)}, f32[16,128]{1,0:T(8,128)S(1)}, u32[]{:S(2)}, u32[]{:S(2)}) collective-permute-start(f32[16,128]{1,0:T(8,128)S(1)} %add.13), channel_id=1, source_target_pairs={{0,8},{2,10},{4,12},{6,14},{8,0},{10,2},{12,4},{14,6},{1,9},{3,11}... | collective-permute-start | bytes 24584 | tf_op jit(solution)/shard_map/ppermute | solution.py:628
  29.7 2.0 %collective-permute-done.7 = f32[16,128]{1,0:T(8,128)S(1)} collective-permute-done((f32[16,128]{1,0:T(8,128)S(1)}, f32[16,128]{1,0:T(8,128)S(1)}, u32[]{:S(2)}, u32[]{:S(2)}) %collective-permute-start.7) | collective-permute-done | bytes 8224 | tf_op jit(solution)/shard_map/ppermute | solution.py:628
  31.7 0.0 collective-permute-start.8
  31.7 1.2 %collective-permute-done.8 = f32[16,128]{1,0:T(8,128)S(1)} collective-permute-done((f32[16,128]{1,0:T(8,128)S(1)}, f32[16,128]{1,0:T(8,128)S(1)}, u32[]{:S(2)}, u32[]{:S(2)}) %collective-permute-start.8) | collective-permute-done | bytes 8224 | tf_op jit(solution)/shard_map/ppermute | solution.py:631
  32.9 1.1 %combine.1 = (f32[128,1024]{1,0:T(8,128)}, f32[128,1024]{1,0:T(8,128)}) custom-call(f32[16,128]{1,0:T(8,128)S(1)} %add.15.gram_ref, f32[7,128,1152]{2,1,0:T(8,128)S(1)} %get-tuple-element.28.kept, f32[7,16,1152]{2,1,0:T(8,128)S(1)} %get-tuple-element.29.edges), custom_call_target="tpu_custom_call" | custom-call | flops 1835008 | bytes 4718592 | tf_op jit(solution)/shard_map/combine/pallas_call | solution.py:634
  (7 shorter events, 0.0 us)
Async XLA Ops:
  0.6 5.4 %copy-start.3 = (s32[128,1024]{1,0:T(8,128)S(1)}, s32[128,1024]{1,0:T(8,128)}, u32[]{:S(2)}) copy-start(s32[128,1024]{1,0:T(8,128)} %refs_1_.5) | copy-start | bytes 1572868
  0.6 5.4 %copy-start = (f32[8,128,1024]{2,1,0:T(8,128)S(1)}, f32[8,128,1024]{2,1,0:T(8,128)}, u32[]{:S(2)}) copy-start(f32[8,128,1024]{2,1,0:T(8,128)} %refs_5_.5) | copy-start | bytes 12582916
  0.7 5.4 %copy-start.4 = (f32[128,1024]{1,0:T(8,128)S(1)}, f32[128,1024]{1,0:T(8,128)}, u32[]{:S(2)}) copy-start(f32[128,1024]{1,0:T(8,128)} %refs_2_.5) | copy-start | bytes 1572868
  0.7 5.4 %copy-start.5 = (f32[128,1024]{1,0:T(8,128)S(1)}, f32[128,1024]{1,0:T(8,128)}, u32[]{:S(2)}) copy-start(f32[128,1024]{1,0:T(8,128)} %refs_3_.5) | copy-start | bytes 1572868
  0.7 5.4 %copy-start.1 = (f32[2,128,1024]{2,1,0:T(8,128)S(1)}, f32[2,128,1024]{2,1,0:T(8,128)}, u32[]{:S(2)}) copy-start(f32[2,128,1024]{2,1,0:T(8,128)} %refs_4_.5) | copy-start | bytes 3145732
  0.7 5.4 %copy-start.2 = (f32[128,1024]{1,0:T(8,128)S(1)}, f32[128,1024]{1,0:T(8,128)}, u32[]{:S(2)}) copy-start(f32[128,1024]{1,0:T(8,128)} %refs_0_.5) | copy-start | bytes 1572868
  2.3 15.3 %collective-permute-start.1 = (f32[552,128]{1,0:T(8,128)S(1)}, f32[552,128]{1,0:T(8,128)S(1)}, u32[]{:S(2)}, u32[]{:S(2)}) collective-permute-start(f32[552,128]{1,0:T(8,128)S(1)} %get-tuple-element.19), channel_id=1, source_target_pairs={{0,2},{2,0},{4,6},{6,4},{8,10},{10,8},{12,14},{14,12},{1,3},{3,1},... | collective-permute-start | bytes 847880 | tf_op jit(solution)/shard_map/ppermute | solution.py:584
  5.4 12.2 %collective-permute-start.2 = (f32[552,128]{1,0:T(8,128)S(1)}, f32[552,128]{1,0:T(8,128)S(1)}, u32[]{:S(2)}, u32[]{:S(2)}) collective-permute-start(f32[552,128]{1,0:T(8,128)S(1)} %get-tuple-element.20), channel_id=1, source_target_pairs={{2,4},{4,2},{6,8},{8,6},{10,12},{12,10},{3,5},{5,3},{7,9},{9,7},{1... | collective-permute-start | bytes 847880 | tf_op jit(solution)/shard_map/ppermute | solution.py:586
  6.5 5.1 %collective-permute-start = (f32[128,128]{1,0:T(8,128)S(1)}, f32[128,128]{1,0:T(8,128)S(1)}, u32[]{:S(2)}, u32[]{:S(2)}) collective-permute-start(f32[128,128]{1,0:T(8,128)S(1)} %columns.1), channel_id=1, source_target_pairs={{0,1},{1,0},{2,3},{3,2},{4,5},{5,4},{6,7},{7,6},{8,9},{9,8},{10,11... | collective-permute-start | bytes 196616 | tf_op jit(solution)/shard_map/ppermute | solution.py:583
  6.5 11.1 %collective-permute-start.3 = (f32[8,128]{1,0:T(8,128)S(1)}, f32[8,128]{1,0:T(8,128)S(1)}, u32[]{:S(2)}, u32[]{:S(2)}) collective-permute-start(f32[8,128]{1,0:T(8,128)S(1)} %get-tuple-element.21), channel_id=1, source_target_pairs={{0,3},{1,2},{2,1},{3,0},{4,7},{5,6},{6,5},{7,4},{8,11},{9,10},{10,... | collective-permute-start | bytes 12296 | tf_op jit(solution)/shard_map/ppermute | solution.py:585
  10.9 6.7 %collective-permute-start.4 = (f32[8,128]{1,0:T(8,128)S(1)}, f32[8,128]{1,0:T(8,128)S(1)}, u32[]{:S(2)}, u32[]{:S(2)}) collective-permute-start(f32[8,128]{1,0:T(8,128)S(1)} %get-tuple-element.16.refs_6_), channel_id=1, source_target_pairs={{2,5},{3,4},{4,3},{5,2},{6,9},{7,8},{8,7},{9,6},{10,13},{11,12},{1... | collective-permute-start | bytes 12296 | tf_op jit(solution)/shard_map/ppermute | solution.py:587
  18.9 4.6 %collective-permute-start.5 = (f32[16,128]{1,0:T(8,128)S(1)}, f32[16,128]{1,0:T(8,128)S(1)}, u32[]{:S(2)}, u32[]{:S(2)}) collective-permute-start(f32[16,128]{1,0:T(8,128)S(1)} %get-tuple-element.27), channel_id=1, source_target_pairs={{0,2},{2,0},{4,6},{6,4},{8,10},{10,8},{12,14},{14,12},{1,3},{3,1},... | collective-permute-start | bytes 24584 | tf_op jit(solution)/shard_map/ppermute | solution.py:628
  23.5 3.7 %collective-permute-start.6 = (f32[16,128]{1,0:T(8,128)S(1)}, f32[16,128]{1,0:T(8,128)S(1)}, u32[]{:S(2)}, u32[]{:S(2)}) collective-permute-start(f32[16,128]{1,0:T(8,128)S(1)} %add.12), channel_id=1, source_target_pairs={{0,4},{2,6},{4,0},{6,2},{8,12},{10,14},{12,8},{14,10},{1,5},{3,7},... | collective-permute-start | bytes 24584 | tf_op jit(solution)/shard_map/ppermute | solution.py:628
  27.1 4.5 %collective-permute-start.7 = (f32[16,128]{1,0:T(8,128)S(1)}, f32[16,128]{1,0:T(8,128)S(1)}, u32[]{:S(2)}, u32[]{:S(2)}) collective-permute-start(f32[16,128]{1,0:T(8,128)S(1)} %add.13), channel_id=1, source_target_pairs={{0,8},{2,10},{4,12},{6,14},{8,0},{10,2},{12,4},{14,6},{1,9},{3,11}... | collective-permute-start | bytes 24584 | tf_op jit(solution)/shard_map/ppermute | solution.py:628
  31.7 1.2 %collective-permute-start.8 = (f32[16,128]{1,0:T(8,128)S(1)}, f32[16,128]{1,0:T(8,128)S(1)}, u32[]{:S(2)}, u32[]{:S(2)}) collective-permute-start(f32[16,128]{1,0:T(8,128)S(1)} %add.14), channel_id=1, source_target_pairs={{0,1},{1,0},{2,3},{3,2},{4,5},{5,4},{6,7},{7,6},{8,9},{9,8},{10,11... | collective-permute-start | bytes 24584 | tf_op jit(solution)/shard_map/ppermute | solution.py:631
